TPU v7x, 32 devices: a whole 2x2x4 slice. The times are simulated.
32 devices in a mesh: seq: 8 (over z, x), stream: 4 (over y, core).
Axes of the slice: x: 2, y: 2, z: 4, core: 2. Of those that a mesh axis runs over, the one named last changes fastest.
Arguments:
- tokens: bfloat16 [4, 4096, 1024], P('stream', 'seq'), may hold values from -6 to 6
- cotangent: bfloat16 [4, 4096, 1024], P('stream', 'seq'), may hold values from -6 to 6
- lengths: int32 [4, 4], P('stream'), may hold values from 64 to 3072, as said below
- order: int32 [4, 4], P('stream'), may hold values from 0 to 3, each once within a row
- weights: float32 [12, 1024, 1024], P(None, 'seq')
- momentum: float32 [12, 1024, 1024], P(None, 'seq')
- small_params: float32 [13312], P('seq')
- moment_one: float32 [13312], P('seq'), may hold values from -40 to 40
- moment_two: float32 [13312], P('seq'), may hold values from 163.84 to 3276.8
Outputs:
- block_out: bfloat16 [4, 4096, 1024], P('stream', 'seq')
- input_grad: float32 [4, 4096, 1024], P('stream', 'seq')
- new_weights: float32 [12, 1024, 1024], P(None, 'seq')
- new_momentum: float32 [12, 1024, 1024], P(None, 'seq')
- new_small: float32 [13312], P('seq')
- new_moment_one: float32 [13312], P('seq')
- new_moment_two: float32 [13312], P('seq')
Inputs may be any that keep to these rules, and one draw needn't show every extreme that they name: Each row holds the four lengths 48 * 64, 768, 192 and 64 in some order; they sum to 4096. `order`: each row is a permutation of 0 to 3.
All inputs are finite; a program needn't handle non-finite values.
Results may differ from a plain program's by a relative error of at most 0.006.
The roundings to bfloat16 on the way count: a program that leaves them out, or rounds other values in their place, can miss the bound.
Values may be sent and summed in bfloat16 or wider, within the bound.
A program may use at most 384 MiB of HBM per device.

v0:
```python
import jax
import jax.numpy as jnp
from jax import lax
from jax.sharding import PartitionSpec as P

D = 1024
HEADS = 16
HEAD_DIM = 64
FF = 4096
STEP = 10


highest = lax.Precision.HIGHEST


def passed_along(array, axis, by):
    count = lax.axis_size(axis)
    pairs = [(i, i + by) for i in range(count) if 0 <= i + by < count]
    return lax.ppermute(array, axis, pairs)


def layer_norm(values, gain, offset):
    center = values - jnp.mean(values, axis=-1, keepdims=True)
    spread = jnp.mean(center * center, axis=-1, keepdims=True)
    return center * lax.rsqrt(spread + 1e-05) * gain + offset


def feature(values):
    return jax.nn.elu(values) + 1.0


def segment_of(lengths_row, order_row, positions):
    places = jnp.arange(lengths_row.shape[0], dtype=jnp.int32)
    packed = jnp.sum(
        jnp.where(order_row[:, None] == places[None, :], lengths_row[None, :], 0), axis=1
    )
    ends = jnp.cumsum(packed)
    return jnp.sum((positions[:, None] >= ends[None, :]).astype(jnp.int32), axis=1)


def split_small(vector, width):
    pieces = [vector[index * width : (index + 1) * width] for index in range(9)]
    return pieces + [vector[9 * width :]]


def unit_rates(blocks):
    return jnp.array([0.5, 0.5, 0.5, 4.0] + [0.5] * blocks + [0.25] * blocks, dtype=jnp.float32)


def pack_state(matrix, totals, passes):
    flags = jnp.zeros_like(totals[:, None, :]) + passes
    return jnp.concatenate([matrix, totals[:, None, :], flags], axis=1)


def combine_states(earlier, later):
    scale = later[:, -1:, :]
    head_rows = later[:, :-1, :] + scale * earlier[:, :-1, :]
    return jnp.concatenate([head_rows, earlier[:, -1:, :] * scale], axis=1)


def relay_forward(own):

    def forward_turn(turn, running):
        return passed_along(combine_states(running, own), "seq", 1)

    arriving = lax.fori_loop(0, lax.axis_size("seq") - 1, forward_turn, jnp.zeros_like(own))
    return arriving


def relay_backward(own):

    def backward_turn(turn, running):
        return passed_along(combine_states(running, own).astype(jnp.bfloat16), "seq", -1).astype(
            jnp.float32
        )

    leaving = lax.fori_loop(0, lax.axis_size("seq") - 1, backward_turn, jnp.zeros_like(own))
    return leaving


def newton_schulz(matrices):
    norms = jnp.sqrt(jnp.sum(matrices * matrices, axis=(1, 2), keepdims=True))
    current = matrices / (norms + 1e-07)
    for turn in range(5):
        gram = jnp.einsum("sij,skj->sik", current, current, precision=highest)
        poly = -4.775 * gram + 2.0315 * jnp.einsum("sij,sjk->sik", gram, gram, precision=highest)
        current = 3.4445 * current + jnp.einsum("sij,sjk->sik", poly, current, precision=highest)
    return current


def local(
    tokens, cotangent, lengths, order, weights, momentum, small_params, moment_one, moment_two
):
    group = tokens.shape[1]
    width = tokens.shape[2]
    heads = HEADS
    depth = HEAD_DIM
    blocks = FF // D
    units = weights.shape[0]
    nseq = lax.axis_size("seq")
    gathered, small_low = (
        lax.all_gather(weights.astype(jnp.bfloat16), "seq", axis=1, tiled=True),
        lax.all_gather(small_params.astype(jnp.bfloat16), "seq", axis=0, tiled=True),
    )
    small = small_low.astype(jnp.float32)
    gain_one, bias_one, gain_two, bias_two, bias_q, bias_k, bias_v, bias_o, bias_down, bias_up = (
        split_small(small, width)
    )
    w_query = gathered[0]
    w_key = gathered[1]
    w_value = gathered[2]
    w_out = gathered[3]
    w_up = gathered[4 : 4 + blocks]
    w_down = gathered[4 + blocks :].reshape(blocks * width, width)
    start = lax.axis_index("seq") * group
    positions = start + jnp.arange(group, dtype=jnp.int32)
    segment = segment_of(lengths[0], order[0], positions)
    before = segment_of(lengths[0], order[0], jnp.reshape(start - 1, (1,)))[0]
    offsets = jnp.arange(group, dtype=jnp.int32)
    keep = ((offsets[None, :] <= offsets[:, None]) & (segment[:, None] == segment[None, :])).astype(
        jnp.float32
    )
    incoming = (segment == before).astype(jnp.float32)
    finals = (segment == segment[-1]).astype(jnp.float32)
    passes = (segment[-1] == before).astype(jnp.float32)
    inputs = tokens[0].astype(jnp.float32)
    normed = layer_norm(inputs, gain_one, bias_one).astype(jnp.bfloat16)
    query_pre = jnp.dot(normed, w_query, preferred_element_type=jnp.float32) + bias_q
    key_pre = jnp.dot(normed, w_key, preferred_element_type=jnp.float32) + bias_k
    value_pre = jnp.dot(normed, w_value, preferred_element_type=jnp.float32) + bias_v
    query_low = feature(query_pre).astype(jnp.bfloat16).reshape(group, heads, depth)
    key_low = feature(key_pre).astype(jnp.bfloat16).reshape(group, heads, depth)
    value_low = value_pre.astype(jnp.bfloat16).reshape(group, heads, depth)
    scores = (
        jnp.einsum("thd,shd->hts", query_low, key_low, preferred_element_type=jnp.float32)
        * keep[None]
    )
    denom = jnp.sum(scores, axis=2).T
    scores_low = scores.astype(jnp.bfloat16)
    numer = jnp.einsum("hts,she->the", scores_low, value_low, preferred_element_type=jnp.float32)
    keys_last = key_low * finals.astype(jnp.bfloat16)[:, None, None]
    own_state = jnp.einsum("shd,she->hde", keys_last, value_low, preferred_element_type=jnp.float32)
    own_total = jnp.sum(keys_last.astype(jnp.float32), axis=0)
    arriving = relay_forward(pack_state(own_state, own_total, passes))
    state_in = arriving[:, :depth, :]
    total_in = arriving[:, depth, :]
    query_wide = query_low.astype(jnp.float32)
    numer = numer + incoming[:, None, None] * jnp.einsum(
        "thd,hde->the", query_wide, state_in, precision=highest
    )
    denom = denom + incoming[:, None] * jnp.einsum(
        "thd,hd->th", query_wide, total_in, precision=highest
    )
    attended = (numer / denom[:, :, None]).reshape(group, width).astype(jnp.bfloat16)
    resid = inputs + jnp.dot(attended, w_out, preferred_element_type=jnp.float32) + bias_o
    hidden = layer_norm(resid, gain_two, bias_two).astype(jnp.bfloat16)
    up_pre = (
        jnp.einsum("td,jdf->tjf", hidden, w_up, preferred_element_type=jnp.float32).reshape(
            group, blocks * width
        )
        + bias_up
    )
    active = jax.nn.gelu(up_pre).astype(jnp.bfloat16)
    output = resid + jnp.dot(active, w_down, preferred_element_type=jnp.float32) + bias_down
    block_out = output.astype(jnp.bfloat16)[None]
    grad_out = cotangent[0]
    grad_down = jnp.einsum("tf,td->fd", active, grad_out, preferred_element_type=jnp.float32)
    grad_bias_down = jnp.sum(grad_out.astype(jnp.float32), axis=0)
    grad_active = jnp.einsum("td,fd->tf", grad_out, w_down, preferred_element_type=jnp.float32)
    _, gelu_pull = jax.vjp(jax.nn.gelu, up_pre)
    grad_up_low = gelu_pull(grad_active)[0].astype(jnp.bfloat16)
    grad_up_blocks = grad_up_low.reshape(group, blocks, width)
    grad_w_up = jnp.einsum(
        "td,tjf->jdf", hidden, grad_up_blocks, preferred_element_type=jnp.float32
    )
    grad_bias_up = jnp.sum(grad_up_low.astype(jnp.float32), axis=0)
    grad_hidden = jnp.einsum(
        "tjf,jdf->td", grad_up_blocks, w_up, preferred_element_type=jnp.float32
    )
    _, norm_two_pull = jax.vjp(layer_norm, resid, gain_two, bias_two)
    grad_resid_norm, grad_gain_two, grad_bias_two = norm_two_pull(grad_hidden)
    grad_resid = grad_out.astype(jnp.float32) + grad_resid_norm
    grad_branch = grad_resid.astype(jnp.bfloat16)
    grad_w_out = jnp.einsum("tk,td->kd", attended, grad_branch, preferred_element_type=jnp.float32)
    grad_bias_o = jnp.sum(grad_branch.astype(jnp.float32), axis=0)
    grad_ratio = jnp.einsum(
        "td,kd->tk", grad_branch, w_out, preferred_element_type=jnp.float32
    ).reshape(group, heads, depth)
    grad_numer = (grad_ratio / denom[:, :, None]).astype(jnp.bfloat16)
    grad_denom = -jnp.sum(grad_ratio * numer, axis=2) / (denom * denom)
    grad_scores = jnp.einsum(
        "the,she->hts", grad_numer, value_low, preferred_element_type=jnp.float32
    )
    grad_scores_low = ((grad_scores + grad_denom.T[:, :, None]) * keep[None]).astype(jnp.bfloat16)
    grad_query = jnp.einsum(
        "hts,shd->thd", grad_scores_low, key_low, preferred_element_type=jnp.float32
    )
    grad_key = jnp.einsum(
        "hts,thd->shd", grad_scores_low, query_low, preferred_element_type=jnp.float32
    )
    grad_value = jnp.einsum(
        "hts,the->she", scores_low, grad_numer, preferred_element_type=jnp.float32
    )
    numer_grad_wide = grad_numer.astype(jnp.float32)
    grad_query = grad_query + incoming[:, None, None] * (
        jnp.einsum("the,hde->thd", numer_grad_wide, state_in, precision=highest)
        + grad_denom[:, :, None] * total_in[None]
    )
    query_masked = query_low * incoming.astype(jnp.bfloat16)[:, None, None]
    grad_state_in = jnp.einsum(
        "thd,the->hde", query_masked, grad_numer, preferred_element_type=jnp.float32
    )
    grad_total_in = jnp.einsum(
        "thd,th->hd", query_wide * incoming[:, None, None], grad_denom, precision=highest
    )
    leaving = relay_backward(pack_state(grad_state_in, grad_total_in, passes))
    grad_state = leaving[:, :depth, :]
    grad_total = leaving[:, depth, :]
    value_wide = value_low.astype(jnp.float32)
    key_wide = key_low.astype(jnp.float32)
    grad_key = grad_key + finals[:, None, None] * (
        jnp.einsum("she,hde->shd", value_wide, grad_state, precision=highest) + grad_total[None]
    )
    grad_value = grad_value + finals[:, None, None] * jnp.einsum(
        "shd,hde->she", key_wide, grad_state, precision=highest
    )
    _, query_pull = jax.vjp(feature, query_pre)
    _, key_pull = jax.vjp(feature, key_pre)
    grad_query_low = query_pull(grad_query.reshape(group, width))[0].astype(jnp.bfloat16)
    grad_key_low = key_pull(grad_key.reshape(group, width))[0].astype(jnp.bfloat16)
    grad_value_low = grad_value.reshape(group, width).astype(jnp.bfloat16)
    grad_w_query = jnp.einsum(
        "tk,tj->kj", normed, grad_query_low, preferred_element_type=jnp.float32
    )
    grad_w_key = jnp.einsum("tk,tj->kj", normed, grad_key_low, preferred_element_type=jnp.float32)
    grad_w_value = jnp.einsum(
        "tk,tj->kj", normed, grad_value_low, preferred_element_type=jnp.float32
    )
    grad_bias_q = jnp.sum(grad_query_low.astype(jnp.float32), axis=0)
    grad_bias_k = jnp.sum(grad_key_low.astype(jnp.float32), axis=0)
    grad_bias_v = jnp.sum(grad_value_low.astype(jnp.float32), axis=0)
    grad_normed = jnp.einsum(
        "tj,kj->tk", grad_query_low, w_query, preferred_element_type=jnp.float32
    )
    grad_normed = grad_normed + jnp.einsum(
        "tj,kj->tk", grad_key_low, w_key, preferred_element_type=jnp.float32
    )
    grad_normed = grad_normed + jnp.einsum(
        "tj,kj->tk", grad_value_low, w_value, preferred_element_type=jnp.float32
    )
    _, norm_one_pull = jax.vjp(layer_norm, inputs, gain_one, bias_one)
    grad_inputs_norm, grad_gain_one, grad_bias_one = norm_one_pull(grad_normed)
    input_grad = (grad_resid + grad_inputs_norm)[None]
    grad_units = jnp.concatenate(
        [
            jnp.stack([grad_w_query, grad_w_key, grad_w_value, grad_w_out]),
            grad_w_up,
            grad_down.reshape(blocks, width, width),
        ],
        axis=0,
    )
    grad_small = jnp.concatenate(
        [
            grad_gain_one,
            grad_bias_one,
            grad_gain_two,
            grad_bias_two,
            grad_bias_q,
            grad_bias_k,
            grad_bias_v,
            grad_bias_o,
            grad_bias_down,
            grad_bias_up,
        ]
    )
    part_units, part_small = (
        lax.psum_scatter(grad_units, "seq", scatter_dimension=1, tiled=True),
        lax.psum_scatter(grad_small, "seq", scatter_dimension=0, tiled=True),
    )
    row_units, row_small = lax.psum((part_units, part_small), "stream")
    new_momentum = 0.5 * momentum + row_units
    slots_dev = (units + nseq - 1) // nseq
    spare = slots_dev * nseq - units
    outgoing = jnp.concatenate(
        [new_momentum, jnp.zeros((spare,) + new_momentum.shape[1:], jnp.float32)], axis=0
    )
    owned = lax.all_to_all(outgoing, "seq", split_axis=0, concat_axis=1, tiled=True)
    ortho = newton_schulz(owned)
    returned = lax.all_to_all(
        ortho.astype(jnp.bfloat16), "seq", split_axis=1, concat_axis=0, tiled=True
    ).astype(ortho.dtype)
    update = returned[:units]
    rates = unit_rates(blocks)
    new_weights = weights - rates[:, None, None] * (update + 0.01 * weights)
    first_new = 0.9 * moment_one + 0.1 * row_small
    second_new = 0.95 * moment_two + 0.05 * row_small * row_small
    adjusted = first_new / (1.0 - 0.9**STEP) / (jnp.sqrt(second_new / (1.0 - 0.95**STEP)) + 1e-08)
    new_small = small_params - 0.05 * (adjusted + 0.01 * small_params)
    return (block_out, input_grad, new_weights, new_momentum, new_small, first_new, second_new)


def solution(mesh):
    in_specs = (
        P("stream", "seq", None),
        P("stream", "seq", None),
        P("stream", None),
        P("stream", None),
        P(None, "seq", None),
        P(None, "seq", None),
        P("seq"),
        P("seq"),
        P("seq"),
    )
    out_specs = (
        P("stream", "seq", None),
        P("stream", "seq", None),
        P(None, "seq", None),
        P(None, "seq", None),
        P("seq"),
        P("seq"),
        P("seq"),
    )
    return jax.shard_map(local, mesh=mesh, in_specs=in_specs, out_specs=out_specs, check_vma=False)
```

profile of v0, /device:TPU:31, one launch (start us, length us, event | category | flops | bytes accessed | tf_op | source)
XLA Modules:
  0.0 2636.7 jit_solution(14871604133822994485)
XLA Ops:
  12.4 55.0 %all-gather = bf16[8,1,1664]{2,1,0:T(2,128)(2,1)S(1)} all-gather(bf16[1,1,1664]{2,1,0:T(2,128)(2,1)S(1)} %reshape.358), channel_id=1, replica_groups=mesh['seq'=8,'stream'=4] {'seq'}, dimensions={0}, use_global_device_ids=true | all-gather | bytes 29952 | tf_op jit(solution)/shard_map/all_gather | solution.py:103
  73.9 419.9 %all-gather.3.cloned.1.call-done = bf16[12,1024,1024]{2,1,0:T(8,128)(2,1)} async-done(((bf16[12,128,1024]{2,1,0:T(8,128)(2,1)}), bf16[12,1024,1024]{2,1,0:T(8,128)(2,1)}) %all-gather.3.cloned.1.call-update) | async-done | bytes 25165840 | tf_op jit(solution)/shard_map/all_gather | solution.py:102
  517.7 108.7 %while.29 = (s32[]{:T(128)}, f32[16,66,64]{1,2,0:T(8,128)S(1)}, f32[]{:T(128)}, f32[16,65,64]{1,2,0:T(8,128)}, s32[]{:T(128)}) while((s32[]{:T(128)}, f32[16,66,64]{1,2,0:T(8,128)S(1)}, f32[]{:T(128)}, f32[16,65,64]{1,2,0:T(8,128)}, s32[]{:T(128)}) %tuple.125), condition=%wide.region_8.9_spmd.clone.clone, body=%wide.region_7.8_spmd.clone.clone.sunk | while | flops 201730 | bytes 2429037 | solution.py:66
  521.3 13.8 collective-permute-done
  538.7 13.8 collective-permute-done
  556.1 12.9 collective-permute-done
  572.6 12.0 collective-permute-done
  588.2 11.1 collective-permute-done
  602.9 10.1 collective-permute-done
  616.6 9.5 collective-permute-done
  644.8 10.4 fusion.44
  655.2 8.7 copy.223
  663.9 8.9 copy.224
  672.9 7.7 slice.154
  680.5 16.0 convert_reduce_fusion
  696.6 14.9 copy.266
  711.5 11.1 fusion.93
  727.6 10.2 fusion.71
  755.5 75.3 %while.30 = (s32[]{:T(128)}, f32[16,66,64]{2,1,0:T(8,128)S(1)}, f32[]{:T(128)}, f32[16,65,64]{2,1,0:T(8,128)}, s32[]{:T(128)}, /*index=5*/s32[]{:T(128)}) while((s32[]{:T(128)}, f32[16,66,64]{2,1,0:T(8,128)S(1)}, f32[]{:T(128)}, f32[16,65,64]{2,1,0:T(8,128)}, s32[]{:T(128)}, /*index=5*/s32[]{:T(128)}) %tuple.128), condition=%wide.region_16.17_spmd.clone.clone.clone, body=%wide.region_15.16_spmd.clone.clone.clone.sunk | while | flops 607235 | bytes 2429055 | solution.py:77
  780.6 6.6 collective-permute-done.1
  868.4 8.6 bitcast_dynamic-update-slice_fusion
  877.0 6.5 copy.263
  883.5 10.5 convolution_dynamic-update-slice_fusion
  894.1 806.3 %reduce-scatter.2.cloned.1.call-done = f32[12,128,1024]{1,2,0:T(8,128)} async-done(((f32[12,1024,1024]{1,2,0:T(8,128)}), f32[12,128,1024]{1,2,0:T(8,128)}) %reduce-scatter.2.cloned.1.call-update) | async-done | bytes 6291472 | tf_op jit(solution)/shard_map/reduce_scatter | solution.py:277
  1700.4 6.6 copy.238
  1707.0 115.8 %all-reduce.4.cloned.1.call-done = f32[12,128,1024]{1,2,0:T(8,128)} async-done(((f32[12,128,1024]{1,2,0:T(8,128)}), f32[12,128,1024]{1,2,0:T(8,128)}) %all-reduce.4.cloned.1.call-update) | async-done | bytes 6291472 | tf_op jit(solution)/shard_map/psum | solution.py:280
  1830.7 186.2 %all_to_all.27 = f32[16,128,1024]{1,2,0:T(8,128)} all-to-all(f32[16,128,1024]{1,2,0:T(8,128)S(1)} %concatenate.33), channel_id=1, replica_groups=mesh['seq'=8,'stream'=4] {'seq'}, dimensions={0} | all-to-all | bytes 16777216 | tf_op jit(solution)/shard_map/all_to_all | solution.py:287
  2016.9 8.7 copy.246
  2033.3 26.9 %fusion.189 = f32[2,1024,1024]{2,1,0:T(8,128)S(1)} fusion(f32[2,1024,1024]{2,1,0:T(8,128)S(1)} %bitcast_divide_fusion), kind=kOutput, calls=%fused_computation.262 | convolution fusion | flops 25769803776 | bytes 16777216 | tf_op jit(solution)/shard_map/sij,skj->sik/dot_general | solution.py:85
  2063.5 29.3 %fusion.190 = f32[2,1024,1024]{2,1,0:T(8,128)} fusion(f32[2,1024,1024]{2,1,0:T(8,128)S(1)} %fusion.189), kind=kOutput, calls=%fused_computation.263 | convolution fusion | flops 25769803776 | bytes 16777216 | tf_op jit(solution)/shard_map/sij,sjk->sik/dot_general | solution.py:86
  2092.8 30.7 %multiply_add_fusion.4 = f32[2,1024,1024]{2,1,0:T(8,128)S(1)} fusion(f32[2,1024,1024]{2,1,0:T(8,128)S(1)} %bitcast_divide_fusion, f32[2,1024,1024]{2,1,0:T(8,128)} %fusion.190, f32[2,1024,1024]{2,1,0:T(8,128)} %copy-done.81), kind=kOutput, calls=%fused_computation.61 | convolution fusion | flops 25780289536 | bytes 33554432 | tf_op jit(solution)/shard_map/sij,sjk->sik/dot_general | solution.py:87
  2123.5 26.8 %fusion.191 = f32[2,1024,1024]{2,1,0:T(8,128)S(1)} fusion(f32[2,1024,1024]{2,1,0:T(8,128)S(1)} %multiply_add_fusion.4), kind=kOutput, calls=%fused_computation.264 | convolution fusion | flops 25769803776 | bytes 16777216 | tf_op jit(solution)/shard_map/sij,skj->sik/dot_general | solution.py:85
  2150.4 29.3 %fusion.192 = f32[2,1024,1024]{2,1,0:T(8,128)} fusion(f32[2,1024,1024]{2,1,0:T(8,128)S(1)} %fusion.191), kind=kOutput, calls=%fused_computation.265 | convolution fusion | flops 25769803776 | bytes 16777216 | tf_op jit(solution)/shard_map/sij,sjk->sik/dot_general | solution.py:86
  2179.7 29.8 %multiply_add_fusion.3 = f32[2,1024,1024]{2,1,0:T(8,128)S(1)} fusion(f32[2,1024,1024]{2,1,0:T(8,128)S(1)} %multiply_add_fusion.4, f32[2,1024,1024]{2,1,0:T(8,128)} %fusion.192, f32[2,1024,1024]{2,1,0:T(8,128)S(1)} %fusion.191), kind=kOutput, calls=%fused_computation.56 | convolution fusion | flops 25780289536 | bytes 33554432 | tf_op jit(solution)/shard_map/sij,sjk->sik/dot_general | solution.py:87
  2209.4 27.1 %fusion.193 = f32[2,1024,1024]{2,1,0:T(8,128)S(1)} fusion(f32[2,1024,1024]{2,1,0:T(8,128)S(1)} %multiply_add_fusion.3), kind=kOutput, calls=%fused_computation.266 | convolution fusion | flops 25769803776 | bytes 16777216 | tf_op jit(solution)/shard_map/sij,skj->sik/dot_general | solution.py:85
  2236.5 29.3 %fusion.194 = f32[2,1024,1024]{2,1,0:T(8,128)} fusion(f32[2,1024,1024]{2,1,0:T(8,128)S(1)} %fusion.193), kind=kOutput, calls=%fused_computation.267 | convolution fusion | flops 25769803776 | bytes 16777216 | tf_op jit(solution)/shard_map/sij,sjk->sik/dot_general | solution.py:86
  2265.8 29.8 %multiply_add_fusion.2 = f32[2,1024,1024]{2,1,0:T(8,128)S(1)} fusion(f32[2,1024,1024]{2,1,0:T(8,128)S(1)} %multiply_add_fusion.3, f32[2,1024,1024]{2,1,0:T(8,128)} %fusion.194, f32[2,1024,1024]{2,1,0:T(8,128)S(1)} %fusion.193), kind=kOutput, calls=%fused_computation.51 | convolution fusion | flops 25780289536 | bytes 33554432 | tf_op jit(solution)/shard_map/sij,sjk->sik/dot_general | solution.py:87
  2295.6 27.1 %fusion.195 = f32[2,1024,1024]{2,1,0:T(8,128)S(1)} fusion(f32[2,1024,1024]{2,1,0:T(8,128)S(1)} %multiply_add_fusion.2), kind=kOutput, calls=%fused_computation.268 | convolution fusion | flops 25769803776 | bytes 16777216 | tf_op jit(solution)/shard_map/sij,skj->sik/dot_general | solution.py:85
  2322.6 29.3 %fusion.196 = f32[2,1024,1024]{2,1,0:T(8,128)} fusion(f32[2,1024,1024]{2,1,0:T(8,128)S(1)} %fusion.195), kind=kOutput, calls=%fused_computation.269 | convolution fusion | flops 25769803776 | bytes 16777216 | tf_op jit(solution)/shard_map/sij,sjk->sik/dot_general | solution.py:86
  2351.9 29.8 %multiply_add_fusion.1 = f32[2,1024,1024]{2,1,0:T(8,128)S(1)} fusion(f32[2,1024,1024]{2,1,0:T(8,128)S(1)} %multiply_add_fusion.2, f32[2,1024,1024]{2,1,0:T(8,128)} %fusion.196, f32[2,1024,1024]{2,1,0:T(8,128)S(1)} %fusion.195), kind=kOutput, calls=%fused_computation.46 | convolution fusion | flops 25780289536 | bytes 33554432 | tf_op jit(solution)/shard_map/sij,sjk->sik/dot_general | solution.py:87
  2381.7 27.1 %fusion.197 = f32[2,1024,1024]{2,1,0:T(8,128)S(1)} fusion(f32[2,1024,1024]{2,1,0:T(8,128)S(1)} %multiply_add_fusion.1), kind=kOutput, calls=%fused_computation.270 | convolution fusion | flops 25769803776 | bytes 16777216 | tf_op jit(solution)/shard_map/sij,skj->sik/dot_general | solution.py:85
  2408.8 29.3 %fusion.198 = f32[2,1024,1024]{2,1,0:T(8,128)} fusion(f32[2,1024,1024]{2,1,0:T(8,128)S(1)} %fusion.197), kind=kOutput, calls=%fused_computation.271 | convolution fusion | flops 25769803776 | bytes 16777216 | tf_op jit(solution)/shard_map/sij,sjk->sik/dot_general | solution.py:86
  2438.0 29.9 %add_convert_fusion = bf16[2,1024,1024]{2,1,0:T(8,128)(2,1)S(1)} fusion(f32[2,1024,1024]{2,1,0:T(8,128)S(1)} %multiply_add_fusion.1, f32[2,1024,1024]{2,1,0:T(8,128)} %fusion.198, f32[2,1024,1024]{2,1,0:T(8,128)S(1)} %fusion.197), kind=kOutput, calls=%fused_computation.37 | convolution fusion | flops 25782386688 | bytes 29360128 | tf_op jit(solution)/shard_map/sij,sjk->sik/dot_general | solution.py:87
  2468.0 6.3 copy.247
  2494.5 95.3 %all-reduce.1 = f32[13312]{0:T(1024)S(1)} all-reduce(f32[13312]{0:T(1024)S(1)} %constant_dynamic-update-slice_fusion.1), channel_id=3, replica_groups=mesh['seq'=8,'stream'=4] {'seq'}, use_global_device_ids=true, to_apply=%region_32.33.clone | all-reduce | flops 13312 | bytes 106496
  2589.8 12.3 psum.15
  2602.8 12.2 fusion.119
  2615.0 6.6 copy.250
  (358 shorter events, 252.7 us)
Async XLA Ops:
  7.2 60.3 %copy-start.76 = (s32[1,4]{1,0:T(1,128)S(1)}, s32[1,4]{1,0:T(1,128)}, u32[]{:S(2)}) copy-start(s32[1,4]{1,0:T(1,128)} %param.16) | copy-start | bytes 52
  7.2 60.3 %copy-start.77 = (s32[1,4]{1,0:T(1,128)S(1)}, s32[1,4]{1,0:T(1,128)}, u32[]{:S(2)}) copy-start(s32[1,4]{1,0:T(1,128)} %param.17) | copy-start | bytes 52
  7.2 63.3 %copy-start.3 = (bf16[1,512,1024]{2,1,0:T(8,128)(2,1)S(1)}, bf16[1,512,1024]{2,1,0:T(8,128)(2,1)}, u32[]{:S(2)}) copy-start(bf16[1,512,1024]{2,1,0:T(8,128)(2,1)} %param.14) | copy-start | bytes 3145732
  7.2 486.6 %all-gather.3.cloned.1.call-start = ((), (), s32[]{:S(2)}) async-start(), calls=%async_computation.3 | async-start | bytes 28311552 | tf_op jit(solution)/shard_map/all_gather | solution.py:102
  12.3 1688.1 %reduce-scatter.2.cloned.1.call-start = ((), (), s32[]{:S(2)}) async-start(), calls=%async_computation.4 | async-start | bytes 56623104 | tf_op jit(solution)/shard_map/reduce_scatter | solution.py:277
  70.5 677.0 %copy-start.34 = (f32[4096]{0:T(1024)}, f32[4096]{0:T(1024)S(1)}, u32[]{:S(2)}) copy-start(f32[4096]{0:T(1024)S(1)} %slice.153) | copy-start | bytes 49156
  70.8 790.2 %copy-start.38 = (f32[512]{0:T(512)}, f32[512]{0:T(512)S(1)}, u32[]{:S(2)}) copy-start(f32[512]{0:T(512)S(1)} %broadcast_multiply_fusion.1) | copy-start | bytes 6148
  71.2 427.8 %copy-start.50 = (f32[512]{0:T(512)}, f32[512]{0:T(512)S(1)}, u32[]{:S(2)}) copy-start(f32[512]{0:T(512)S(1)} %fusion.84) | copy-start | bytes 6148
  71.2 437.2 %copy-start.45 = (f32[512]{0:T(512)}, f32[512]{0:T(512)S(1)}, u32[]{:S(2)}) copy-start(f32[512]{0:T(512)S(1)} %fusion.149) | copy-start | bytes 6148
  73.1 678.7 %copy-start.41 = (f32[512]{0:T(512)}, f32[512]{0:T(512)S(1)}, u32[]{:S(2)}) copy-start(f32[512]{0:T(512)S(1)} %get-tuple-element.337) | copy-start | bytes 6148
  73.7 425.3 %copy-start.56 = (f32[1024]{0:T(1024)}, f32[1024]{0:T(1024)S(1)}, u32[]{:S(2)}) copy-start(f32[1024]{0:T(1024)S(1)} %get-tuple-element.355) | copy-start | bytes 12292
  73.7 427.5 %copy-start.54 = (f32[1024]{0:T(1024)}, f32[1024]{0:T(1024)S(1)}, u32[]{:S(2)}) copy-start(f32[1024]{0:T(1024)S(1)} %get-tuple-element.354) | copy-start | bytes 12292
  73.7 434.7 %copy-start.71 = (f32[1024]{0:T(1024)}, f32[1024]{0:T(1024)S(1)}, u32[]{:S(2)}) copy-start(f32[1024]{0:T(1024)S(1)} %get-tuple-element.357) | copy-start | bytes 12292
  73.7 570.2 %copy-start.69 = (f32[1024]{0:T(1024)}, f32[1024]{0:T(1024)S(1)}, u32[]{:S(2)}) copy-start(f32[1024]{0:T(1024)S(1)} %get-tuple-element.351) | copy-start | bytes 12292
  73.7 648.9 %copy-start.62 = (f32[1024]{0:T(1024)}, f32[1024]{0:T(1024)S(1)}, u32[]{:S(2)}) copy-start(f32[1024]{0:T(1024)S(1)} %get-tuple-element.352) | copy-start | bytes 12292
  73.7 787.3 %copy-start.36 = (f32[1024]{0:T(1024)}, f32[1024]{0:T(1024)S(1)}, u32[]{:S(2)}) copy-start(f32[1024]{0:T(1024)S(1)} %get-tuple-element.358) | copy-start | bytes 12292
  520.0 15.1 collective-permute-start
  537.5 15.1 collective-permute-start
  554.8 14.2 collective-permute-start
  571.4 13.3 collective-permute-start
  586.9 12.3 collective-permute-start
  601.6 11.4 collective-permute-start
  615.3 10.7 collective-permute-start
  643.5 79.1 %copy-start.52 = (f32[512]{0:T(512)}, f32[512]{0:T(512)S(1)}, u32[]{:S(2)}) copy-start(f32[512]{0:T(512)S(1)} %broadcast_multiply_fusion) | copy-start | bytes 6148
  643.9 78.8 %copy-start.64 = (f32[512]{0:T(512)}, f32[512]{0:T(512)S(1)}, u32[]{:S(2)}) copy-start(f32[512]{0:T(512)S(1)} %fusion.150) | copy-start | bytes 6148
  672.9 7.7 copy-start.21
  711.5 11.1 copy-start.18
  727.6 10.3 copy-start.14
  727.6 10.3 copy-start.10
  740.4 7.1 slice-start
  755.5 79.7 %copy-start.11 = (bf16[512,1024]{0,1:T(8,128)(2,1)S(1)}, bf16[512,1024]{0,1:T(8,128)(2,1)}, u32[]{:S(2)}) copy-start(bf16[512,1024]{0,1:T(8,128)(2,1)} %copy.217) | copy-start | bytes 3145732
  756.8 7.9 collective-permute-start.1
  766.1 9.3 collective-permute-start.1
  776.8 10.4 collective-permute-start.1
  788.6 9.9 collective-permute-start.1
  799.8 9.2 collective-permute-start.1
  810.3 10.0 collective-permute-start.1
  821.7 9.1 collective-permute-start.1
  830.9 11.4 copy-start.42
  839.3 9.5 copy-start.55
  839.3 9.5 copy-start.57
  894.1 928.7 %all-reduce.4.cloned.1.call-start = ((), (), s32[]{:S(2)}) async-start(), calls=%async_computation.5 | async-start | bytes 12582912 | tf_op jit(solution)/shard_map/psum | solution.py:280
  2474.3 147.2 %all-to-all-start.1 = ((bf16[2,1024,1024]{2,0,1:T(2,128)(2,1)}), bf16[2,1024,1024]{2,0,1:T(2,128)(2,1)}, u32[]{:S(2)}, u32[]{:S(2)}) async-start(bf16[2,1024,1024]{2,0,1:T(2,128)(2,1)} %copy.247), calls=%async_computation.2 | async-start | bytes 8388608 | tf_op jit(solution)/shard_map/all_to_all | solution.py:289
  2491.0 111.1 %copy-start.44 = (f32[1664]{0:T(1024)S(1)}, f32[1664]{0:T(1024)}, u32[]{:S(2)}) copy-start(f32[1664]{0:T(1024)} %param.20) | copy-start | bytes 19972
  2491.0 111.1 %copy-start.66 = (f32[1664]{0:T(1024)S(1)}, f32[1664]{0:T(1024)}, u32[]{:S(2)}) copy-start(f32[1664]{0:T(1024)} %param.21) | copy-start | bytes 19972
  2491.1 111.1 %copy-start.67 = (f32[1664]{0:T(1024)S(1)}, f32[1664]{0:T(1024)}, u32[]{:S(2)}) copy-start(f32[1664]{0:T(1024)} %param.22) | copy-start | bytes 19972
  2491.1 111.7 %copy-start.20 = (f32[512,1024]{1,0:T(8,128)S(1)}, f32[512,1024]{1,0:T(8,128)}, u32[]{:S(2)}) copy-start(f32[512,1024]{1,0:T(8,128)} %copy-done.17) | copy-start | bytes 6291460
  2491.1 111.7 %copy-start.68 = (f32[1024]{0:T(1024)S(1)}, f32[1024]{0:T(1024)}, u32[]{:S(2)}) copy-start(f32[1024]{0:T(1024)} %get-tuple-element.350) | copy-start | bytes 12292
  (58 other events, 243.8 us)
Sparse Core Ops, SparseCore 0:
  12.4 481.3 all-gather.2
  894.2 806.1 reduce-scatter.1
  1702.9 119.8 all-reduce.3
where the time goes:
time: 2650 us; the launch traced here: 2640 us
  waiting for transfers between devices  1460 us (55%)
  matrix products  588 us (22%)
  blocking collectives  349 us (13%)
  local copies, waits for them, and re-layouts  109 us (4%)
  other arithmetic  66.7 us (3%)
  starting transfers between devices  44.9 us (2%)
    reduce_scatter x1, waiting for transfers between devices, local(): lax.psum_scatter(grad_units, 'seq', scatter_dimension=1, tiled=True)  806 us
    all_gather x1, waiting for transfers between devices, local(): lax.all_gather(weights.astype(jnp.bfloat16), 'seq', axis=1, tiled=True)  420 us
    all_to_all x1, blocking collectives, local(): lax.all_to_all(outgoing, 'seq', split_axis=0, concat_axis=1, tiled=True)  186 us
    dot_general x5, matrix products, newton_schulz(): jnp.einsum('sij,sjk->sik', poly, current, precision=highest)  150 us
    dot_general x5, matrix products, newton_schulz(): jnp.einsum('sij,sjk->sik', gram, gram, precision=highest)  146 us
    dot_general x5, matrix products, newton_schulz(): gram = jnp.einsum('sij,skj->sik', current, current, precision=highest)  135 us
    ppermute x14, waiting for transfers between devices, passed_along(): return lax.ppermute(array, axis, pairs)  119 us
    psum x1, waiting for transfers between devices, local(): row_units, row_small = lax.psum((part_units, part_small), 'stream')  116 us
  transfers between devices with their start and end apart: 18, of which 17 were waited for; matrix products, arithmetic and copies ran while one was open for 2% of the time, Pallas kernels for 0%

commit v1 on v0

--- a/solution.py
+++ b/solution.py
@@ -1,7 +1,607 @@
+import functools
+
 import jax
 import jax.numpy as jnp
 from jax import lax
+from jax.experimental import pallas as pl
+from jax.experimental.pallas import tpu as pltpu
 from jax.sharding import PartitionSpec as P
+
+MESH = pl.DeviceIdType.MESH
+DMA = pltpu.SemaphoreType.DMA
+ANY = pl.BlockSpec(memory_space=pl.ANY)
+VMEM = pl.BlockSpec(memory_space=pltpu.VMEM)
+VMEM_LIMIT = 62 << 20
+
+
+def places():
+    seq = lax.axis_index("seq")
+    stream = lax.axis_index("stream")
+    return seq // 2, seq % 2, stream // 2, stream % 2
+
+
+def device(z, x, y, c):
+    return {"seq": z * 2 + x, "stream": y * 2 + c}
+
+
+def greet(peers):
+    barrier = pltpu.get_barrier_semaphore()
+    for peer in peers:
+        pl.semaphore_signal(barrier, inc=1, device_id=peer, device_id_type=MESH)
+    pl.semaphore_wait(barrier, len(peers))
+
+
+def remote(source, target, sent, received, peer):
+    return pltpu.make_async_remote_copy(
+        src_ref=source,
+        dst_ref=target,
+        send_sem=sent,
+        recv_sem=received,
+        device_id=peer,
+        device_id_type=MESH,
+    )
+
+
+def others_along_seq(z, x, y, c, count):
+    straight = [device(lax.rem(z + k, count), x, y, c) for k in range(1, count)]
+    across = [device(lax.rem(z + k, count), 1 - x, y, c) for k in range(count)]
+    return straight, across
+
+
+def gather_kernel(
+    count, w_ref, small_ref, out_ref, small_out, own_sem, zs, zr, ps, pr, ss, sr
+):
+    batches = w_ref.shape[0]
+    z, x, y, c = places()
+    straight, across = others_along_seq(z, x, y, c, count)
+    pair = [device(z, 1 - x, y, c), device(z, x, 1 - y, c), device(z, x, y, 1 - c)]
+    greet(straight + across + pair[1:])
+    small = []
+    for k, peer in enumerate(straight + across):
+        small.append(remote(small_ref, small_out.at[z * 2 + x], ss.at[k], sr.at[k], peer))
+        small[-1].start()
+    own = [
+        pltpu.make_async_copy(w_ref, out_ref.at[:, :, :, z, x], own_sem.at[0]),
+        pltpu.make_async_copy(small_ref, small_out.at[z * 2 + x], own_sem.at[1]),
+    ]
+    spread = {}
+
+    def send_own(b):
+        for k in range(1, count):
+            spread[b, k] = remote(
+                w_ref.at[b, y, c], out_ref.at[b, y, c, z, x],
+                zs.at[b, k - 1], zr.at[b, k - 1], straight[k - 1],
+            )
+            spread[b, k].start()
+
+    send_own(0)
+    for copy in own:
+        copy.start()
+    first, second, third = [], [], []
+    total = batches * count
+
+    def send(kept, phase, index, source, target, peer):
+        kept.append(remote(source, target, ps.at[phase, index], pr.at[phase, index], peer))
+        kept[-1].start()
+
+    for step in range(total + 3):
+        index = step
+        if index < total:
+            b, k = divmod(index, count)
+            there = lax.rem(z - k + count, count)
+            if k == 0:
+                send(first, 0, index, w_ref.at[b, y, c], out_ref.at[b, y, c, z, x], pair[0])
+            else:
+                spread[b, k].wait_recv()
+                block = out_ref.at[b, y, c, there, x]
+                send(first, 0, index, block, block, pair[(k + b) % 2])
+            if k == min(1, count - 1) and b + 1 < batches:
+                send_own(b + 1)
+        index = step - 1
+        if 0 <= index < total:
+            b, k = divmod(index, count)
+            there = lax.rem(z - k + count, count)
+            first[index].wait_recv()
+            if k == 0:
+                block, peer = out_ref.at[b, y, c, z, 1 - x], pair[1]
+            elif (k + b) % 2 == 0:
+                block, peer = out_ref.at[b, y, c, there], pair[1]
+            else:
+                block, peer = out_ref.at[b, :, c, there, x], pair[0]
+            send(second, 1, index, block, block, peer)
+        index = step - 2
+        if 0 <= index < total:
+            b, k = divmod(index, count)
+            there = lax.rem(z - k + count, count)
+            second[index].wait_recv()
+            block = out_ref.at[b, :, c, z, 1 - x] if k == 0 else out_ref.at[b, :, c, there]
+            send(third, 2, index, block, block, pair[2])
+        index = step - 3
+        if 0 <= index < total:
+            third[index].wait_recv()
+    for copy in list(spread.values()) + first + second + third:
+        copy.wait_send()
+    for copy in small + own:
+        copy.wait()
+
+
+def gather(weights, small, nseq):
+    units, rows, width = weights.shape
+    count = nseq // 2
+    batches = units // 4
+    steps = batches * count
+    out, small_out = pl.pallas_call(
+        functools.partial(gather_kernel, count),
+        out_shape=(
+            jax.ShapeDtypeStruct((batches, 2, 2, count, 2, rows, width), weights.dtype),
+            jax.ShapeDtypeStruct((nseq,) + small.shape, small.dtype),
+        ),
+        in_specs=[VMEM, VMEM],
+        out_specs=[ANY, VMEM],
+        scratch_shapes=[
+            DMA((2,)),
+            DMA((batches, count - 1)),
+            DMA((batches, count - 1)),
+            DMA((3, steps)),
+            DMA((3, steps)),
+            DMA((nseq - 1,)),
+            DMA((nseq - 1,)),
+        ],
+        compiler_params=pltpu.CompilerParams(
+            collective_id=0, has_side_effects=True, vmem_limit_bytes=VMEM_LIMIT
+        ),
+    )(weights.reshape(batches, 2, 2, rows, width), small)
+    return out.reshape(units, nseq * rows, width), small_out
+
+
+CHUNK = 32
+
+
+def add_into(target, left, right):
+    rows = target.shape[-2]
+
+    def body(index, carry):
+        span = pl.ds(pl.multiple_of(index * CHUNK, CHUNK), CHUNK)
+        total = left[span, :].astype(jnp.float32) + right[span, :].astype(jnp.float32)
+        target[span, :] = total.astype(target.dtype)
+        return carry
+
+    lax.fori_loop(0, rows // CHUNK, body, 0)
+
+
+def reduce_kernel(
+    count, wide_ref, low_ref, small_ref, out_ref, small_out,
+    core_wide, core_low, own_wide, own_low, fs_wide, fs_low, fr_wide, fr_low, kept_first,
+    ss_wide, ss_low, sr_wide, sr_low, kept_second, zs_wide, zs_low, zr_wide, zr_low,
+    sm_recv, sm_part, sm_pair,
+    load_sem, cs, cr, fs, fr, es, er, zs, zr, ms, mr,
+):
+    z, x, y, c = places()
+    straight, across = others_along_seq(z, x, y, c, count)
+    pair = [device(z, 1 - x, y, c), device(z, x, 1 - y, c), device(z, x, y, 1 - c)]
+    greet(straight + across + pair[1:])
+    wide_count, low_count = wide_ref.shape[0], low_ref.shape[0]
+    order = [("low", b) for b in reversed(range(low_count))] + [
+        ("wide", b) for b in range(wide_count)
+    ]
+    steps = [(kind, b, k) for kind, b in order for k in range(count)]
+    total = len(steps)
+    small = []
+    seqs = [lax.rem(z + k, count) * 2 + x for k in range(1, count)] + [
+        lax.rem(z + k, count) * 2 + 1 - x for k in range(count)
+    ]
+    for k, (peer, there) in enumerate(zip(straight + across, seqs)):
+        small.append(remote(small_ref.at[there], sm_recv.at[k], ms.at[k], mr.at[k], peer))
+        small[-1].start()
+
+    def at(index):
+        kind, b, k = steps[index]
+        there = lax.rem(z + 1 + k, count)
+        source = wide_ref if kind == "wide" else low_ref
+        slot = b * count + k
+        return kind, b, k, there, source, slot
+
+    loads, cores, firsts, seconds, spread = [], [], [], [], {}
+    ring = 3
+
+    def pick(kind, wide, low):
+        return wide if kind == "wide" else low
+
+    def start_core(index):
+        kind, b, k, there, source, slot = at(index)
+        target = pick(kind, core_wide, core_low).at[slot]
+        copy = remote(source.at[b, :, 1 - c, there], target, cs.at[index], cr.at[index], pair[2])
+        copy.start()
+        cores.append(copy)
+
+    def start_load(index):
+        kind, b, k, there, source, slot = at(index)
+        target = pick(kind, own_wide, own_low).at[index % 2]
+        copy = pltpu.make_async_copy(source.at[b, :, c, there], target, load_sem.at[index])
+        copy.start()
+        loads.append(copy)
+
+    for index in range(min(3, total)):
+        start_core(index)
+    start_load(0)
+    for step in range(total + 3):
+        index = step
+        if index < total:
+            kind, b, k, there, source, slot = at(index)
+            if index + 1 < total:
+                start_load(index + 1)
+            if index + 3 < total:
+                start_core(index + 3)
+            loads[index].wait()
+            cores[index].wait_recv()
+            own = pick(kind, own_wide, own_low).at[index % 2]
+            got = pick(kind, core_wide, core_low).at[slot]
+            if index >= ring:
+                firsts[index - ring].wait_send()
+            out = pick(kind, fs_wide, fs_low).at[index % ring]
+            kept = kept_first.at[index % ring]
+            for j in range(2):
+                if k % 2 == 0:
+                    add_into(out.at[j], own.at[1 - y, j], got.at[1 - y, j])
+                    add_into(kept.at[j], own.at[y, j], got.at[y, j])
+                else:
+                    add_into(out.at[j], own.at[j, 1 - x], got.at[j, 1 - x])
+                    add_into(kept.at[j], own.at[j, x], got.at[j, x])
+            target = pick(kind, fr_wide, fr_low).at[slot]
+            copy = remote(out, target, fs.at[index], fr.at[index], pair[1 - k % 2])
+            copy.start()
+            firsts.append(copy)
+        index = step - 1
+        if 0 <= index < total:
+            kind, b, k, there, source, slot = at(index)
+            firsts[index].wait_recv()
+            kept = kept_first.at[index % ring]
+            got = pick(kind, fr_wide, fr_low).at[slot]
+            if index >= ring:
+                seconds[index - ring].wait_send()
+            out = pick(kind, ss_wide, ss_low).at[index % ring]
+            mine = x if k % 2 == 0 else y
+            add_into(out, kept.at[1 - mine], got.at[1 - mine])
+            add_into(kept_second.at[index % ring], kept.at[mine], got.at[mine])
+            target = pick(kind, sr_wide, sr_low).at[slot]
+            copy = remote(out, target, es.at[index], er.at[index], pair[k % 2])
+            copy.start()
+            seconds.append(copy)
+        index = step - 2
+        if 0 <= index < total:
+            kind, b, k, there, source, slot = at(index)
+            seconds[index].wait_recv()
+            got = pick(kind, sr_wide, sr_low).at[slot]
+            batch = b if kind == "wide" else wide_count + b
+            if k < count - 1:
+                out = pick(kind, zs_wide, zs_low).at[b, k]
+                add_into(out, kept_second.at[index % ring], got)
+                target = pick(kind, zr_wide, zr_low).at[b, k]
+                spread[index] = remote(out, target, zs.at[batch, k], zr.at[batch, k], straight[k])
+                spread[index].start()
+            else:
+                add_into(out_ref.at[batch], kept_second.at[index % ring], got)
+        index = step - 3
+        if 0 <= index < total:
+            kind, b, k, there, source, slot = at(index)
+            if k == count - 1:
+                batch = b if kind == "wide" else wide_count + b
+                for j in range(count - 1):
+                    spread[index - (count - 1) + j].wait_recv()
+                    add_into(out_ref.at[batch], out_ref.at[batch], pick(kind, zr_wide, zr_low).at[b, j])
+    part = small_ref[z * 2 + x]
+    for k, copy in enumerate(small):
+        copy.wait_recv()
+        part = part + sm_recv[k]
+    sm_part[0] = part
+    tail = []
+    for j in range(2):
+        copy = remote(sm_part.at[j], sm_pair.at[j], ms.at[len(small) + j], mr.at[len(small) + j], pair[1 + j])
+        copy.start()
+        copy.wait_recv()
+        tail.append(copy)
+        if j == 0:
+            sm_part[1] = sm_part[0] + sm_pair[0]
+        else:
+            small_out[...] = sm_part[1] + sm_pair[1]
+    for copy in small + tail + cores + firsts[-ring:] + seconds[-ring:] + list(spread.values()):
+        copy.wait_send()
+
+
+def reduce_rows(wide, low, small, nseq):
+    count = nseq // 2
+    wide_count, low_count = wide.shape[0] // 4, low.shape[0] // 4
+    width = wide.shape[-1]
+    rows = wide.shape[1] // nseq
+    batches = wide_count + low_count
+    steps = batches * count
+    wide = wide.reshape(wide_count, 2, 2, count, 2, rows, width)
+    low = low.reshape(low_count, 2, 2, count, 2, rows, width)
+    f32, bf16 = jnp.float32, jnp.bfloat16
+    V = pltpu.VMEM
+    nw, nl = wide_count * count, low_count * count
+    return pl.pallas_call(
+        functools.partial(reduce_kernel, count),
+        out_shape=(
+            jax.ShapeDtypeStruct((batches, rows, width), f32),
+            jax.ShapeDtypeStruct(small.shape[1:], f32),
+        ),
+        in_specs=[ANY, ANY, VMEM],
+        out_specs=[VMEM, VMEM],
+        scratch_shapes=[
+            V((nw, 2, 2, rows, width), f32),
+            V((nl, 2, 2, rows, width), bf16),
+            V((2, 2, 2, rows, width), f32),
+            V((2, 2, 2, rows, width), bf16),
+            V((3, 2, rows, width), f32),
+            V((3, 2, rows, width), bf16),
+            V((nw, 2, rows, width), f32),
+            V((nl, 2, rows, width), bf16),
+            V((3, 2, rows, width), f32),
+            V((3, rows, width), f32),
+            V((3, rows, width), bf16),
+            V((nw, rows, width), f32),
+            V((nl, rows, width), bf16),
+            V((3, rows, width), f32),
+            V((wide_count, count - 1, rows, width), f32),
+            V((low_count, count - 1, rows, width), bf16),
+            V((wide_count, count - 1, rows, width), f32),
+            V((low_count, count - 1, rows, width), bf16),
+            V((nseq - 1,) + small.shape[1:], f32),
+            V((2,) + small.shape[1:], f32),
+            V((2,) + small.shape[1:], f32),
+            DMA((steps,)),
+            DMA((steps,)),
+            DMA((steps,)),
+            DMA((steps,)),
+            DMA((steps,)),
+            DMA((steps,)),
+            DMA((steps,)),
+            DMA((batches, count - 1)),
+            DMA((batches, count - 1)),
+            DMA((nseq + 1,)),
+            DMA((nseq + 1,)),
+        ],
+        compiler_params=pltpu.CompilerParams(
+            collective_id=1, has_side_effects=True, vmem_limit_bytes=VMEM_LIMIT
+        ),
+    )(wide, low, small)
+
+
+SHIFTS = (0.0, 0.0, 0.1, 0.7, 0.7)
+FINE = (False, False, False, True, True)
+BAND = 256
+
+
+def split_two(values):
+    high = values.astype(jnp.bfloat16)
+    return high, (values - high.astype(jnp.float32)).astype(jnp.bfloat16)
+
+
+def dot(left, right, transposed=False):
+    dims = (((1,), (1 if transposed else 0,)), ((), ()))
+    return lax.dot_general(left, right, dims, preferred_element_type=jnp.float32)
+
+
+def orthogonalize(full, xh, xl, gram, gram_low):
+    size = full.shape[0]
+    bands = size // BAND
+
+    def span(index):
+        return pl.ds(pl.multiple_of(index * BAND, BAND), BAND)
+
+    def square(index, total):
+        part = full[span(index), :]
+        return total + jnp.sum(part * part)
+
+    norm = jnp.sqrt(lax.fori_loop(0, bands, square, jnp.float32(0.0)))
+    scale = 1.0 / (norm + 1e-07)
+
+    def begin(index, carry):
+        part = full[span(index), :] * scale
+        full[span(index), :] = part
+        xh[0, span(index), :] = part.astype(jnp.bfloat16)
+        return carry
+
+    lax.fori_loop(0, bands, begin, 0)
+    for turn in range(len(SHIFTS)):
+        shift, fine = SHIFTS[turn], FINE[turn]
+        now, later = turn % 2, 1 - turn % 2
+        more = turn + 1 < len(SHIFTS) and FINE[turn + 1]
+
+        def form(index, carry):
+            rows = span(index)
+            left = xh[now, rows, :]
+            block = dot(left, xh[now], True)
+            if fine:
+                block += dot(left, xl[now], True) + dot(xl[now, rows, :], xh[now], True)
+            if shift:
+                across = lax.broadcasted_iota(jnp.int32, block.shape, 1)
+                down = lax.broadcasted_iota(jnp.int32, block.shape, 0) + index * BAND
+                block = jnp.where(across == down, block - shift, block)
+            gram[rows, :] = block
+            gram_low[rows, :] = block.astype(jnp.bfloat16)
+            return carry
+
+        lax.fori_loop(0, bands, form, 0)
+        linear = -4.775 + 2.0 * 2.0315 * shift
+        scaled = 3.4445 - 4.775 * shift + 2.0315 * shift * shift
+
+        def advance(index, carry):
+            rows = span(index)
+            poly = linear * gram[rows, :] + 2.0315 * dot(gram_low[rows, :], gram_low[...])
+            if fine:
+                high, low = split_two(poly)
+                step = dot(high, xh[now]) + dot(high, xl[now]) + dot(low, xh[now])
+            else:
+                step = dot(poly.astype(jnp.bfloat16), xh[now])
+            moved = scaled * full[rows, :] + step
+            full[rows, :] = moved
+            if more:
+                high, low = split_two(moved)
+                xh[later, rows, :] = high
+                xl[later, rows, :] = low
+            else:
+                xh[later, rows, :] = moved.astype(jnp.bfloat16)
+            return carry
+
+        lax.fori_loop(0, bands, advance, 0)
+    return len(SHIFTS) % 2
+
+
+def muon_kernel(
+    count, g_ref, mom_ref, all_ref, rows_ref,
+    mom_own, moved, full, xh, xl, gram, gram_low,
+    load_sem, own_sem, ms, mr, ys, yr, os_, or_, fs, fr, gs, gr,
+):
+    z, x, y, c = places()
+    seq = z * 2 + x
+    nseq = count * 2
+    batches, rows, width = g_ref.shape
+    straight, across = others_along_seq(z, x, y, c, count)
+    pair = [device(z, x, 1 - y, c), device(z, x, y, 1 - c)]
+    greet(straight + across + pair)
+    load = pltpu.make_async_copy(mom_ref.at[:, y, c], mom_own, load_sem)
+    load.start()
+    keep = pltpu.make_async_copy(g_ref, all_ref.at[:, y, c], own_sem.at[0])
+    keep.start()
+    load.wait()
+    owner = [2 * b + c + 1 for b in range(batches)]
+
+    def block(where):
+        return full.at[pl.ds(pl.multiple_of(where * rows, rows), rows)]
+
+    for b in range(batches):
+        for j in range(rows // CHUNK):
+            span = slice(j * CHUNK, (j + 1) * CHUNK)
+            moved[b, span, :] = 0.5 * mom_own[b, span, :] + g_ref[b, span, :]
+
+        @pl.when(seq != owner[b])
+        def _():
+            remote(
+                moved.at[b], block(seq), ms.at[b], mr.at[seq],
+                {"seq": owner[b], "stream": y * 2 + c},
+            ).start()
+
+        @pl.when(seq == owner[b])
+        def _():
+            pltpu.make_async_copy(moved.at[b], block(seq), own_sem.at[1]).start()
+
+    over = remote(g_ref, all_ref.at[:, y, c], ys.at[0], yr.at[0], pair[0])
+    over.start()
+    is_owner = (seq == owner[0]) | (seq == owner[1]) | (seq == owner[2])
+
+    @pl.when(is_owner)
+    def _():
+        pltpu.make_async_copy(moved.at[0], block(seq), own_sem.at[1]).wait()
+        for k in range(1, nseq):
+            there = lax.rem(seq + k, nseq)
+            remote(moved.at[0], block(there), ms.at[0], mr.at[there], pair[0]).wait_recv()
+        orthogonalize(full, xh, xl, gram, gram_low)
+
+    final = len(SHIFTS) % 2
+
+    def result(where):
+        return xh.at[final, pl.ds(pl.multiple_of(where * rows, rows), rows)]
+
+    for b in range(batches):
+        target = rows_ref.at[b, y, c]
+
+        @pl.when(seq == owner[b])
+        def _():
+            pltpu.make_async_copy(result(seq), target, own_sem.at[2]).start()
+            for k in range(1, nseq):
+                there = lax.rem(seq + k, nseq)
+                remote(
+                    result(there), target, os_.at[k - 1], or_.at[b],
+                    {"seq": there, "stream": y * 2 + c},
+                ).start()
+
+    keep.wait()
+    over.wait_recv()
+    share = remote(all_ref.at[:, :, c], all_ref.at[:, :, c], ys.at[1], yr.at[1], pair[1])
+    share.start()
+    hops = []
+    for b in range(batches):
+        target = rows_ref.at[b, y, c]
+
+        @pl.when(seq == owner[b])
+        def _():
+            pltpu.make_async_copy(result(seq), target, own_sem.at[2]).wait()
+
+        @pl.when(seq != owner[b])
+        def _():
+            remote(result(seq), target, os_.at[0], or_.at[b], pair[0]).wait_recv()
+
+        hop = remote(target, target, fs.at[b], fr.at[b], pair[0])
+        hop.start()
+        hops.append(hop)
+    lasts = []
+    for b in range(batches):
+        hops[b].wait_recv()
+        target = rows_ref.at[b, :, c]
+        last = remote(target, target, gs.at[b], gr.at[b], pair[1])
+        last.start()
+        lasts.append(last)
+    for last in lasts:
+        last.wait_recv()
+    share.wait_recv()
+    for copy in [over, share] + hops + lasts:
+        copy.wait_send()
+    for b in range(batches):
+
+        @pl.when(seq != owner[b])
+        def _():
+            remote(moved.at[b], block(seq), ms.at[b], mr.at[seq], pair[0]).wait_send()
+
+        @pl.when(seq == owner[b])
+        def _():
+            for k in range(1, nseq):
+                there = lax.rem(seq + k, nseq)
+                remote(result(there), rows_ref.at[b, y, c], os_.at[k - 1], or_.at[b], pair[0]).wait_send()
+
+
+def muon(sums, momentum, nseq):
+    count = nseq // 2
+    batches, rows, width = sums.shape
+    units = momentum.shape[0]
+    f32, bf16 = jnp.float32, jnp.bfloat16
+    V = pltpu.VMEM
+    whole, ortho = pl.pallas_call(
+        functools.partial(muon_kernel, count),
+        out_shape=(
+            jax.ShapeDtypeStruct((batches, 2, 2, rows, width), f32),
+            jax.ShapeDtypeStruct((batches, 2, 2, rows, width), bf16),
+        ),
+        in_specs=[VMEM, ANY],
+        out_specs=[ANY, ANY],
+        scratch_shapes=[
+            V((batches, rows, width), f32),
+            V((batches, rows, width), f32),
+            V((width, width), f32),
+            V((2, width, width), bf16),
+            V((2, width, width), bf16),
+            V((width, width), f32),
+            V((width, width), bf16),
+            DMA,
+            DMA((3,)),
+            DMA((batches,)),
+            DMA((nseq,)),
+            DMA((2,)),
+            DMA((2,)),
+            DMA((nseq - 1,)),
+            DMA((batches,)),
+            DMA((batches,)),
+            DMA((batches,)),
+            DMA((batches,)),
+            DMA((batches,)),
+        ],
+        compiler_params=pltpu.CompilerParams(
+            collective_id=2, has_side_effects=True, vmem_limit_bytes=VMEM_LIMIT
+        ),
+    )(sums, momentum.reshape(batches, 2, 2, rows, width))
+    return whole.reshape(units, rows, width), ortho.reshape(units, rows, width)
+
 
 D = 1024
 HEADS = 16
@@ -78,14 +678,10 @@
     return leaving
 
 
-def newton_schulz(matrices):
-    norms = jnp.sqrt(jnp.sum(matrices * matrices, axis=(1, 2), keepdims=True))
-    current = matrices / (norms + 1e-07)
-    for turn in range(5):
-        gram = jnp.einsum("sij,skj->sik", current, current, precision=highest)
-        poly = -4.775 * gram + 2.0315 * jnp.einsum("sij,sjk->sik", gram, gram, precision=highest)
-        current = 3.4445 * current + jnp.einsum("sij,sjk->sik", poly, current, precision=highest)
-    return current
+def padded(vector):
+    short = 2048 - vector.shape[-1]
+    edges = [(0, 0)] * (vector.ndim - 1) + [(0, short)]
+    return jnp.pad(vector, edges).reshape(vector.shape[:-1] + (16, 128))
 
 
 def local(
@@ -98,10 +694,11 @@
     blocks = FF // D
     units = weights.shape[0]
     nseq = lax.axis_size("seq")
-    gathered, small_low = (
-        lax.all_gather(weights.astype(jnp.bfloat16), "seq", axis=1, tiled=True),
-        lax.all_gather(small_params.astype(jnp.bfloat16), "seq", axis=0, tiled=True),
-    )
+    share = small_params.shape[0]
+    gathered, small_low = gather(
+        weights.astype(jnp.bfloat16), padded(small_params.astype(jnp.bfloat16)), nseq
+    )
+    small_low = small_low.reshape(nseq, 2048)[:, :share].reshape(nseq * share)
     small = small_low.astype(jnp.float32)
     gain_one, bias_one, gain_two, bias_two, bias_q, bias_k, bias_v, bias_o, bias_down, bias_up = (
         split_small(small, width)
@@ -251,14 +848,10 @@
     _, norm_one_pull = jax.vjp(layer_norm, inputs, gain_one, bias_one)
     grad_inputs_norm, grad_gain_one, grad_bias_one = norm_one_pull(grad_normed)
     input_grad = (grad_resid + grad_inputs_norm)[None]
-    grad_units = jnp.concatenate(
-        [
-            jnp.stack([grad_w_query, grad_w_key, grad_w_value, grad_w_out]),
-            grad_w_up,
-            grad_down.reshape(blocks, width, width),
-        ],
-        axis=0,
-    )
+    grad_wide = jnp.stack([grad_w_query, grad_w_key, grad_w_value, grad_w_out])
+    grad_low = jnp.concatenate(
+        [grad_w_up, grad_down.reshape(blocks, width, width)], axis=0
+    ).astype(jnp.bfloat16)
     grad_small = jnp.concatenate(
         [
             grad_gain_one,
@@ -273,23 +866,13 @@
             grad_bias_up,
         ]
     )
-    part_units, part_small = (
-        lax.psum_scatter(grad_units, "seq", scatter_dimension=1, tiled=True),
-        lax.psum_scatter(grad_small, "seq", scatter_dimension=0, tiled=True),
-    )
-    row_units, row_small = lax.psum((part_units, part_small), "stream")
+    sums, row_small = reduce_rows(
+        grad_wide, grad_low, padded(grad_small.reshape(nseq, share)), nseq
+    )
+    row_small = row_small.reshape(2048)[:share]
+    row_units, update = muon(sums, momentum, nseq)
     new_momentum = 0.5 * momentum + row_units
-    slots_dev = (units + nseq - 1) // nseq
-    spare = slots_dev * nseq - units
-    outgoing = jnp.concatenate(
-        [new_momentum, jnp.zeros((spare,) + new_momentum.shape[1:], jnp.float32)], axis=0
-    )
-    owned = lax.all_to_all(outgoing, "seq", split_axis=0, concat_axis=1, tiled=True)
-    ortho = newton_schulz(owned)
-    returned = lax.all_to_all(
-        ortho.astype(jnp.bfloat16), "seq", split_axis=1, concat_axis=0, tiled=True
-    ).astype(ortho.dtype)
-    update = returned[:units]
+    update = update.astype(jnp.float32)
     rates = unit_rates(blocks)
     new_weights = weights - rates[:, None, None] * (update + 0.01 * weights)
     first_new = 0.9 * moment_one + 0.1 * row_small

time: 2650 us -> 935 us (0.35)
  waiting for transfers between devices: 1460 us -> 120 us
  Pallas kernels: 0 us -> 472 us
  matrix products: 588 us -> 161 us
  blocking collectives: 349 us -> 0 us
  local copies, waits for them, and re-layouts: 109 us -> 54.7 us
    reduce_scatter x1 -> x0, waiting for transfers between devices: 806 us -> none  [local(): lax.psum_scatter(grad_units, 'seq', scatter_dimension=1, tiled=True)]
    pallas_call x0 -> x3, Pallas kernels: none -> 472 us  [the longest x1 196 us: reduce_rows(): pl.pallas_call(functools.partial(reduce_kernel, count), out_shape=(jax.Sh...]
    dot_general x15 -> x0, matrix products: 431 us -> none  [the longest x5 150 us: newton_schulz(): jnp.einsum('sij,sjk->sik', poly, current, precision=highest)]
    all_gather x1 -> x0, waiting for transfers between devices: 420 us -> none  [local(): lax.all_gather(weights.astype(jnp.bfloat16), 'seq', axis=1, tiled=True)]
    all_to_all x1 -> x0, blocking collectives: 186 us -> none  [local(): lax.all_to_all(outgoing, 'seq', split_axis=0, concat_axis=1, tiled=True)]
    psum x1 -> x0, waiting for transfers between devices: 116 us -> none  [local(): row_units, row_small = lax.psum((part_units, part_small), 'stream')]
    unnamed x1 -> x0, blocking collectives: 95.3 us -> none
    all_gather x1 -> x0, blocking collectives: 55 us -> none  [local(): lax.all_gather(small_params.astype(jnp.bfloat16), 'seq', axis=0, tiled=True)]
  transfers between devices with their start and end apart: 18 -> 14, of which waited for: 17 -> 14; matrix products, arithmetic and copies ran while one was open for 2% -> 0% of each run, Pallas kernels for 0% -> 0%
where the time goes in v1:
time: 935 us; the launch traced here: 924 us
  Pallas kernels  472 us (50%)
  matrix products  161 us (17%)
  waiting for transfers between devices  120 us (13%)
  other arithmetic  74.1 us (8%)
  local copies, waits for them, and re-layouts  54.7 us (6%)
  starting transfers between devices  38.1 us (4%)
    pallas_call x1, Pallas kernels, reduce_rows(): pl.pallas_call(functools.partial(reduce_kernel, count), out_shape=(jax.Sh...  196 us
    pallas_call x1, Pallas kernels, muon(): pl.pallas_call(functools.partial(muon_kernel, count), out_shape=(jax.Shap...  139 us
    pallas_call x1, Pallas kernels, gather(): pl.pallas_call(functools.partial(gather_kernel, count), out_shape=(jax.Sh...  137 us
    ppermute x14, waiting for transfers between devices, passed_along(): return lax.ppermute(array, axis, pairs)  120 us
    ppermute x14, starting transfers between devices, passed_along(): return lax.ppermute(array, axis, pairs)  38.1 us
  transfers between devices with their start and end apart: 14, of which 14 were waited for; matrix products, arithmetic and copies ran while one was open for 0% of the time, Pallas kernels for 0%

profile of v1, /device:TPU:31, one launch (start us, length us, event | category | flops | bytes accessed | tf_op | source)
XLA Modules:
  0.0 924.0 jit_solution(12225502508103799206)
XLA Ops:
  0.6 5.0 convert_element_type.211
  6.2 137.2 %shard_map.153 = (bf16[3,2,2,4,2,128,1024]{6,5,4,3,2,1,0:T(8,128)(2,1)}, bf16[8,16,128]{2,1,0:T(8,128)(2,1)}) custom-call(bf16[3,2,2,128,1024]{4,3,2,1,0:T(8,128)(2,1)} %bitcast.298, bf16[16,128]{1,0:T(8,128)(2,1)} %pad_bitcast_fusion.1.small_ref), custom_call_target="tpu_custom_call" | custom-call | tf_op jit(solution)/shard_map/pallas_call | solution.py:133
  145.7 5.1 fusion.68
  156.2 5.3 convert_reduce_fusion.7
  163.1 9.4 %multiply_reduce_fusion = (f32[16,512]{1,0:T(8,128)S(1)}, f32[16,512,512]{1,2,0:T(8,128)}) fusion(f32[512,512]{0,1:T(8,128)S(1)} %fusion.92, bf16[512,16,64]{0,2,1:T(8,128)(2,1)} %bitcast.279, bf16[512,16,64]{0,2,1:T(8,128)(2,1)S(1)} %bitcast.275), kind=kOutput, calls=%fused_computation.15 | convolution fusion | flops 545251328 | bytes 19955712 | tf_op jit(solution)/shard_map/thd,shd->hts/dot_general | solution.py:732
  174.9 4.2 add_convert_fusion.5
  183.4 103.3 %while.29 = (s32[]{:T(128)}, f32[16,66,64]{1,2,0:T(8,128)S(1)}, f32[]{:T(128)}, f32[16,65,64]{1,2,0:T(8,128)S(1)}, s32[]{:T(128)}) while((s32[]{:T(128)}, f32[16,66,64]{1,2,0:T(8,128)S(1)}, f32[]{:T(128)}, f32[16,65,64]{1,2,0:T(8,128)S(1)}, s32[]{:T(128)}) %tuple.118), condition=%wide.region_8.9_spmd.clone.clone, body=%wide.region_7.8_spmd.clone.clone.sunk | while | flops 201730 | bytes 2429037 | solution.py:666
  186.0 14.3 %collective-permute-done = f32[16,66,64]{1,2,0:T(8,128)S(1)} collective-permute-done((f32[16,66,64]{1,2,0:T(8,128)}, f32[16,66,64]{1,2,0:T(8,128)S(1)}, u32[]{:S(2)}, u32[]{:S(2)}) %collective-permute-start) | collective-permute-done | bytes 270368 | tf_op jit(solution)/shard_map/while/body/eval_jaxpr/ppermute | solution.py:619
  202.8 13.4 %collective-permute-done = f32[16,66,64]{1,2,0:T(8,128)S(1)} collective-permute-done((f32[16,66,64]{1,2,0:T(8,128)}, f32[16,66,64]{1,2,0:T(8,128)S(1)}, u32[]{:S(2)}, u32[]{:S(2)}) %collective-permute-start) | collective-permute-done | bytes 270368 | tf_op jit(solution)/shard_map/while/body/eval_jaxpr/ppermute | solution.py:619
  218.8 13.4 %collective-permute-done = f32[16,66,64]{1,2,0:T(8,128)S(1)} collective-permute-done((f32[16,66,64]{1,2,0:T(8,128)}, f32[16,66,64]{1,2,0:T(8,128)S(1)}, u32[]{:S(2)}, u32[]{:S(2)}) %collective-permute-start) | collective-permute-done | bytes 270368 | tf_op jit(solution)/shard_map/while/body/eval_jaxpr/ppermute | solution.py:619
  234.7 12.5 %collective-permute-done = f32[16,66,64]{1,2,0:T(8,128)S(1)} collective-permute-done((f32[16,66,64]{1,2,0:T(8,128)}, f32[16,66,64]{1,2,0:T(8,128)S(1)}, u32[]{:S(2)}, u32[]{:S(2)}) %collective-permute-start) | collective-permute-done | bytes 270368 | tf_op jit(solution)/shard_map/while/body/eval_jaxpr/ppermute | solution.py:619
  249.8 11.5 %collective-permute-done = f32[16,66,64]{1,2,0:T(8,128)S(1)} collective-permute-done((f32[16,66,64]{1,2,0:T(8,128)}, f32[16,66,64]{1,2,0:T(8,128)S(1)}, u32[]{:S(2)}, u32[]{:S(2)}) %collective-permute-start) | collective-permute-done | bytes 270368 | tf_op jit(solution)/shard_map/while/body/eval_jaxpr/ppermute | solution.py:619
  263.9 10.6 %collective-permute-done = f32[16,66,64]{1,2,0:T(8,128)S(1)} collective-permute-done((f32[16,66,64]{1,2,0:T(8,128)}, f32[16,66,64]{1,2,0:T(8,128)S(1)}, u32[]{:S(2)}, u32[]{:S(2)}) %collective-permute-start) | collective-permute-done | bytes 270368 | tf_op jit(solution)/shard_map/while/body/eval_jaxpr/ppermute | solution.py:619
  277.1 9.5 %collective-permute-done = f32[16,66,64]{1,2,0:T(8,128)S(1)} collective-permute-done((f32[16,66,64]{1,2,0:T(8,128)}, f32[16,66,64]{1,2,0:T(8,128)S(1)}, u32[]{:S(2)}, u32[]{:S(2)}) %collective-permute-start) | collective-permute-done | bytes 270368 | tf_op jit(solution)/shard_map/while/body/eval_jaxpr/ppermute | solution.py:619
  288.8 8.1 fusion.34
  299.4 4.6 fusion.132
  303.9 11.9 %fusion.130 = (bf16[1,2,2,4,2,128,1024]{6,5,4,3,2,1,0:T(8,128)(2,1)}, bf16[1,2,2,4,2,128,1024]{6,5,4,3,2,1,0:T(8,128)(2,1)}) fusion(bf16[3,2,2,4,2,128,1024]{6,5,4,3,2,1,0:T(8,128)(2,1)} %get-tuple-element.152), kind=kLoop, calls=%fused_computation.219 | loop fusion | bytes 33554432 | tf_op jit(solution)/shard_map/slice | solution.py:710
  315.9 11.4 %copy.125 = bf16[4,1024,1024]{2,1,0:T(8,128)(2,1)} copy(bf16[4,1024,1024]{1,2,0:T(8,128)(2,1)} %bitcast.271) | data formatting | bytes 16777216 | tf_op jit(solution)/shard_map/td,jdf->tjf/dot_general | solution.py:755
  329.5 13.7 %fusion.21 = (bf16[4096,512]{0,1:T(8,128)(2,1)}, f32[512,4096]{1,0:T(8,128)}) fusion(f32[4096]{0:T(1024)S(1)} %slice.148, bf16[4096,1024]{1,0:T(8,128)(2,1)} %bitcast.299, f32[512,1024]{1,0:T(8,128)S(1)} %copy-done.13, f32[1024]{0:T(1024)S(1)} %get-tuple-element.308, f32[1024]{0:T(1024)S(1)} %get-tuple-element.309, f32[512]{0:T(512)S(1)} %fusion.107, ...), kind=kOutput, calls=%fused_computation.34 | convolution fusion | flops 4318560256 | bytes 23097344 | tf_op jit(solution)/shard_map/td,jdf->tjf/dot_general | solution.py:755
  343.2 10.1 %fusion.77 = bf16[1,512,1024]{2,1,0:T(8,128)(2,1)} fusion(f32[512,1024]{1,0:T(8,128)S(1)} %copy-done.13, bf16[4096,1024]{1,0:T(8,128)(2,1)S(1)} %bitcast.305, f32[512,4096]{1,0:T(8,128)} %get-tuple-element.330, f32[4096]{0:T(1024)S(1)} %slice.148, f32[1024]{0:T(1024)S(1)} %get-tuple-element.307), kind=kOutput, calls=%fused_computation.138 | convolution fusion | flops 4317511680 | bytes 19943424 | tf_op jit(solution)/shard_map/dot_general | solution.py:761
  355.3 16.7 %convert_reduce_fusion = (f32[4096]{0:T(1024)}, bf16[512,4096]{1,0:T(8,128)(2,1)}) fusion(f32[512,4096]{1,0:T(8,128)} %get-tuple-element.330, f32[4096]{0:T(1024)S(1)} %slice.148, bf16[4096,1024]{1,0:T(8,128)(2,1)} %bitcast.302, bf16[1,512,1024]{2,1,0:T(8,128)(2,1)S(1)} %copy-done.16), kind=kOutput, calls=%fused_computation.40 | convolution fusion | flops 4343197696 | bytes 22052864 | tf_op jit(solution)/shard_map/td,fd->tf/dot_general | solution.py:766
  371.9 9.0 fusion.55
  388.2 9.8 %fusion.33 = f32[16,64,512]{2,1,0:T(8,128)} fusion(bf16[512,16,64]{0,2,1:T(8,128)(2,1)S(1)} %get-tuple-element.302, f32[16,512,512]{1,2,0:T(8,128)} %get-tuple-element.322, f32[512,512]{0,1:T(8,128)S(1)} %fusion.92), kind=kOutput, calls=%fused_computation.59 | convolution fusion | flops 545259520 | bytes 20971520 | tf_op jit(solution)/shard_map/hts,the->she/dot_general | solution.py:798
  406.4 74.0 %while.30 = (s32[]{:T(128)}, f32[16,66,64]{2,1,0:T(8,128)S(1)}, f32[]{:T(128)}, f32[16,65,64]{2,1,0:T(8,128)}, s32[]{:T(128)}, /*index=5*/s32[]{:T(128)}) while((s32[]{:T(128)}, f32[16,66,64]{2,1,0:T(8,128)S(1)}, f32[]{:T(128)}, f32[16,65,64]{2,1,0:T(8,128)}, s32[]{:T(128)}, /*index=5*/s32[]{:T(128)}) %tuple.121), condition=%wide.region_16.17_spmd.clone.clone.clone, body=%wide.region_15.16_spmd.clone.clone.clone.sunk | while | flops 607235 | bytes 2429055 | solution.py:677
  407.7 4.3 collective-permute-start.1
  417.0 3.8 collective-permute-start.1
  420.8 5.0 collective-permute-done.1
  431.0 6.1 collective-permute-done.1
  438.5 3.8 collective-permute-start.1
  442.3 6.3 collective-permute-done.1
  450.0 4.1 collective-permute-start.1
  454.1 5.4 collective-permute-done.1
  461.0 4.1 collective-permute-start.1
  465.1 4.5 collective-permute-done.1
  471.0 5.1 collective-permute-start.1
  476.1 4.1 collective-permute-done.1
  483.4 4.6 fusion.69
  499.1 5.0 fusion.134
  510.4 4.4 convert_reduce_fusion.5
  531.2 6.1 pad_maximum_fusion.2
  537.2 6.5 copy.157
  543.8 7.2 convolution_convert_fusion
  551.0 10.1 %convert_bitcast_fusion = bf16[4,1024,1024]{2,1,0:T(8,128)(2,1)} fusion(bf16[64,4,8,1024]{3,2,1,0:T(8,128)(2,1)} %bitcast.320, f32[512,1024]{1,0:T(8,128)S(1)} %copy-done.14, f32[1024]{0:T(1024)S(1)} %copy-done.57, f32[1024]{0:T(1024)S(1)} %copy-done.50, f32[512]{0:T(512)S(1)} %copy-done.52, f32[512]{0:T(512)S(1)} %copy-done.42), kind=kOutput, calls=%fused_computation.41 | convolution fusion | flops 4301783040 | bytes 14692352 | tf_op jit(solution)/shard_map/td,tjf->jdf/dot_general | solution.py:770
  561.1 10.5 %pad_maximum_fusion.3 = bf16[8,1024,1024]{2,1,0:T(8,128)(2,1)} fusion(bf16[4,1024,1024]{2,1,0:T(8,128)(2,1)S(1)} %convolution_convert_fusion, bf16[4,1024,1024]{2,1,0:T(8,128)(2,1)} %convert_bitcast_fusion), kind=kLoop, calls=%fused_computation.13 | loop fusion | flops 8388608 | bytes 33554432 | tf_op jit(solution)/shard_map/concatenate | solution.py:852
  572.5 195.7 %shard_map.154 = (f32[3,128,1024]{2,1,0:T(8,128)}, f32[16,128]{1,0:T(8,128)}) custom-call(f32[1,2,2,4,2,128,1024]{6,5,4,3,2,1,0:T(8,128)} %bitcast.269, bf16[2,2,2,4,2,128,1024]{6,5,4,3,2,1,0:T(8,128)(2,1)} %bitcast.270, f32[8,16,128]{2,1,0:T(8,128)} %bitcast.310), custom_call_target="tpu_custom_call" | custom-call | tf_op jit(solution)/shard_map/pallas_call | solution.py:323
  768.3 139.0 %shard_map.155 = (f32[3,2,2,128,1024]{4,3,2,1,0:T(8,128)}, bf16[3,2,2,128,1024]{4,3,2,1,0:T(8,128)(2,1)}) custom-call(f32[3,128,1024]{2,1,0:T(8,128)} %get-tuple-element.155.g_ref, f32[3,2,2,128,1024]{4,3,2,1,0:T(8,128)} %bitcast.289), custom_call_target="tpu_custom_call" | custom-call | tf_op jit(solution)/shard_map/pallas_call | solution.py:570
  907.3 8.3 fusion.26
  915.7 7.4 bitcast_add_fusion
  (291 shorter events, 111.4 us)
Async XLA Ops:
  5.6 138.8 %copy-start.63 = (s32[1,4]{1,0:T(1,128)S(1)}, s32[1,4]{1,0:T(1,128)}, u32[]{:S(2)}) copy-start(s32[1,4]{1,0:T(1,128)} %param.16) | copy-start | bytes 52
  5.6 138.8 %copy-start.64 = (s32[1,4]{1,0:T(1,128)S(1)}, s32[1,4]{1,0:T(1,128)}, u32[]{:S(2)}) copy-start(s32[1,4]{1,0:T(1,128)} %param.17) | copy-start | bytes 52
  144.3 11.9 %copy-start.43 = (f32[1024]{0:T(1024)}, f32[1024]{0:T(1024)S(1)}, u32[]{:S(2)}) copy-start(f32[1024]{0:T(1024)S(1)} %get-tuple-element.311) | copy-start | bytes 12292
  144.3 30.6 %copy-start.30 = (f32[1024]{0:T(1024)}, f32[1024]{0:T(1024)S(1)}, u32[]{:S(2)}) copy-start(f32[1024]{0:T(1024)S(1)} %get-tuple-element.315) | copy-start | bytes 12292
  144.3 30.6 %copy-start.58 = (f32[1024]{0:T(1024)}, f32[1024]{0:T(1024)S(1)}, u32[]{:S(2)}) copy-start(f32[1024]{0:T(1024)S(1)} %get-tuple-element.314) | copy-start | bytes 12292
  144.3 185.0 %copy-start.56 = (f32[1024]{0:T(1024)}, f32[1024]{0:T(1024)S(1)}, u32[]{:S(2)}) copy-start(f32[1024]{0:T(1024)S(1)} %get-tuple-element.308) | copy-start | bytes 12292
  144.4 236.6 %copy-start.49 = (f32[1024]{0:T(1024)}, f32[1024]{0:T(1024)S(1)}, u32[]{:S(2)}) copy-start(f32[1024]{0:T(1024)S(1)} %get-tuple-element.309) | copy-start | bytes 12292
  145.3 29.6 %copy-start.32 = (f32[512]{0:T(512)}, f32[512]{0:T(512)S(1)}, u32[]{:S(2)}) copy-start(f32[512]{0:T(512)S(1)} %broadcast_multiply_fusion.1) | copy-start | bytes 6148
  145.7 29.2 %copy-start.36 = (f32[512]{0:T(512)}, f32[512]{0:T(512)S(1)}, u32[]{:S(2)}) copy-start(f32[512]{0:T(512)S(1)} %fusion.106) | copy-start | bytes 6148
  184.7 15.6 %collective-permute-start = (f32[16,66,64]{1,2,0:T(8,128)}, f32[16,66,64]{1,2,0:T(8,128)S(1)}, u32[]{:S(2)}, u32[]{:S(2)}) collective-permute-start(f32[16,66,64]{1,2,0:T(8,128)} %pad_maximum_fusion.8), channel_id=1, source_target_pairs={{0,4},{4,8},{8,12},{12,16},{16,20},{20,24},{24,28},{1,5},{5,9},{9,... | collective-permute-start | bytes 811016 | tf_op jit(solution)/shard_map/while/body/eval_jaxpr/ppermute | solution.py:619
  201.5 14.7 %collective-permute-start = (f32[16,66,64]{1,2,0:T(8,128)}, f32[16,66,64]{1,2,0:T(8,128)S(1)}, u32[]{:S(2)}, u32[]{:S(2)}) collective-permute-start(f32[16,66,64]{1,2,0:T(8,128)} %pad_maximum_fusion.8), channel_id=1, source_target_pairs={{0,4},{4,8},{8,12},{12,16},{16,20},{20,24},{24,28},{1,5},{5,9},{9,... | collective-permute-start | bytes 811016 | tf_op jit(solution)/shard_map/while/body/eval_jaxpr/ppermute | solution.py:619
  217.5 14.7 %collective-permute-start = (f32[16,66,64]{1,2,0:T(8,128)}, f32[16,66,64]{1,2,0:T(8,128)S(1)}, u32[]{:S(2)}, u32[]{:S(2)}) collective-permute-start(f32[16,66,64]{1,2,0:T(8,128)} %pad_maximum_fusion.8), channel_id=1, source_target_pairs={{0,4},{4,8},{8,12},{12,16},{16,20},{20,24},{24,28},{1,5},{5,9},{9,... | collective-permute-start | bytes 811016 | tf_op jit(solution)/shard_map/while/body/eval_jaxpr/ppermute | solution.py:619
  233.5 13.7 %collective-permute-start = (f32[16,66,64]{1,2,0:T(8,128)}, f32[16,66,64]{1,2,0:T(8,128)S(1)}, u32[]{:S(2)}, u32[]{:S(2)}) collective-permute-start(f32[16,66,64]{1,2,0:T(8,128)} %pad_maximum_fusion.8), channel_id=1, source_target_pairs={{0,4},{4,8},{8,12},{12,16},{16,20},{20,24},{24,28},{1,5},{5,9},{9,... | collective-permute-start | bytes 811016 | tf_op jit(solution)/shard_map/while/body/eval_jaxpr/ppermute | solution.py:619
  248.5 12.8 %collective-permute-start = (f32[16,66,64]{1,2,0:T(8,128)}, f32[16,66,64]{1,2,0:T(8,128)S(1)}, u32[]{:S(2)}, u32[]{:S(2)}) collective-permute-start(f32[16,66,64]{1,2,0:T(8,128)} %pad_maximum_fusion.8), channel_id=1, source_target_pairs={{0,4},{4,8},{8,12},{12,16},{16,20},{20,24},{24,28},{1,5},{5,9},{9,... | collective-permute-start | bytes 811016 | tf_op jit(solution)/shard_map/while/body/eval_jaxpr/ppermute | solution.py:619
  262.6 11.9 %collective-permute-start = (f32[16,66,64]{1,2,0:T(8,128)}, f32[16,66,64]{1,2,0:T(8,128)S(1)}, u32[]{:S(2)}, u32[]{:S(2)}) collective-permute-start(f32[16,66,64]{1,2,0:T(8,128)} %pad_maximum_fusion.8), channel_id=1, source_target_pairs={{0,4},{4,8},{8,12},{12,16},{16,20},{20,24},{24,28},{1,5},{5,9},{9,... | collective-permute-start | bytes 811016 | tf_op jit(solution)/shard_map/while/body/eval_jaxpr/ppermute | solution.py:619
  275.8 10.7 %collective-permute-start = (f32[16,66,64]{1,2,0:T(8,128)}, f32[16,66,64]{1,2,0:T(8,128)S(1)}, u32[]{:S(2)}, u32[]{:S(2)}) collective-permute-start(f32[16,66,64]{1,2,0:T(8,128)} %pad_maximum_fusion.8), channel_id=1, source_target_pairs={{0,4},{4,8},{8,12},{12,16},{16,20},{20,24},{24,28},{1,5},{5,9},{9,... | collective-permute-start | bytes 811016 | tf_op jit(solution)/shard_map/while/body/eval_jaxpr/ppermute | solution.py:619
  288.7 8.1 copy-start.24
  288.8 8.1 copy-start.4
  327.3 53.7 %copy-start.41 = (f32[512]{0:T(512)}, f32[512]{0:T(512)S(1)}, u32[]{:S(2)}) copy-start(f32[512]{0:T(512)S(1)} %broadcast_multiply_fusion) | copy-start | bytes 6148
  327.3 15.9 %slice-start.2 = ((s8[8388608]{0:T(1024)(128)(4,1)}), s8[4194304]{0:T(1024)(128)(4,1)S(1)}, s32[]{:S(2)}) async-start(s8[8388608]{0:T(1024)(128)(4,1)} %bitcast.303), calls=%async_computation.2 | async-start | bytes 8388608
  329.5 51.5 %copy-start.51 = (f32[512]{0:T(512)}, f32[512]{0:T(512)S(1)}, u32[]{:S(2)}) copy-start(f32[512]{0:T(512)S(1)} %fusion.107) | copy-start | bytes 6148
  329.5 13.7 %slice-start.3 = ((s8[8388608]{0:T(1024)(128)(4,1)}), s8[4194304]{0:T(1024)(128)(4,1)S(1)}, s32[]{:S(2)}) async-start(s8[8388608]{0:T(1024)(128)(4,1)} %bitcast.303), calls=%async_computation.3 | async-start | bytes 8388608
  343.2 12.0 %copy-start.16 = (bf16[1,512,1024]{2,1,0:T(8,128)(2,1)S(1)}, bf16[1,512,1024]{2,1,0:T(8,128)(2,1)}, u32[]{:S(2)}) copy-start(bf16[1,512,1024]{2,1,0:T(8,128)(2,1)} %param.15) | copy-start | bytes 3145732
  353.3 18.6 %slice-start = ((s8[8388608]{0:T(1024)(128)(4,1)}), s8[4194304]{0:T(1024)(128)(4,1)S(1)}, s32[]{:S(2)}) async-start(s8[8388608]{0:T(1024)(128)(4,1)} %bitcast.272), calls=%async_computation | async-start | bytes 8388608
  355.3 16.7 %slice-start.1 = ((s8[8388608]{0:T(1024)(128)(4,1)}), s8[4194304]{0:T(1024)(128)(4,1)S(1)}, s32[]{:S(2)}) async-start(s8[8388608]{0:T(1024)(128)(4,1)} %bitcast.272), calls=%async_computation.1 | async-start | bytes 8388608
  387.1 10.9 %copy-start.28 = (f32[512,16]{0,1:T(8,128)}, f32[512,16]{0,1:T(8,128)S(1)}, u32[]{:S(2)}) copy-start(f32[512,16]{0,1:T(8,128)S(1)} %get-tuple-element.301) | copy-start | bytes 98308
  407.7 7.9 collective-permute-start.1
  417.0 8.9 collective-permute-start.1
  427.2 10.0 %collective-permute-start.1 = (bf16[16,66,64]{2,1,0:T(8,128)(2,1)S(1)}, bf16[16,66,64]{2,1,0:T(8,128)(2,1)S(1)}, u32[]{:S(2)}, u32[]{:S(2)}) collective-permute-start(bf16[16,66,64]{2,1,0:T(8,128)(2,1)S(1)} %pad_maximum_fusion.9), channel_id=1, source_target_pairs={{4,0},{8,4},{12,8},{16,12},{20,16},{24,20},{28,24},{5,1},{9,5},{13... | collective-permute-start | bytes 405512 | tf_op jit(solution)/shard_map/while/body/eval_jaxpr/ppermute | solution.py:619
  438.5 10.2 %collective-permute-start.1 = (bf16[16,66,64]{2,1,0:T(8,128)(2,1)S(1)}, bf16[16,66,64]{2,1,0:T(8,128)(2,1)S(1)}, u32[]{:S(2)}, u32[]{:S(2)}) collective-permute-start(bf16[16,66,64]{2,1,0:T(8,128)(2,1)S(1)} %pad_maximum_fusion.9), channel_id=1, source_target_pairs={{4,0},{8,4},{12,8},{16,12},{20,16},{24,20},{28,24},{5,1},{9,5},{13... | collective-permute-start | bytes 405512 | tf_op jit(solution)/shard_map/while/body/eval_jaxpr/ppermute | solution.py:619
  450.0 9.6 %collective-permute-start.1 = (bf16[16,66,64]{2,1,0:T(8,128)(2,1)S(1)}, bf16[16,66,64]{2,1,0:T(8,128)(2,1)S(1)}, u32[]{:S(2)}, u32[]{:S(2)}) collective-permute-start(bf16[16,66,64]{2,1,0:T(8,128)(2,1)S(1)} %pad_maximum_fusion.9), channel_id=1, source_target_pairs={{4,0},{8,4},{12,8},{16,12},{20,16},{24,20},{28,24},{5,1},{9,5},{13... | collective-permute-start | bytes 405512 | tf_op jit(solution)/shard_map/while/body/eval_jaxpr/ppermute | solution.py:619
  461.0 8.7 collective-permute-start.1
  471.0 9.3 %collective-permute-start.1 = (bf16[16,66,64]{2,1,0:T(8,128)(2,1)S(1)}, bf16[16,66,64]{2,1,0:T(8,128)(2,1)S(1)}, u32[]{:S(2)}, u32[]{:S(2)}) collective-permute-start(bf16[16,66,64]{2,1,0:T(8,128)(2,1)S(1)} %pad_maximum_fusion.9), channel_id=1, source_target_pairs={{4,0},{8,4},{12,8},{16,12},{20,16},{24,20},{28,24},{5,1},{9,5},{13... | collective-permute-start | bytes 405512 | tf_op jit(solution)/shard_map/while/body/eval_jaxpr/ppermute | solution.py:619
  543.7 7.2 copy-start.14
  543.7 7.2 copy-start.42
  543.7 7.3 copy-start.50
  543.7 7.3 copy-start.52
  543.7 7.3 copy-start.57
  561.1 10.6 %copy-start.61 = (f32[1024]{0:T(1024)S(1)}, f32[1024]{0:T(1024)}, u32[]{:S(2)}) copy-start(f32[1024]{0:T(1024)} %get-tuple-element.259) | copy-start | bytes 12292
  561.1 10.6 %copy-start.60 = (f32[1024]{0:T(1024)S(1)}, f32[1024]{0:T(1024)}, u32[]{:S(2)}) copy-start(f32[1024]{0:T(1024)} %get-tuple-element.263) | copy-start | bytes 12292
  561.1 10.7 %copy-start.47 = (f32[1024]{0:T(1024)S(1)}, f32[1024]{0:T(1024)}, u32[]{:S(2)}) copy-start(f32[1024]{0:T(1024)} %get-tuple-element.285) | copy-start | bytes 12292
  561.1 10.7 %copy-start.48 = (f32[4096]{0:T(1024)S(1)}, f32[4096]{0:T(1024)}, u32[]{:S(2)}) copy-start(f32[4096]{0:T(1024)} %get-tuple-element.333) | copy-start | bytes 49156
  768.3 139.1 %copy-start.62 = (f32[12]{0:T(128)S(1)}, f32[12]{0:T(128)}, u32[]{:S(2)}) copy-start(f32[12]{0:T(128)} %constant.110.clone) | copy-start | bytes 148
  907.3 8.4 copy-start.15
  915.7 7.5 copy-start.35
  915.7 7.5 copy-start.53
  915.7 7.5 copy-start.54
  915.7 7.5 copy-start.55
  (38 other events, 123.7 us)

commit v2 on v1

--- a/solution.py
+++ b/solution.py
@@ -46,112 +46,6 @@
     straight = [device(lax.rem(z + k, count), x, y, c) for k in range(1, count)]
     across = [device(lax.rem(z + k, count), 1 - x, y, c) for k in range(count)]
     return straight, across
-
-
-def gather_kernel(
-    count, w_ref, small_ref, out_ref, small_out, own_sem, zs, zr, ps, pr, ss, sr
-):
-    batches = w_ref.shape[0]
-    z, x, y, c = places()
-    straight, across = others_along_seq(z, x, y, c, count)
-    pair = [device(z, 1 - x, y, c), device(z, x, 1 - y, c), device(z, x, y, 1 - c)]
-    greet(straight + across + pair[1:])
-    small = []
-    for k, peer in enumerate(straight + across):
-        small.append(remote(small_ref, small_out.at[z * 2 + x], ss.at[k], sr.at[k], peer))
-        small[-1].start()
-    own = [
-        pltpu.make_async_copy(w_ref, out_ref.at[:, :, :, z, x], own_sem.at[0]),
-        pltpu.make_async_copy(small_ref, small_out.at[z * 2 + x], own_sem.at[1]),
-    ]
-    spread = {}
-
-    def send_own(b):
-        for k in range(1, count):
-            spread[b, k] = remote(
-                w_ref.at[b, y, c], out_ref.at[b, y, c, z, x],
-                zs.at[b, k - 1], zr.at[b, k - 1], straight[k - 1],
-            )
-            spread[b, k].start()
-
-    send_own(0)
-    for copy in own:
-        copy.start()
-    first, second, third = [], [], []
-    total = batches * count
-
-    def send(kept, phase, index, source, target, peer):
-        kept.append(remote(source, target, ps.at[phase, index], pr.at[phase, index], peer))
-        kept[-1].start()
-
-    for step in range(total + 3):
-        index = step
-        if index < total:
-            b, k = divmod(index, count)
-            there = lax.rem(z - k + count, count)
-            if k == 0:
-                send(first, 0, index, w_ref.at[b, y, c], out_ref.at[b, y, c, z, x], pair[0])
-            else:
-                spread[b, k].wait_recv()
-                block = out_ref.at[b, y, c, there, x]
-                send(first, 0, index, block, block, pair[(k + b) % 2])
-            if k == min(1, count - 1) and b + 1 < batches:
-                send_own(b + 1)
-        index = step - 1
-        if 0 <= index < total:
-            b, k = divmod(index, count)
-            there = lax.rem(z - k + count, count)
-            first[index].wait_recv()
-            if k == 0:
-                block, peer = out_ref.at[b, y, c, z, 1 - x], pair[1]
-            elif (k + b) % 2 == 0:
-                block, peer = out_ref.at[b, y, c, there], pair[1]
-            else:
-                block, peer = out_ref.at[b, :, c, there, x], pair[0]
-            send(second, 1, index, block, block, peer)
-        index = step - 2
-        if 0 <= index < total:
-            b, k = divmod(index, count)
-            there = lax.rem(z - k + count, count)
-            second[index].wait_recv()
-            block = out_ref.at[b, :, c, z, 1 - x] if k == 0 else out_ref.at[b, :, c, there]
-            send(third, 2, index, block, block, pair[2])
-        index = step - 3
-        if 0 <= index < total:
-            third[index].wait_recv()
-    for copy in list(spread.values()) + first + second + third:
-        copy.wait_send()
-    for copy in small + own:
-        copy.wait()
-
-
-def gather(weights, small, nseq):
-    units, rows, width = weights.shape
-    count = nseq // 2
-    batches = units // 4
-    steps = batches * count
-    out, small_out = pl.pallas_call(
-        functools.partial(gather_kernel, count),
-        out_shape=(
-            jax.ShapeDtypeStruct((batches, 2, 2, count, 2, rows, width), weights.dtype),
-            jax.ShapeDtypeStruct((nseq,) + small.shape, small.dtype),
-        ),
-        in_specs=[VMEM, VMEM],
-        out_specs=[ANY, VMEM],
-        scratch_shapes=[
-            DMA((2,)),
-            DMA((batches, count - 1)),
-            DMA((batches, count - 1)),
-            DMA((3, steps)),
-            DMA((3, steps)),
-            DMA((nseq - 1,)),
-            DMA((nseq - 1,)),
-        ],
-        compiler_params=pltpu.CompilerParams(
-            collective_id=0, has_side_effects=True, vmem_limit_bytes=VMEM_LIMIT
-        ),
-    )(weights.reshape(batches, 2, 2, rows, width), small)
-    return out.reshape(units, nseq * rows, width), small_out
 
 
 CHUNK = 32
@@ -603,6 +497,516 @@
     return whole.reshape(units, rows, width), ortho.reshape(units, rows, width)
 
 
+HALF = 64
+PAIR = 128
+
+
+def matrix(w_ref, batch, index):
+    block = w_ref[batch, index // 2, index % 2]
+    return block.reshape(block.shape[0] * block.shape[1] * block.shape[2], block.shape[3])
+
+
+def norm_rows(values, gain, offset):
+    center = values - jnp.mean(values, axis=-1, keepdims=True)
+    spread = jnp.mean(center * center, axis=-1, keepdims=True)
+    return center * lax.rsqrt(spread + 1e-05) * gain + offset
+
+
+def lanes_of(head):
+    lane = lax.broadcasted_iota(jnp.int32, (1, PAIR), 1)
+    return (lane // HALF) == head
+
+
+def block_diagonal():
+    row = lax.broadcasted_iota(jnp.int32, (PAIR, PAIR), 0)
+    lane = lax.broadcasted_iota(jnp.int32, (PAIR, PAIR), 1)
+    return (row // HALF) == (lane // HALF)
+
+
+def pair_span(index):
+    return pl.ds(pl.multiple_of(index * PAIR, PAIR), PAIR)
+
+
+def band_span(index):
+    return pl.ds(pl.multiple_of(index * BAND, BAND), BAND)
+
+
+def dot_down(left, right):
+    return lax.dot_general(left, right, (((0,), (0,)), ((), ())), preferred_element_type=jnp.float32)
+
+
+def pack_message(left_ref, right_ref, scale_ref, row_ref, message):
+    diagonal = block_diagonal()
+    for j in range(4):
+        parts = []
+        for p in (2 * j, 2 * j + 1):
+            lanes = slice(p * PAIR, (p + 1) * PAIR)
+            scale = scale_ref[...]
+            left = (left_ref[:, lanes].astype(jnp.float32) * scale).astype(jnp.bfloat16)
+            parts.append(dot_down(left, right_ref[:, lanes]))
+            if row_ref is None:
+                total = jnp.sum(left.astype(jnp.float32), axis=0, keepdims=True)
+            else:
+                total = jnp.sum(left.astype(jnp.float32) * row_ref[:, lanes], axis=0, keepdims=True)
+            for half in range(2):
+                message[half, 256 + p : 257 + p, :] = total
+        block = jnp.where(diagonal, parts[0], pltpu.roll(parts[1], HALF, 1))
+        message[j // 2, (j % 2) * PAIR : (j % 2 + 1) * PAIR, :] = block
+
+
+def unpack_message(message, p):
+    diagonal = block_diagonal()
+    j = p // 2
+    block = message[j // 2, (j % 2) * PAIR : (j % 2 + 1) * PAIR, :]
+    if p % 2:
+        block = pltpu.roll(block, HALF, 1)
+    block = jnp.where(diagonal, block, 0.0)
+    row = message[0, 256 + p : 257 + p, :]
+    column = jnp.transpose(jnp.broadcast_to(row, (PAIR, PAIR)))
+    return block, jnp.where(diagonal, column, 0.0)
+
+
+class Relay:
+    def __init__(self, count, coef, own, across, part, spread, total, result, sems, places_):
+        self.count, self.coef, self.own, self.across = count, coef, own, across
+        self.part, self.spread, self.total, self.result = part, spread, total, result
+        self.send, self.recv = sems
+        self.z, self.x, self.y, self.c = places_
+        self.pair = device(self.z, 1 - self.x, self.y, self.c)
+
+    def swap(self):
+        self.first = remote(self.own, self.across, self.send.at[0], self.recv.at[0], self.pair)
+        self.first.start()
+
+    def spread_out(self):
+        self.first.wait_recv()
+        self.part[...] = self.coef[0] * self.own[self.x] + self.coef[1] * self.across[self.x]
+        self.copies = []
+        for k in range(1, self.count):
+            peer = device(lax.rem(self.z + k, self.count), self.x, self.y, self.c)
+            copy = remote(self.part, self.spread.at[k - 1], self.send.at[k], self.recv.at[k], peer)
+            copy.start()
+            self.copies.append(copy)
+
+    def join(self):
+        total = jnp.zeros_like(self.part)
+        for k, copy in enumerate(self.copies):
+            copy.wait_recv()
+            total = total + self.coef[4 + k] * self.spread[k]
+        self.total[self.x] = total
+        half = self.total.at[self.x]
+        self.last = remote(half, half, self.send.at[self.count], self.recv.at[self.count], self.pair)
+        self.last.start()
+
+    def finish(self):
+        self.last.wait_recv()
+        for half in range(2):
+            self.result[half] = self.coef[2] * self.total[half] + self.coef[3] * self.across[half]
+
+    def wait_sends(self):
+        for copy in [self.first, self.last] + self.copies:
+            copy.wait_send()
+
+
+def head_scores(q_ref, k_ref, keep_ref, lanes, head, band):
+    rows = slice(band * BAND, (band + 1) * BAND)
+    upto = slice(0, (band + 1) * BAND)
+    query = jnp.where(lanes_of(head), q_ref[rows, lanes], 0)
+    return dot(query, k_ref[upto, lanes], True) * keep_ref[rows, upto]
+
+
+def attend_pair(p, q_ref, k_ref, v_ref, keep_ref, num_ref, den_ref):
+    lanes = pair_span(p)
+    group = q_ref.shape[0]
+    value = v_ref[:, lanes]
+    first = lanes_of(0)
+    for band in range(group // BAND):
+        rows = slice(band * BAND, (band + 1) * BAND)
+        sums, totals = [], []
+        for head in range(2):
+            scores = head_scores(q_ref, k_ref, keep_ref, lanes, head, band)
+            totals.append(jnp.sum(scores, axis=1, keepdims=True))
+            sums.append(dot(scores.astype(jnp.bfloat16), value[: (band + 1) * BAND]))
+        num_ref[rows, lanes] = jnp.where(first, sums[0], sums[1])
+        den_ref[rows, lanes] = jnp.where(first, totals[0], totals[1])
+
+
+def image_ends(lengths_ref, order_ref):
+    images = lengths_ref.shape[1]
+    ends, running = [], jnp.int32(0)
+    for j in range(images):
+        for i in range(images):
+            running = running + jnp.where(order_ref[0, j] == i, lengths_ref[0, i], 0)
+        ends.append(running)
+    return ends
+
+
+def segment_at(ends, positions):
+    found = jnp.zeros_like(positions)
+    for end in ends:
+        found = found + jnp.where(positions >= end, 1, 0)
+    return found
+
+
+def same(left, right):
+    return jnp.where(left == right, 1.0, 0.0)
+
+
+def fill_masks(ends, start, group, keep_ref, flags_ref):
+    for band in range(group // BAND):
+        rows = slice(band * BAND, (band + 1) * BAND)
+        down = lax.broadcasted_iota(jnp.int32, (BAND, group), 0) + band * BAND
+        along = lax.broadcasted_iota(jnp.int32, (BAND, group), 1)
+        mine = segment_at(ends, down + start)
+        theirs = segment_at(ends, along + start)
+        keep_ref[rows, :] = jnp.where(along <= down, same(mine, theirs), 0.0)
+        narrow = mine[:, :PAIR]
+        flags_ref[0, rows, :] = same(narrow, segment_at(ends, start - 1))
+        flags_ref[1, rows, :] = same(narrow, segment_at(ends, start + group - 1))
+
+
+def pass_at(ends, block, group):
+    return same(segment_at(ends, block * group + group - 1), segment_at(ends, block * group - 1))
+
+
+def forward_factors(ends, group, count, z, x):
+    both = [pass_at(ends, 2 * z, group), pass_at(ends, 2 * z + 1, group)]
+    near = [jnp.where(x == 0, both[1], 1.0), jnp.where(x == 0, 1.0, both[1])]
+    near += [jnp.where(x == 0, 1.0, both[0]), jnp.where(x == 0, 0.0, 1.0)]
+    running, far = jnp.float32(1.0), []
+    for k in range(1, count):
+        far.append(jnp.where(z - k >= 0, running, 0.0))
+        there = jnp.maximum(z - k, 0)
+        running = running * pass_at(ends, 2 * there, group) * pass_at(ends, 2 * there + 1, group)
+    return near + far
+
+
+def backward_factors(ends, group, count, z, x):
+    both = [pass_at(ends, 2 * z, group), pass_at(ends, 2 * z + 1, group)]
+    near = [jnp.where(x == 0, 1.0, both[0]), jnp.where(x == 0, both[0], 1.0)]
+    near += [jnp.where(x == 0, both[1], 1.0), jnp.where(x == 0, 1.0, 0.0)]
+    running, ahead = jnp.float32(1.0), []
+    for k in range(1, count):
+        ahead.append(jnp.where(z + k < count, running, 0.0))
+        there = jnp.minimum(z + k, count - 1)
+        running = running * pass_at(ends, 2 * there, group) * pass_at(ends, 2 * there + 1, group)
+    return near + ahead[::-1]
+
+
+def forward_kernel(
+    count, aligned, x_ref, w_ref, small_ref, lengths_ref, order_ref,
+    w_out, out_ref, rows_ref, low_ref, pre_ref, ratio_ref, left_ref, resid_ref, up_ref, act_ref, state_ref,
+    w_all, stage, small_in, keep, flags, h1, q, k, v, num, den, o, resid, h2, act, turned, act_turned, message, across, part, spread, total_ref, state,
+    load_sem, out_sem, zs, zr, ps, pr, ss, sr, rs, rr,
+):
+    z, x, y, c = places()
+    straight, far = others_along_seq(z, x, y, c, count)
+    pair = [device(z, 1 - x, y, c), device(z, x, 1 - y, c), device(z, x, y, 1 - c)]
+    batches = w_ref.shape[0]
+    rows, width = w_ref.shape[3:]
+    group = x_ref.shape[0]
+    bands = group // BAND
+    loads = []
+    for b in range(batches):
+        for i in range(4):
+            copy = pltpu.make_async_copy(
+                w_ref.at[b, i // 2, i % 2],
+                stage.at[b, pl.ds(i * rows, rows)],
+                load_sem.at[b, i],
+            )
+            copy.start()
+            loads.append(copy)
+    greet(straight + far + pair[1:])
+    small = []
+    if aligned:
+        for j, peer in enumerate(straight + far):
+            small.append(remote(small_ref, small_in.at[z * 2 + x], ss.at[j], sr.at[j], peer))
+            small[-1].start()
+        small_in[z * 2 + x] = small_ref[...]
+    spread_w = {}
+
+    def cast_own(b):
+        for i in range(4):
+            loads[b * 4 + i].wait()
+            for j in range(rows // CHUNK):
+                span = slice(j * CHUNK, (j + 1) * CHUNK)
+                at = slice(i * rows + j * CHUNK, i * rows + (j + 1) * CHUNK)
+                w_all[b, i // 2, i % 2, z, x, span, :] = stage[b, at, :].astype(jnp.bfloat16)
+
+    def send_own(b):
+        for j in range(1, count):
+            block = w_all.at[b, y, c, z, x]
+            spread_w[b, j] = remote(block, block, zs.at[b, j - 1], zr.at[b, j - 1], straight[j - 1])
+            spread_w[b, j].start()
+
+    first, second, third, outs, waited = [], [], [], [], []
+    plan = [(b, 0) for b in range(batches)]
+    plan += [(b, j) for b in range(batches) for j in range(1, count)]
+    total = len(plan)
+
+    def send(kept, phase, index, block, peer):
+        kept.append(remote(block, block, ps.at[phase, index], pr.at[phase, index], peer))
+        kept[-1].start()
+
+    def put_out(source, target):
+        copy = pltpu.make_async_copy(source, target, out_sem.at[len(outs)])
+        copy.start()
+        outs.append(copy)
+        return copy
+
+    def tick(step):
+        index = step
+        if index < total:
+            b, j = plan[index]
+            there = lax.rem(z - j + count, count)
+            if j:
+                spread_w[b, j].wait_recv()
+            send(first, 0, index, w_all.at[b, y, c, there, x], pair[(j + b) % 2 if j else 0])
+            if j == min(1, count - 1) and b + 1 < batches:
+                send_own(b + 1)
+        index = step - 1
+        if 0 <= index < total:
+            b, j = plan[index]
+            there = lax.rem(z - j + count, count)
+            first[index].wait_recv()
+            if j == 0:
+                send(second, 1, index, w_all.at[b, y, c, z, 1 - x], pair[1])
+            elif (j + b) % 2 == 0:
+                send(second, 1, index, w_all.at[b, y, c, there], pair[1])
+            else:
+                send(second, 1, index, w_all.at[b, :, c, there, x], pair[0])
+        index = step - 2
+        if 0 <= index < total:
+            b, j = plan[index]
+            there = lax.rem(z - j + count, count)
+            second[index].wait_recv()
+            block = w_all.at[b, :, c, z, 1 - x] if j == 0 else w_all.at[b, :, c, there]
+            send(third, 2, index, block, pair[2])
+        index = step - 3
+        if 0 <= index < total:
+            b, j = plan[index]
+            there = lax.rem(z - j + count, count)
+            third[index].wait_recv()
+            put_out(w_all.at[b, :, :, there], w_out.at[b, :, :, there])
+
+    cast_own(0)
+    send_own(0)
+    tick(0)
+    for b in range(1, batches):
+        cast_own(b)
+        tick(b)
+    if aligned:
+        for copy in small:
+            copy.wait_recv()
+        share_rows = 13 * 1024 // 128 // (count * 2)
+        for j in range(13 * 8):
+            rows_ref[j // 8 : j // 8 + 1, (j % 8) * 128 : (j % 8 + 1) * 128] = small_in[
+                j // share_rows, j % share_rows : j % share_rows + 1, :
+            ]
+    else:
+        rows_ref[0:13, :] = small_ref[...]
+
+    def vector(index):
+        return rows_ref[index : index + 1, :]
+
+    def norm_one(i, carry):
+        span = band_span(i)
+        value = norm_rows(x_ref[span, :].astype(jnp.float32), vector(0), vector(1))
+        h1[span, :] = value.astype(jnp.bfloat16)
+        turned[0, :, span] = jnp.transpose(value).astype(jnp.bfloat16)
+        return carry
+
+    lax.fori_loop(0, bands, norm_one, 0)
+    ends = image_ends(lengths_ref, order_ref)
+    fill_masks(ends, (z * 2 + x) * group, group, keep, flags)
+    factors = forward_factors(ends, group, count, z, x)
+    ready = batches + count - 1 + 3
+    for step in range(batches, ready):
+        tick(step)
+
+    def project(i, carry):
+        span = band_span(i)
+        left = h1[span, :]
+        for index, low in ((0, q), (1, k)):
+            pre = dot(left, matrix(w_all, 0, index)) + vector(4 + index)
+            stage[index, span, :] = pre
+            low[span, :] = jnp.where(pre > 0, pre + 1.0, jnp.exp(jnp.minimum(pre, 0.0))).astype(jnp.bfloat16)
+        v[span, :] = (dot(left, matrix(w_all, 0, 2)) + vector(6)).astype(jnp.bfloat16)
+        return carry
+
+    lax.fori_loop(0, bands, project, 0)
+    pack_message(k, v, flags.at[1], None, message)
+    relay = Relay(count, factors, message, across, part, spread, total_ref, state, (rs, rr), (z, x, y, c))
+    relay.swap()
+    stored = [put_out(stage.at[0], pre_ref.at[0]), put_out(stage.at[1], pre_ref.at[1]), None]
+    for index, low in enumerate((q, k, v)):
+        put_out(low, low_ref.at[index])
+
+    def attend(p, carry):
+        attend_pair(p, q, k, v, keep, num, den)
+        return carry
+
+    pairs = width // PAIR
+    step = ready
+    lax.fori_loop(0, pairs // 4, attend, 0)
+    tick(step)
+    relay.spread_out()
+    lax.fori_loop(pairs // 4, pairs // 2, attend, 0)
+    tick(step + 1)
+    lax.fori_loop(pairs // 2, pairs, attend, 0)
+    relay.join()
+    tick(step + 2)
+    relay.finish()
+    put_out(state, state_ref)
+    for p in range(pairs):
+        block, column = unpack_message(state, p)
+        high, low = split_two(jnp.concatenate([block, column], axis=1))
+        lanes = slice(p * PAIR, (p + 1) * PAIR)
+        for i in range(bands):
+            span = slice(i * BAND, (i + 1) * BAND)
+            query = q[span, lanes]
+            both = dot(query, high) + dot(query, low)
+            flag = flags[0, span, :]
+            top = num[span, lanes] + flag * both[:, :PAIR]
+            bottom = den[span, lanes] + flag * both[:, PAIR:]
+            num[span, lanes] = top
+            den[span, lanes] = bottom
+            o[span, lanes] = (top / bottom).astype(jnp.bfloat16)
+    put_out(num, ratio_ref.at[0])
+    put_out(den, ratio_ref.at[1])
+
+    def close(i, carry):
+        span = band_span(i)
+        value = x_ref[span, :].astype(jnp.float32) + dot(o[span, :], matrix(w_all, 0, 3)) + vector(7)
+        resid[span, :] = value
+        hidden = norm_rows(value, vector(2), vector(3))
+        h2[span, :] = hidden.astype(jnp.bfloat16)
+        turned[2, :, span] = jnp.transpose(hidden).astype(jnp.bfloat16)
+        turned[1, :, span] = jnp.transpose(o[span, :].astype(jnp.float32)).astype(jnp.bfloat16)
+        return carry
+
+    lax.fori_loop(0, bands, close, 0)
+    put_out(turned, left_ref)
+    put_out(resid, resid_ref)
+    step = step + 3
+    ready = batches + 2 * (count - 1) + 3
+    while step < ready:
+        tick(step)
+        step += 1
+    blocks = act.shape[0]
+    turned_out = []
+    for j in range(blocks):
+        if j > 1:
+            turned_out[j - 2].wait()
+            waited.append(turned_out[j - 2])
+        if stored[j % 3] is not None:
+            stored[j % 3].wait()
+            waited.append(stored[j % 3])
+
+        def expand(i, carry):
+            span = band_span(i)
+            pre = dot(h2[span, :], matrix(w_all, 1, j)) + vector(9 + j)
+            stage[j % 3, span, :] = pre
+            value = jax.nn.gelu(pre)
+            act[j, span, :] = value.astype(jnp.bfloat16)
+            act_turned[j % 2, :, span] = jnp.transpose(value).astype(jnp.bfloat16)
+            return carry
+
+        lax.fori_loop(0, bands, expand, 0)
+        stored[j % 3] = put_out(stage.at[j % 3], up_ref.at[j])
+        turned_out.append(put_out(act_turned.at[j % 2], act_ref.at[j]))
+        if step < total + 3:
+            tick(step)
+            step += 1
+    while step < total + 3:
+        tick(step)
+        step += 1
+
+    def project_down(i, carry):
+        span = band_span(i)
+        value = resid[span, :] + vector(8)
+        for j in range(blocks):
+            value += dot(act[j, span, :], matrix(w_all, 2, j))
+        out_ref[span, :] = value.astype(jnp.bfloat16)
+        return carry
+
+    lax.fori_loop(0, bands, project_down, 0)
+    for copy in outs:
+        if not any(copy is other for other in waited):
+            copy.wait()
+    for copy in list(spread_w.values()) + first + second + third + small:
+        copy.wait_send()
+    relay.wait_sends()
+
+
+def forward(x, weights, small, lengths, order, nseq, aligned):
+    group, width = x.shape
+    units, rows, _ = weights.shape
+    count, batches = nseq // 2, units // 4
+    steps = batches * count
+    f32, bf16 = jnp.float32, jnp.bfloat16
+    V, S = pltpu.VMEM, jax.ShapeDtypeStruct
+    blocks = 4
+    smem = pl.BlockSpec(memory_space=pltpu.SMEM)
+    message = (2, 264, PAIR)
+    return pl.pallas_call(
+        functools.partial(forward_kernel, count, aligned),
+        out_shape=(
+            S((batches, 2, 2, count, 2, rows, width), bf16),
+            S((group, width), bf16),
+            S((16, width), f32),
+            S((3, group, width), bf16),
+            S((2, group, width), f32),
+            S((2, group, width), f32),
+            S((3, width, group), bf16),
+            S((group, width), f32),
+            S((blocks, group, width), f32),
+            S((blocks, width, group), bf16),
+            S(message, f32),
+        ),
+        in_specs=[VMEM, ANY, VMEM, smem, smem],
+        out_specs=[ANY, VMEM, VMEM] + [ANY] * 8,
+        scratch_shapes=[
+            V((batches, 2, 2, count, 2, rows, width), bf16),
+            V((3, group, width), f32),
+            V(((nseq,) if aligned else ()) + small.shape, f32),
+            V((group, group), f32),
+            V((2, group, PAIR), f32),
+            V((group, width), bf16),
+            V((group, width), bf16),
+            V((group, width), bf16),
+            V((group, width), bf16),
+            V((group, width), f32),
+            V((group, width), f32),
+            V((group, width), bf16),
+            V((group, width), f32),
+            V((group, width), bf16),
+            V((blocks, group, width), bf16),
+            V((3, width, group), bf16),
+            V((2, width, group), bf16),
+            V(message, f32),
+            V(message, f32),
+            V(message[1:], f32),
+            V((count - 1,) + message[1:], f32),
+            V(message, f32),
+            V(message, f32),
+            DMA((batches, 4)),
+            DMA((steps + 20,)),
+            DMA((batches, count - 1)),
+            DMA((batches, count - 1)),
+            DMA((3, steps)),
+            DMA((3, steps)),
+            DMA((nseq - 1,)),
+            DMA((nseq - 1,)),
+            DMA((count + 1,)),
+            DMA((count + 1,)),
+        ],
+        compiler_params=pltpu.CompilerParams(
+            collective_id=0, has_side_effects=True, vmem_limit_bytes=VMEM_LIMIT
+        ),
+    )(x, weights.reshape(batches, 2, 2, rows, width), small, lengths, order)
+
+
 D = 1024
 HEADS = 16
 HEAD_DIM = 64
@@ -695,20 +1099,21 @@
     units = weights.shape[0]
     nseq = lax.axis_size("seq")
     share = small_params.shape[0]
-    gathered, small_low = gather(
-        weights.astype(jnp.bfloat16), padded(small_params.astype(jnp.bfloat16)), nseq
-    )
-    small_low = small_low.reshape(nseq, 2048)[:, :share].reshape(nseq * share)
-    small = small_low.astype(jnp.float32)
-    gain_one, bias_one, gain_two, bias_two, bias_q, bias_k, bias_v, bias_o, bias_down, bias_up = (
-        split_small(small, width)
-    )
-    w_query = gathered[0]
-    w_key = gathered[1]
-    w_value = gathered[2]
-    w_out = gathered[3]
+    rounded = lax.reduce_precision(small_params, 8, 7)
+    aligned = share % 128 == 0
+    if aligned:
+        shared = padded(rounded)
+    else:
+        shared = lax.all_gather(rounded, "seq", axis=0, tiled=True).reshape(-1, width)
+    (gathered, block_out, rows, low, pre, ratio, left, resid, up, act, state) = forward(
+        tokens[0], weights, shared, lengths, order, nseq, aligned
+    )
+    block_out = block_out[None]
+    gathered = gathered.reshape(units, width, width)
+    w_query, w_key, w_value, w_out = gathered[0], gathered[1], gathered[2], gathered[3]
     w_up = gathered[4 : 4 + blocks]
     w_down = gathered[4 + blocks :].reshape(blocks * width, width)
+    gain_one, bias_one, gain_two, bias_two = rows[0], rows[1], rows[2], rows[3]
     start = lax.axis_index("seq") * group
     positions = start + jnp.arange(group, dtype=jnp.int32)
     segment = segment_of(lengths[0], order[0], positions)
@@ -721,45 +1126,24 @@
     finals = (segment == segment[-1]).astype(jnp.float32)
     passes = (segment[-1] == before).astype(jnp.float32)
     inputs = tokens[0].astype(jnp.float32)
-    normed = layer_norm(inputs, gain_one, bias_one).astype(jnp.bfloat16)
-    query_pre = jnp.dot(normed, w_query, preferred_element_type=jnp.float32) + bias_q
-    key_pre = jnp.dot(normed, w_key, preferred_element_type=jnp.float32) + bias_k
-    value_pre = jnp.dot(normed, w_value, preferred_element_type=jnp.float32) + bias_v
-    query_low = feature(query_pre).astype(jnp.bfloat16).reshape(group, heads, depth)
-    key_low = feature(key_pre).astype(jnp.bfloat16).reshape(group, heads, depth)
-    value_low = value_pre.astype(jnp.bfloat16).reshape(group, heads, depth)
-    scores = (
+    normed = left[0].T
+    query_low, key_low, value_low = [low[i].reshape(group, heads, depth) for i in range(3)]
+    query_pre, key_pre = pre[0], pre[1]
+    numer = ratio[0].reshape(group, heads, depth)
+    denom = ratio[1].reshape(group, heads, depth)[:, :, 0]
+    attended, hidden = left[1].T, left[2].T
+    scores_low = (
         jnp.einsum("thd,shd->hts", query_low, key_low, preferred_element_type=jnp.float32)
         * keep[None]
-    )
-    denom = jnp.sum(scores, axis=2).T
-    scores_low = scores.astype(jnp.bfloat16)
-    numer = jnp.einsum("hts,she->the", scores_low, value_low, preferred_element_type=jnp.float32)
-    keys_last = key_low * finals.astype(jnp.bfloat16)[:, None, None]
-    own_state = jnp.einsum("shd,she->hde", keys_last, value_low, preferred_element_type=jnp.float32)
-    own_total = jnp.sum(keys_last.astype(jnp.float32), axis=0)
-    arriving = relay_forward(pack_state(own_state, own_total, passes))
-    state_in = arriving[:, :depth, :]
-    total_in = arriving[:, depth, :]
+    ).astype(jnp.bfloat16)
     query_wide = query_low.astype(jnp.float32)
-    numer = numer + incoming[:, None, None] * jnp.einsum(
-        "thd,hde->the", query_wide, state_in, precision=highest
-    )
-    denom = denom + incoming[:, None] * jnp.einsum(
-        "thd,hd->th", query_wide, total_in, precision=highest
-    )
-    attended = (numer / denom[:, :, None]).reshape(group, width).astype(jnp.bfloat16)
-    resid = inputs + jnp.dot(attended, w_out, preferred_element_type=jnp.float32) + bias_o
-    hidden = layer_norm(resid, gain_two, bias_two).astype(jnp.bfloat16)
-    up_pre = (
-        jnp.einsum("td,jdf->tjf", hidden, w_up, preferred_element_type=jnp.float32).reshape(
-            group, blocks * width
-        )
-        + bias_up
-    )
-    active = jax.nn.gelu(up_pre).astype(jnp.bfloat16)
-    output = resid + jnp.dot(active, w_down, preferred_element_type=jnp.float32) + bias_down
-    block_out = output.astype(jnp.bfloat16)[None]
+    quads = state[:, :256].reshape(4, 128, 128)
+    state_in = jnp.stack(
+        [quads[:, :64, :64], quads[:, 64:, 64:], quads[:, :64, 64:], quads[:, 64:, :64]], axis=1
+    ).reshape(heads, depth, depth)
+    total_in = state[0, 256:].reshape(heads, depth)
+    up_pre = up.transpose(1, 0, 2).reshape(group, blocks * width)
+    active = act.transpose(2, 0, 1).reshape(group, blocks * width)
     grad_out = cotangent[0]
     grad_down = jnp.einsum("tf,td->fd", active, grad_out, preferred_element_type=jnp.float32)
     grad_bias_down = jnp.sum(grad_out.astype(jnp.float32), axis=0)

time: 935 us -> 749 us (0.80)
  waiting for transfers between devices: 120 us -> 26.3 us
  matrix products: 161 us -> 87 us
  other arithmetic: 74.1 us -> 53.2 us
    ppermute x14 -> x7, waiting for transfers between devices: 120 us -> 26.3 us  [passed_along(): return lax.ppermute(array, axis, pairs)]
    dot_general x11 -> x0, matrix products: 66.4 us -> none  [the longest x1 13.7 us: local(): jnp.einsum('td,jdf->tjf', hidden, w_up, preferred_element_type=jnp.float32)]
    slice x3 -> x13, local copies, waits for them, and re-layouts: 1.92 us -> 29.9 us  [the longest x3 13.8 us: local(): query_pre, key_pre = (pre[0], pre[1])]
    dot_general x2 -> x0, local copies, waits for them, and re-layouts: 17.9 us -> none  [the longest x1 11.4 us: local(): jnp.einsum('td,jdf->tjf', hidden, w_up, preferred_element_type=jnp.float32)]
    ppermute x14 -> x7, starting transfers between devices: 38.1 us -> 35.2 us  [passed_along(): return lax.ppermute(array, axis, pairs)]
  transfers between devices with their start and end apart: 14 -> 7, of which waited for: 14 -> 7; matrix products, arithmetic and copies ran while one was open for 0% -> 0% of each run, Pallas kernels for 0% -> 0%
where the time goes in v2:
time: 749 us; the launch traced here: 739 us
  Pallas kernels  472 us (63%)
  matrix products  87 us (12%)
  local copies, waits for them, and re-layouts  62.2 us (8%)
  other arithmetic  53.2 us (7%)
  starting transfers between devices  35.2 us (5%)
  waiting for transfers between devices  26.3 us (4%)
    pallas_call x1, Pallas kernels, reduce_rows(): pl.pallas_call(functools.partial(reduce_kernel, count), out_shape=(jax.Sh...  189 us
    pallas_call x1, Pallas kernels, forward(): pl.pallas_call(functools.partial(forward_kernel, count, aligned), out_sha...  144 us
    pallas_call x1, Pallas kernels, muon(): pl.pallas_call(functools.partial(muon_kernel, count), out_shape=(jax.Shap...  139 us
    ppermute x7, starting transfers between devices, passed_along(): return lax.ppermute(array, axis, pairs)  35.2 us
    ppermute x7, waiting for transfers between devices, passed_along(): return lax.ppermute(array, axis, pairs)  26.3 us
  transfers between devices with their start and end apart: 7, of which 7 were waited for; matrix products, arithmetic and copies ran while one was open for 0% of the time, Pallas kernels for 0%

profile of v2, /device:TPU:31, one launch (start us, length us, event | category | flops | bytes accessed | tf_op | source)
XLA Modules:
  0.0 739.3 jit_solution(4609195800169877517)
XLA Ops:
  1.9 144.0 %shard_map.153 = (bf16[3,2,2,4,2,128,1024]{6,5,4,3,2,1,0:T(8,128)(2,1)}, bf16[512,1024]{1,0:T(8,128)(2,1)}, f32[16,1024]{1,0:T(8,128)}, bf16[3,512,1024]{2,1,0:T...) custom-call(bf16[512,1024]{1,0:T(8,128)(2,1)} %bitcast.245, ...), custom_call_target="tpu_custom_call" | custom-call | tf_op jit(solution)/shard_map/pallas_call | solution.py:952
  149.0 8.7 %copy.52 = f32[512,4,1024]{0,2,1:T(8,128)} copy(f32[512,4,1024]{2,0,1:T(8,128)} %bitcast.259) | data formatting | bytes 16777216 | tf_op jit(solution)/shard_map/transpose | solution.py:1145
  157.7 10.7 %fusion.82 = (bf16[1,2,2,4,2,128,1024]{6,5,4,3,2,1,0:T(8,128)(2,1)S(1)}, bf16[1,2,2,4,2,128,1024]{6,5,4,3,2,1,0:T(8,128)(2,1)}) fusion(bf16[3,2,2,4,2,128,1024]{6,5,4,3,2,1,0:T(8,128)(2,1)} %get-tuple-element.92), kind=kLoop, calls=%fused_computation.169 | loop fusion | bytes 33554432 | tf_op jit(solution)/shard_map/slice | solution.py:1114
  169.2 14.2 %convert_reduce_fusion = (f32[4096]{0:T(1024)}, bf16[512,4096]{0,1:T(8,128)(2,1)}) fusion(f32[512,4,1024]{0,2,1:T(8,128)S(1)} %copy-done.12, bf16[4096,1024]{1,0:T(8,128)(2,1)} %bitcast.261, bf16[1,512,1024]{2,1,0:T(8,128)(2,1)S(1)} %copy-done.14), kind=kOutput, calls=%fused_computation.26 | convolution fusion | flops 4341100544 | bytes 22036480 | tf_op jit(solution)/shard_map/td,fd->tf/dot_general | solution.py:1150
  183.4 8.1 %fusion.36 = (f32[1024]{0:T(1024)}, f32[512]{0:T(512)S(1)}, f32[1024]{0:T(1024)}, f32[512,1024,1]{1,0,2:T(8,128)S(1)}) fusion(f32[512,1024]{1,0:T(8,128)S(1)} %copy-done.1, f32[512]{0:T(512)S(1)} %fusion.70, f32[512]{0:T(512)S(1)} %broadcast_multiply_fusion.1, f32[1024]{0:T(1024)S(1)} %bitcast.276, bf16[512,4,1024]{0,2,1:T(8,128)(2,1)} %bitcast.282, ...), kind=kOutput, calls=%fused_computation.72 | convolution fusion | flops 4299159040 | bytes 16795648 | tf_op jit(solution)/shard_map/tjf,jdf->td/dot_general | solution.py:1158
  199.6 2.3 copy.62
  203.2 7.5 %fusion.83 = (f32[1,512,1024]{2,1,0:T(8,128)}, f32[1,512,1024]{2,1,0:T(8,128)}, f32[1,512,1024]{2,1,0:T(8,128)}, f32[1,512,1024]{2,1,0:T(8,128)}) fusion(f32[2,512,1024]{2,1,0:T(8,128)} %get-tuple-element.96, f32[2,512,1024]{2,1,0:T(8,128)} %get-tuple-element.98), kind=kLoop, calls=%fused_computation.170 | loop fusion | bytes 16777216 | tf_op jit(solution)/shard_map/slice | solution.py:1131
  210.7 2.9 copy.58
  217.1 2.6 multiply_reduce_fusion
  219.7 2.9 copy.56
  224.4 3.2 fusion.37
  231.6 70.5 %while.15 = (s32[]{:T(128)}, f32[16,66,64]{2,1,0:T(8,128)S(1)}, f32[]{:T(128)}, f32[16,65,64]{2,1,0:T(8,128)S(1)}, s32[]{:T(128)}, /*index=5*/s32[]{:T(128)}) while((s32[]{:T(128)}, f32[16,66,64]{2,1,0:T(8,128)S(1)}, f32[]{:T(128)}, f32[16,65,64]{2,1,0:T(8,128)S(1)}, s32[]{:T(128)}, ...), condition=%wide.region_10.11_spmd.clone.clone.clone, body=%wide.region_9.10_spmd.clone.clone.clone.sunk | while | flops 607235 | bytes 2429055 | solution.py:1081
  231.9 2.9 collective-permute-start
  234.7 5.7 collective-permute-done
  241.7 4.9 collective-permute-start
  246.6 4.8 collective-permute-done
  252.7 4.9 collective-permute-start
  257.7 3.9 collective-permute-done
  262.8 5.1 collective-permute-start
  267.9 3.1 collective-permute-done
  272.3 5.9 collective-permute-start
  278.2 2.9 collective-permute-done
  282.4 5.8 collective-permute-start
  288.2 2.9 collective-permute-done
  292.4 5.5 collective-permute-start
  298.0 2.9 collective-permute-done
  302.1 3.6 fusion.64
  306.9 8.3 %convert_reduce_fusion.4 = (f32[16,64]{1,0:T(8,128)}, bf16[16,64,512]{2,1,0:T(8,128)(2,1)}) fusion(f32[16,64,512]{2,1,0:T(8,128)} %fusion.64, f32[512]{0:T(512)S(1)} %get-tuple-element.214, bf16[512,16,64]{0,2,1:T(8,128)(2,1)} %copy-done.9, bf16[512,16,64]{0,2,1:T(8,128)(2,1)} %bitcast.251, bf16[512,16,64]{0,2,1:T(8,128)(2,1)} %bitcast.257, ...), kind=kOutput, calls=%fused_computation.74 | convolution fusion | flops 1084750848 | bytes 7346176 | tf_op jit(solution)/shard_map/hts,the->she/dot_general | solution.py:1182
  315.2 4.6 fusion.26
  319.7 3.0 copy.61
  322.7 2.3 copy.57
  325.0 4.5 multiply_convert_fusion.1
  331.1 2.3 copy-done
  333.8 2.6 convert_reduce_fusion.5
  336.4 4.6 fusion.27
  341.0 3.4 copy.54
  345.6 6.1 fusion.87
  351.8 2.0 convert_reduce_fusion.6
  354.4 3.6 fusion.76
  359.2 2.1 convert_reduce_fusion.2
  367.3 6.6 pad_maximum_fusion.1
  374.0 4.9 convolution_convert_fusion
  378.9 7.0 convert_bitcast_fusion
  386.0 6.6 pad_maximum_fusion.2
  393.5 189.3 %shard_map.154 = (f32[3,128,1024]{2,1,0:T(8,128)}, f32[16,128]{1,0:T(8,128)}) custom-call(f32[1,2,2,4,2,128,1024]{6,5,4,3,2,1,0:T(8,128)} %bitcast.241, bf16[2,2,2,4,2,128,1024]{6,5,4,3,2,1,0:T(8,128)(2,1)} %bitcast.242, f32[8,16,128]{2,1,0:T(8,128)} %bitcast.270), custom_call_target="tpu_custom_call" | custom-call | tf_op jit(solution)/shard_map/pallas_call | solution.py:217
  582.8 138.8 %shard_map.155 = (f32[3,2,2,128,1024]{4,3,2,1,0:T(8,128)}, bf16[3,2,2,128,1024]{4,3,2,1,0:T(8,128)(2,1)}) custom-call(f32[3,128,1024]{2,1,0:T(8,128)} %get-tuple-element.103.g_ref, f32[3,2,2,128,1024]{4,3,2,1,0:T(8,128)} %bitcast.244), custom_call_target="tpu_custom_call" | custom-call | tf_op jit(solution)/shard_map/pallas_call | solution.py:464
  721.7 8.3 %fusion.16 = f32[12,128,1024]{2,1,0:T(8,128)} fusion(f32[12,128,1024]{2,1,0:T(8,128)} %param.16, bf16[3,2,2,128,1024]{4,3,2,1,0:T(8,128)(2,1)} %get-tuple-element.104, f32[12]{0:T(128)S(1)} %copy-done.40), kind=kLoop, calls=%fused_computation.31 | loop fusion | flops 7864320 | bytes 15728688 | tf_op jit(solution)/shard_map/sub | solution.py:1261
  730.0 7.4 %bitcast_add_fusion = f32[12,128,1024]{2,1,0:T(8,128)} fusion(f32[3,2,2,128,1024]{4,3,2,1,0:T(8,128)S(1)} %copy-done.13, f32[12,128,1024]{2,1,0:T(8,128)} %param.17), kind=kLoop, calls=%fused_computation.32 | loop fusion | flops 3145728 | bytes 18874368 | tf_op jit(solution)/shard_map/add | solution.py:1258
  (200 shorter events, 45.6 us)
Async XLA Ops:
  145.9 2.7 copy-start.1
  157.7 11.0 %copy-start.12 = (f32[512,4,1024]{0,2,1:T(8,128)S(1)}, f32[512,4,1024]{0,2,1:T(8,128)}, u32[]{:S(2)}) copy-start(f32[512,4,1024]{0,2,1:T(8,128)} %copy.52) | copy-start | bytes 25165828
  157.7 11.5 %copy-start.14 = (bf16[1,512,1024]{2,1,0:T(8,128)(2,1)S(1)}, bf16[1,512,1024]{2,1,0:T(8,128)(2,1)}, u32[]{:S(2)}) copy-start(bf16[1,512,1024]{2,1,0:T(8,128)(2,1)} %param.13) | copy-start | bytes 3145732
  183.4 8.1 %copy-start.2 = (f32[512,1024]{1,0:T(8,128)S(1)}, f32[512,1024]{1,0:T(8,128)}, u32[]{:S(2)}) copy-start(f32[512,1024]{1,0:T(8,128)} %get-tuple-element.95) | copy-start | bytes 6291460
  191.5 2.2 copy-start.20
  203.2 21.2 %copy-start.38 = (f32[512]{0:T(512)}, f32[512]{0:T(512)S(1)}, u32[]{:S(2)}) copy-start(f32[512]{0:T(512)S(1)} %get-tuple-element.188) | copy-start | bytes 6148
  213.6 1.9 copy-start.15
  215.5 1.6 copy-start.8
  216.5 3.2 copy-start.17
  222.6 5.0 copy-start.7
  231.9 8.6 %collective-permute-start = (bf16[16,66,64]{2,1,0:T(8,128)(2,1)S(1)}, bf16[16,66,64]{2,1,0:T(8,128)(2,1)}, u32[]{:S(2)}, u32[]{:S(2)}) collective-permute-start(bf16[16,66,64]{2,1,0:T(8,128)(2,1)S(1)} %pad_maximum_fusion.6), channel_id=1, source_target_pairs={{4,0},{8,4},{12,8},{16,12},{20,16},{24,20},{28,24},{5,1},{9,5},{13... | collective-permute-start | bytes 405512 | tf_op jit(solution)/shard_map/while/body/eval_jaxpr/ppermute | solution.py:1023
  241.7 9.8 %collective-permute-start = (bf16[16,66,64]{2,1,0:T(8,128)(2,1)S(1)}, bf16[16,66,64]{2,1,0:T(8,128)(2,1)}, u32[]{:S(2)}, u32[]{:S(2)}) collective-permute-start(bf16[16,66,64]{2,1,0:T(8,128)(2,1)S(1)} %pad_maximum_fusion.6), channel_id=1, source_target_pairs={{4,0},{8,4},{12,8},{16,12},{20,16},{24,20},{28,24},{5,1},{9,5},{13... | collective-permute-start | bytes 405512 | tf_op jit(solution)/shard_map/while/body/eval_jaxpr/ppermute | solution.py:1023
  252.7 8.8 %collective-permute-start = (bf16[16,66,64]{2,1,0:T(8,128)(2,1)S(1)}, bf16[16,66,64]{2,1,0:T(8,128)(2,1)}, u32[]{:S(2)}, u32[]{:S(2)}) collective-permute-start(bf16[16,66,64]{2,1,0:T(8,128)(2,1)S(1)} %pad_maximum_fusion.6), channel_id=1, source_target_pairs={{4,0},{8,4},{12,8},{16,12},{20,16},{24,20},{28,24},{5,1},{9,5},{13... | collective-permute-start | bytes 405512 | tf_op jit(solution)/shard_map/while/body/eval_jaxpr/ppermute | solution.py:1023
  262.8 8.3 %collective-permute-start = (bf16[16,66,64]{2,1,0:T(8,128)(2,1)S(1)}, bf16[16,66,64]{2,1,0:T(8,128)(2,1)}, u32[]{:S(2)}, u32[]{:S(2)}) collective-permute-start(bf16[16,66,64]{2,1,0:T(8,128)(2,1)S(1)} %pad_maximum_fusion.6), channel_id=1, source_target_pairs={{4,0},{8,4},{12,8},{16,12},{20,16},{24,20},{28,24},{5,1},{9,5},{13... | collective-permute-start | bytes 405512 | tf_op jit(solution)/shard_map/while/body/eval_jaxpr/ppermute | solution.py:1023
  272.3 8.8 %collective-permute-start = (bf16[16,66,64]{2,1,0:T(8,128)(2,1)S(1)}, bf16[16,66,64]{2,1,0:T(8,128)(2,1)}, u32[]{:S(2)}, u32[]{:S(2)}) collective-permute-start(bf16[16,66,64]{2,1,0:T(8,128)(2,1)S(1)} %pad_maximum_fusion.6), channel_id=1, source_target_pairs={{4,0},{8,4},{12,8},{16,12},{20,16},{24,20},{28,24},{5,1},{9,5},{13... | collective-permute-start | bytes 405512 | tf_op jit(solution)/shard_map/while/body/eval_jaxpr/ppermute | solution.py:1023
  282.4 8.8 %collective-permute-start = (bf16[16,66,64]{2,1,0:T(8,128)(2,1)S(1)}, bf16[16,66,64]{2,1,0:T(8,128)(2,1)}, u32[]{:S(2)}, u32[]{:S(2)}) collective-permute-start(bf16[16,66,64]{2,1,0:T(8,128)(2,1)S(1)} %pad_maximum_fusion.6), channel_id=1, source_target_pairs={{4,0},{8,4},{12,8},{16,12},{20,16},{24,20},{28,24},{5,1},{9,5},{13... | collective-permute-start | bytes 405512 | tf_op jit(solution)/shard_map/while/body/eval_jaxpr/ppermute | solution.py:1023
  292.4 8.5 %collective-permute-start = (bf16[16,66,64]{2,1,0:T(8,128)(2,1)S(1)}, bf16[16,66,64]{2,1,0:T(8,128)(2,1)}, u32[]{:S(2)}, u32[]{:S(2)}) collective-permute-start(bf16[16,66,64]{2,1,0:T(8,128)(2,1)S(1)} %pad_maximum_fusion.6), channel_id=1, source_target_pairs={{4,0},{8,4},{12,8},{16,12},{20,16},{24,20},{28,24},{5,1},{9,5},{13... | collective-permute-start | bytes 405512 | tf_op jit(solution)/shard_map/while/body/eval_jaxpr/ppermute | solution.py:1023
  325.0 4.5 copy-start.6
  329.5 3.9 copy-start
  329.5 3.9 copy-start.19
  329.5 4.2 copy-start.22
  336.4 4.6 copy-start.46
  341.0 3.4 copy-start.24
  341.0 4.0 copy-start.25
  345.6 6.2 copy-start.10
  345.6 6.2 copy-start.21
  345.6 6.2 copy-start.35
  345.6 6.2 copy-start.39
  351.8 2.0 copy-start.4
  351.8 2.0 copy-start.27
  351.8 2.0 copy-start.48
  351.8 2.5 copy-start.49
  359.2 2.1 copy-start.18
  359.2 3.0 copy-start.44
  367.3 6.6 copy-start.43
  385.9 6.7 copy-start.37
  385.9 6.7 copy-start.36
  385.9 6.8 copy-start.34
  385.9 6.8 copy-start.33
  385.9 6.9 copy-start.28
  386.0 6.9 copy-start.29
  582.8 138.8 %copy-start.40 = (f32[12]{0:T(128)S(1)}, f32[12]{0:T(128)}, u32[]{:S(2)}) copy-start(f32[12]{0:T(128)} %constant.92.clone) | copy-start | bytes 148
  721.7 8.4 %copy-start.13 = (f32[3,2,2,128,1024]{4,3,2,1,0:T(8,128)S(1)}, f32[3,2,2,128,1024]{4,3,2,1,0:T(8,128)}, u32[]{:S(2)}) copy-start(f32[3,2,2,128,1024]{4,3,2,1,0:T(8,128)} %get-tuple-element.105) | copy-start | bytes 18874372
  730.0 7.5 %copy-start.26 = (f32[1664]{0:T(1024)S(1)}, f32[1664]{0:T(1024)}, u32[]{:S(2)}) copy-start(f32[1664]{0:T(1024)} %param.18) | copy-start | bytes 19972
  730.0 7.5 %copy-start.30 = (f32[1664]{0:T(1024)S(1)}, f32[1664]{0:T(1024)}, u32[]{:S(2)}) copy-start(f32[1664]{0:T(1024)} %param.19) | copy-start | bytes 19972
  730.0 7.5 %copy-start.31 = (f32[1664]{0:T(1024)S(1)}, f32[1664]{0:T(1024)}, u32[]{:S(2)}) copy-start(f32[1664]{0:T(1024)} %param.20) | copy-start | bytes 19972
  730.0 7.5 %copy-start.32 = (f32[16,128]{1,0:T(8,128)S(1)}, f32[16,128]{1,0:T(8,128)}, u32[]{:S(2)}) copy-start(f32[16,128]{1,0:T(8,128)} %get-tuple-element.106) | copy-start | bytes 24580
  730.0 8.1 %copy-start.23 = (bf16[512,1024]{1,0:T(8,128)(2,1)S(1)}, bf16[512,1024]{1,0:T(8,128)(2,1)}, u32[]{:S(2)}) copy-start(bf16[512,1024]{1,0:T(8,128)(2,1)} %get-tuple-element.91) | copy-start | bytes 3145732
  (9 other events, 11.5 us)

commit v3 on v2

--- a/solution.py
+++ b/solution.py
@@ -49,217 +49,6 @@
 
 
 CHUNK = 32
-
-
-def add_into(target, left, right):
-    rows = target.shape[-2]
-
-    def body(index, carry):
-        span = pl.ds(pl.multiple_of(index * CHUNK, CHUNK), CHUNK)
-        total = left[span, :].astype(jnp.float32) + right[span, :].astype(jnp.float32)
-        target[span, :] = total.astype(target.dtype)
-        return carry
-
-    lax.fori_loop(0, rows // CHUNK, body, 0)
-
-
-def reduce_kernel(
-    count, wide_ref, low_ref, small_ref, out_ref, small_out,
-    core_wide, core_low, own_wide, own_low, fs_wide, fs_low, fr_wide, fr_low, kept_first,
-    ss_wide, ss_low, sr_wide, sr_low, kept_second, zs_wide, zs_low, zr_wide, zr_low,
-    sm_recv, sm_part, sm_pair,
-    load_sem, cs, cr, fs, fr, es, er, zs, zr, ms, mr,
-):
-    z, x, y, c = places()
-    straight, across = others_along_seq(z, x, y, c, count)
-    pair = [device(z, 1 - x, y, c), device(z, x, 1 - y, c), device(z, x, y, 1 - c)]
-    greet(straight + across + pair[1:])
-    wide_count, low_count = wide_ref.shape[0], low_ref.shape[0]
-    order = [("low", b) for b in reversed(range(low_count))] + [
-        ("wide", b) for b in range(wide_count)
-    ]
-    steps = [(kind, b, k) for kind, b in order for k in range(count)]
-    total = len(steps)
-    small = []
-    seqs = [lax.rem(z + k, count) * 2 + x for k in range(1, count)] + [
-        lax.rem(z + k, count) * 2 + 1 - x for k in range(count)
-    ]
-    for k, (peer, there) in enumerate(zip(straight + across, seqs)):
-        small.append(remote(small_ref.at[there], sm_recv.at[k], ms.at[k], mr.at[k], peer))
-        small[-1].start()
-
-    def at(index):
-        kind, b, k = steps[index]
-        there = lax.rem(z + 1 + k, count)
-        source = wide_ref if kind == "wide" else low_ref
-        slot = b * count + k
-        return kind, b, k, there, source, slot
-
-    loads, cores, firsts, seconds, spread = [], [], [], [], {}
-    ring = 3
-
-    def pick(kind, wide, low):
-        return wide if kind == "wide" else low
-
-    def start_core(index):
-        kind, b, k, there, source, slot = at(index)
-        target = pick(kind, core_wide, core_low).at[slot]
-        copy = remote(source.at[b, :, 1 - c, there], target, cs.at[index], cr.at[index], pair[2])
-        copy.start()
-        cores.append(copy)
-
-    def start_load(index):
-        kind, b, k, there, source, slot = at(index)
-        target = pick(kind, own_wide, own_low).at[index % 2]
-        copy = pltpu.make_async_copy(source.at[b, :, c, there], target, load_sem.at[index])
-        copy.start()
-        loads.append(copy)
-
-    for index in range(min(3, total)):
-        start_core(index)
-    start_load(0)
-    for step in range(total + 3):
-        index = step
-        if index < total:
-            kind, b, k, there, source, slot = at(index)
-            if index + 1 < total:
-                start_load(index + 1)
-            if index + 3 < total:
-                start_core(index + 3)
-            loads[index].wait()
-            cores[index].wait_recv()
-            own = pick(kind, own_wide, own_low).at[index % 2]
-            got = pick(kind, core_wide, core_low).at[slot]
-            if index >= ring:
-                firsts[index - ring].wait_send()
-            out = pick(kind, fs_wide, fs_low).at[index % ring]
-            kept = kept_first.at[index % ring]
-            for j in range(2):
-                if k % 2 == 0:
-                    add_into(out.at[j], own.at[1 - y, j], got.at[1 - y, j])
-                    add_into(kept.at[j], own.at[y, j], got.at[y, j])
-                else:
-                    add_into(out.at[j], own.at[j, 1 - x], got.at[j, 1 - x])
-                    add_into(kept.at[j], own.at[j, x], got.at[j, x])
-            target = pick(kind, fr_wide, fr_low).at[slot]
-            copy = remote(out, target, fs.at[index], fr.at[index], pair[1 - k % 2])
-            copy.start()
-            firsts.append(copy)
-        index = step - 1
-        if 0 <= index < total:
-            kind, b, k, there, source, slot = at(index)
-            firsts[index].wait_recv()
-            kept = kept_first.at[index % ring]
-            got = pick(kind, fr_wide, fr_low).at[slot]
-            if index >= ring:
-                seconds[index - ring].wait_send()
-            out = pick(kind, ss_wide, ss_low).at[index % ring]
-            mine = x if k % 2 == 0 else y
-            add_into(out, kept.at[1 - mine], got.at[1 - mine])
-            add_into(kept_second.at[index % ring], kept.at[mine], got.at[mine])
-            target = pick(kind, sr_wide, sr_low).at[slot]
-            copy = remote(out, target, es.at[index], er.at[index], pair[k % 2])
-            copy.start()
-            seconds.append(copy)
-        index = step - 2
-        if 0 <= index < total:
-            kind, b, k, there, source, slot = at(index)
-            seconds[index].wait_recv()
-            got = pick(kind, sr_wide, sr_low).at[slot]
-            batch = b if kind == "wide" else wide_count + b
-            if k < count - 1:
-                out = pick(kind, zs_wide, zs_low).at[b, k]
-                add_into(out, kept_second.at[index % ring], got)
-                target = pick(kind, zr_wide, zr_low).at[b, k]
-                spread[index] = remote(out, target, zs.at[batch, k], zr.at[batch, k], straight[k])
-                spread[index].start()
-            else:
-                add_into(out_ref.at[batch], kept_second.at[index % ring], got)
-        index = step - 3
-        if 0 <= index < total:
-            kind, b, k, there, source, slot = at(index)
-            if k == count - 1:
-                batch = b if kind == "wide" else wide_count + b
-                for j in range(count - 1):
-                    spread[index - (count - 1) + j].wait_recv()
-                    add_into(out_ref.at[batch], out_ref.at[batch], pick(kind, zr_wide, zr_low).at[b, j])
-    part = small_ref[z * 2 + x]
-    for k, copy in enumerate(small):
-        copy.wait_recv()
-        part = part + sm_recv[k]
-    sm_part[0] = part
-    tail = []
-    for j in range(2):
-        copy = remote(sm_part.at[j], sm_pair.at[j], ms.at[len(small) + j], mr.at[len(small) + j], pair[1 + j])
-        copy.start()
-        copy.wait_recv()
-        tail.append(copy)
-        if j == 0:
-            sm_part[1] = sm_part[0] + sm_pair[0]
-        else:
-            small_out[...] = sm_part[1] + sm_pair[1]
-    for copy in small + tail + cores + firsts[-ring:] + seconds[-ring:] + list(spread.values()):
-        copy.wait_send()
-
-
-def reduce_rows(wide, low, small, nseq):
-    count = nseq // 2
-    wide_count, low_count = wide.shape[0] // 4, low.shape[0] // 4
-    width = wide.shape[-1]
-    rows = wide.shape[1] // nseq
-    batches = wide_count + low_count
-    steps = batches * count
-    wide = wide.reshape(wide_count, 2, 2, count, 2, rows, width)
-    low = low.reshape(low_count, 2, 2, count, 2, rows, width)
-    f32, bf16 = jnp.float32, jnp.bfloat16
-    V = pltpu.VMEM
-    nw, nl = wide_count * count, low_count * count
-    return pl.pallas_call(
-        functools.partial(reduce_kernel, count),
-        out_shape=(
-            jax.ShapeDtypeStruct((batches, rows, width), f32),
-            jax.ShapeDtypeStruct(small.shape[1:], f32),
-        ),
-        in_specs=[ANY, ANY, VMEM],
-        out_specs=[VMEM, VMEM],
-        scratch_shapes=[
-            V((nw, 2, 2, rows, width), f32),
-            V((nl, 2, 2, rows, width), bf16),
-            V((2, 2, 2, rows, width), f32),
-            V((2, 2, 2, rows, width), bf16),
-            V((3, 2, rows, width), f32),
-            V((3, 2, rows, width), bf16),
-            V((nw, 2, rows, width), f32),
-            V((nl, 2, rows, width), bf16),
-            V((3, 2, rows, width), f32),
-            V((3, rows, width), f32),
-            V((3, rows, width), bf16),
-            V((nw, rows, width), f32),
-            V((nl, rows, width), bf16),
-            V((3, rows, width), f32),
-            V((wide_count, count - 1, rows, width), f32),
-            V((low_count, count - 1, rows, width), bf16),
-            V((wide_count, count - 1, rows, width), f32),
-            V((low_count, count - 1, rows, width), bf16),
-            V((nseq - 1,) + small.shape[1:], f32),
-            V((2,) + small.shape[1:], f32),
-            V((2,) + small.shape[1:], f32),
-            DMA((steps,)),
-            DMA((steps,)),
-            DMA((steps,)),
-            DMA((steps,)),
-            DMA((steps,)),
-            DMA((steps,)),
-            DMA((steps,)),
-            DMA((batches, count - 1)),
-            DMA((batches, count - 1)),
-            DMA((nseq + 1,)),
-            DMA((nseq + 1,)),
-        ],
-        compiler_params=pltpu.CompilerParams(
-            collective_id=1, has_side_effects=True, vmem_limit_bytes=VMEM_LIMIT
-        ),
-    )(wide, low, small)
 
 
 SHIFTS = (0.0, 0.0, 0.1, 0.7, 0.7)
@@ -1007,79 +796,582 @@
     )(x, weights.reshape(batches, 2, 2, rows, width), small, lengths, order)
 
 
-D = 1024
-HEADS = 16
-HEAD_DIM = 64
-FF = 4096
-STEP = 10
-
-
-highest = lax.Precision.HIGHEST
-
-
-def passed_along(array, axis, by):
-    count = lax.axis_size(axis)
-    pairs = [(i, i + by) for i in range(count) if 0 <= i + by < count]
-    return lax.ppermute(array, axis, pairs)
-
-
-def layer_norm(values, gain, offset):
+def gelu_slope(values):
+    cube = 0.044715 * values * values
+    bend = jnp.tanh(0.7978845608028654 * values * (1.0 + cube))
+    return 0.5 * (1.0 + bend) + 0.5 * values * (1.0 - bend * bend) * (
+        0.7978845608028654 * (1.0 + 3.0 * cube)
+    )
+
+
+def norm_back(values, upstream, gain):
     center = values - jnp.mean(values, axis=-1, keepdims=True)
     spread = jnp.mean(center * center, axis=-1, keepdims=True)
-    return center * lax.rsqrt(spread + 1e-05) * gain + offset
-
-
-def feature(values):
-    return jax.nn.elu(values) + 1.0
-
-
-def segment_of(lengths_row, order_row, positions):
-    places = jnp.arange(lengths_row.shape[0], dtype=jnp.int32)
-    packed = jnp.sum(
-        jnp.where(order_row[:, None] == places[None, :], lengths_row[None, :], 0), axis=1
+    scale = lax.rsqrt(spread + 1e-05)
+    unit = center * scale
+    inner = upstream * gain
+    back = inner - jnp.mean(inner, axis=-1, keepdims=True)
+    back = scale * (back - unit * jnp.mean(inner * unit, axis=-1, keepdims=True))
+    return back, unit
+
+
+def pick_message(message, p):
+    down = pl.ds(pl.multiple_of(((p // 2) % 2) * PAIR, PAIR), PAIR)
+    block = message[p // 4, down, :]
+    block = jnp.where(p % 2 == 1, pltpu.roll(block, HALF, 1), block)
+    block = jnp.where(block_diagonal(), block, 0.0)
+    return split_two(block), message[0, pl.ds(256 + p, 1), :]
+
+
+class Sums:
+    def __init__(self, count, place, wide, product, bufs, sems, sums_ref):
+        self.count = count
+        self.z, self.x, self.y, self.c = z, x, y, c = place
+        self.wide, self.product, self.sums_ref = wide, product, sums_ref
+        (self.core_out, self.core_in, self.own, self.first_out, self.first_in, self.kept_one,
+         self.second_out, self.second_in, self.kept_two, self.far_out, self.far_in) = bufs
+        (self.cs, self.cr, self.fs, self.fr, self.es, self.er, self.zs, self.zr,
+         self.credit_core, self.credit_first, self.credit_second) = sems
+        self.pair = [device(z, 1 - x, y, c), device(z, x, 1 - y, c), device(z, x, y, 1 - c)]
+        self.steps = [(b, k) for b in (2, 1, 0) for k in range(count)]
+        self.total = len(self.steps)
+        self.cores, self.firsts, self.seconds, self.fars = [], [], [], {}
+        self.rows = sums_ref.shape[1]
+
+    def there(self, i):
+        return lax.rem(self.z + 1 + self.steps[i][1], self.count)
+
+    def parts(self, i):
+        return (0, 1) if self.steps[i][0] in self.wide else (0,)
+
+    def span(self, ref, i):
+        return ref if len(self.parts(i)) == 2 else ref.at[pl.ds(0, 1)]
+
+    def give(self, semaphore, peer):
+        pl.semaphore_signal(semaphore, inc=1, device_id=peer, device_id_type=MESH)
+
+    def store(self, value, targets):
+        high = value.astype(jnp.bfloat16)
+        targets[0][...] = high
+        if len(targets) == 2:
+            targets[1][...] = (value - high.astype(jnp.float32)).astype(jnp.bfloat16)
+
+    def add(self, i, base, got, send, keep):
+        def body(index, carry):
+            at = pl.ds(pl.multiple_of(index * CHUNK, CHUNK), CHUNK)
+            value = base[at, :]
+            for part in got:
+                value = value + part[at, :].astype(jnp.float32)
+            if keep is not None:
+                keep[at, :] = value
+            else:
+                self.store(value, [ref.at[at] for ref in send])
+            return carry
+
+        lax.fori_loop(0, self.rows // CHUNK, body, 0)
+
+    def stage_a(self, i):
+        slot = i % 2
+        batch = self.steps[i][0]
+        if i >= 2:
+            self.cores[i - 2].wait_send()
+        for yy in range(2):
+            value = self.product(i, batch, yy, 1 - self.c)
+            for xx in range(2):
+                rows = slice(xx * self.rows, (xx + 1) * self.rows)
+                self.store(value[rows], [self.core_out.at[slot, h, yy, xx] for h in self.parts(i)])
+        if i >= 2:
+            pl.semaphore_wait(self.credit_core, 1)
+        source, target = self.span(self.core_out.at[slot], i), self.span(self.core_in.at[slot], i)
+        self.cores.append(remote(source, target, self.cs.at[i], self.cr.at[i], self.pair[2]))
+        self.cores[i].start()
+        for yy in range(2):
+            value = self.product(i, batch, yy, self.c)
+            for xx in range(2):
+                self.own[yy, xx] = value[xx * self.rows : (xx + 1) * self.rows]
+
+    def stage_b(self, i):
+        slot = i % 2
+        k = self.steps[i][1]
+        x, y = self.x, self.y
+        self.cores[i].wait_recv()
+        if i >= 3:
+            self.firsts[i - 3].wait_send()
+        out = self.first_out.at[i % 3]
+        for j in range(2):
+            away, near = ((1 - y, j), (y, j)) if k % 2 == 0 else ((j, 1 - x), (j, x))
+            for at, send, keep in (
+                (away, [out.at[h, j] for h in self.parts(i)], None),
+                (near, None, self.kept_one.at[j]),
+            ):
+                got = [self.core_in.at[slot, h, at[0], at[1]] for h in self.parts(i)]
+                self.add(i, self.own.at[at[0], at[1]], got, send, keep)
+        if i + 2 < self.total:
+            self.give(self.credit_core, self.pair[2])
+        if i >= 4:
+            pl.semaphore_wait(self.credit_first.at[i % 2], 1)
+        peer = self.pair[1 - k % 2]
+        source, target = self.span(out, i), self.span(self.first_in.at[i % 4], i)
+        self.firsts.append(remote(source, target, self.fs.at[i], self.fr.at[i], peer))
+        self.firsts[i].start()
+
+    def stage_c(self, i):
+        k = self.steps[i][1]
+        mine = self.x if k % 2 == 0 else self.y
+        self.firsts[i].wait_recv()
+        if i >= 3:
+            self.seconds[i - 3].wait_send()
+        out = self.second_out.at[i % 3]
+        got = self.first_in.at[i % 4]
+        self.add(i, self.kept_one.at[1 - mine], [got.at[h, 1 - mine] for h in self.parts(i)],
+                 [out.at[h] for h in self.parts(i)], None)
+        self.add(i, self.kept_one.at[mine], [got.at[h, mine] for h in self.parts(i)], None, self.kept_two)
+        if i + 4 < self.total:
+            self.give(self.credit_first.at[i % 2], self.pair[1 - k % 2])
+        if i >= 4:
+            pl.semaphore_wait(self.credit_second.at[i % 2], 1)
+        source, target = self.span(out, i), self.span(self.second_in.at[i % 4], i)
+        self.seconds.append(remote(source, target, self.es.at[i], self.er.at[i], self.pair[k % 2]))
+        self.seconds[i].start()
+
+    def stage_d(self, i):
+        b, k = self.steps[i]
+        self.seconds[i].wait_recv()
+        got = [self.second_in.at[i % 4, h] for h in self.parts(i)]
+        if k < self.count - 1:
+            if i >= self.count:
+                self.fars[i - self.count].wait_send()
+            out = self.far_out.at[k]
+            self.add(i, self.kept_two, got, [out.at[h] for h in self.parts(i)], None)
+            peer = device(self.there(i), self.x, self.y, self.c)
+            source, target = self.span(out, i), self.span(self.far_in.at[b, k], i)
+            self.fars[i] = remote(source, target, self.zs.at[b, k], self.zr.at[b, k], peer)
+            self.fars[i].start()
+        else:
+            self.add(i, self.kept_two, got, None, self.sums_ref.at[b])
+        if i + 4 < self.total:
+            self.give(self.credit_second.at[i % 2], self.pair[k % 2])
+
+    def stage_e(self, i):
+        b, k = self.steps[i]
+        if k < self.count - 1:
+            return
+        for j in range(self.count - 1):
+            self.fars[i - self.count + 1 + j].wait_recv()
+            got = [self.far_in.at[b, j, h] for h in self.parts(i)]
+            self.add(i, self.sums_ref.at[b], got, None, self.sums_ref.at[b])
+
+    def tick(self, i):
+        for lag, stage in ((4, self.stage_e), (3, self.stage_d), (2, self.stage_c), (1, self.stage_b), (0, self.stage_a)):
+            if 0 <= i - lag < self.total:
+                stage(i - lag)
+
+    def wait_sends(self):
+        for copy in self.cores[-2:] + self.firsts[-3:] + self.seconds[-3:]:
+            copy.wait_send()
+        for i, copy in self.fars.items():
+            if i >= self.total - self.count:
+                copy.wait_send()
+
+
+def backward_kernel(
+    count, aligned, x_ref, dy_ref, w_ref, rows_ref, low_ref, pre_ref, ratio_ref, left_ref, resid_ref, up_ref, act_ref,
+    state, lengths_ref, order_ref,
+    grad_ref, sums_ref, small_out,
+    core_out, core_in, own, first_out, first_in, kept_one, second_out, second_in, kept_two, far_out, far_in,
+    big, left, wbuf, ubuf, acc, da, dq_low, dnum, dden, keep, flags, gs,
+    message, across, part, spread, total_ref, state_back, sm_send, sm_recv, sm_part, sm_pair,
+    load_sem, lt_sem, cs, cr, fs, fr, es, er, zs, zr, credit_core, credit_first, credit_second, rs, rr, ms, mr,
+):
+    place = z, x, y, c = places()
+    straight, far = others_along_seq(z, x, y, c, count)
+    pair = [device(z, 1 - x, y, c), device(z, x, 1 - y, c), device(z, x, y, 1 - c)]
+    group, width = x_ref.shape
+    bands = group // BAND
+    pairs = width // PAIR
+    block_rows = 2 * sums_ref.shape[1]
+    f32, bf16 = jnp.float32, jnp.bfloat16
+    issued = []
+
+    def load(source, target):
+        copy = pltpu.make_async_copy(source, target, load_sem.at[len(issued)])
+        copy.start()
+        issued.append(copy)
+        return copy
+
+    def load_left(i):
+        b = sums.steps[i][0]
+        at = pl.ds(pl.multiple_of(sums.there(i) * block_rows, block_rows), block_rows)
+        slot = left.at[i % 2]
+        if b == 2:
+            pieces = [(act_ref.at[:, at], slot)]
+        elif b == 1:
+            pieces = [(left_ref.at[pl.ds(2, 1), at], slot.at[pl.ds(0, 1)])]
+        else:
+            pieces = [(left_ref.at[pl.ds(0, 2), at], slot.at[pl.ds(0, 2)])]
+        copies = [pltpu.make_async_copy(s, t, lt_sem.at[i]) for s, t in pieces]
+        for copy in copies:
+            copy.start()
+        return copies
+
+    lefts = {}
+
+    def product(i, batch, yy, cc):
+        unit = 2 * yy + cc
+        if batch == 2:
+            lhs, rhs = left[i % 2, unit], dy_ref[...]
+        elif batch == 1:
+            lhs, rhs = left[i % 2, 0], big[unit]
+        else:
+            lhs, rhs = left[i % 2, yy * cc], big[unit]
+        return dot(lhs, rhs)
+
+    sums = Sums(
+        count, place, (0,), product,
+        (core_out, core_in, own, first_out, first_in, kept_one, second_out, second_in, kept_two, far_out, far_in),
+        (cs, cr, fs, fr, es, er, zs, zr, credit_core, credit_first, credit_second), sums_ref,
     )
-    ends = jnp.cumsum(packed)
-    return jnp.sum((positions[:, None] >= ends[None, :]).astype(jnp.int32), axis=1)
-
-
-def split_small(vector, width):
-    pieces = [vector[index * width : (index + 1) * width] for index in range(9)]
-    return pieces + [vector[9 * width :]]
-
-
-def unit_rates(blocks):
-    return jnp.array([0.5, 0.5, 0.5, 4.0] + [0.5] * blocks + [0.25] * blocks, dtype=jnp.float32)
-
-
-def pack_state(matrix, totals, passes):
-    flags = jnp.zeros_like(totals[:, None, :]) + passes
-    return jnp.concatenate([matrix, totals[:, None, :], flags], axis=1)
-
-
-def combine_states(earlier, later):
-    scale = later[:, -1:, :]
-    head_rows = later[:, :-1, :] + scale * earlier[:, :-1, :]
-    return jnp.concatenate([head_rows, earlier[:, -1:, :] * scale], axis=1)
-
-
-def relay_forward(own):
-
-    def forward_turn(turn, running):
-        return passed_along(combine_states(running, own), "seq", 1)
-
-    arriving = lax.fori_loop(0, lax.axis_size("seq") - 1, forward_turn, jnp.zeros_like(own))
-    return arriving
-
-
-def relay_backward(own):
-
-    def backward_turn(turn, running):
-        return passed_along(combine_states(running, own).astype(jnp.bfloat16), "seq", -1).astype(
-            jnp.float32
+
+    def tick(i):
+        if i < sums.total:
+            for copy in lefts[i]:
+                copy.wait()
+            if i + 1 < sums.total:
+                lefts[i + 1] = load_left(i + 1)
+        sums.tick(i)
+
+    lefts[0] = load_left(0)
+    blocks = big.shape[0]
+    w_loads = {(2, j): load(w_ref.at[8 + j], wbuf.at[j]) for j in range(2)}
+    u_loads = {j: load(up_ref.at[j], ubuf.at[j]) for j in range(2)}
+    resid_load = load(resid_ref, grad_ref)
+    greet(straight + far + pair[1:])
+    ends = image_ends(lengths_ref, order_ref)
+    fill_masks(ends, (z * 2 + x) * group, group, keep, flags)
+    factors = backward_factors(ends, group, count, z, x)
+    gs[...] = jnp.zeros_like(gs)
+
+    def add_row(index, value, lanes=slice(None)):
+        gs[index : index + 1, lanes] = gs[index : index + 1, lanes] + jnp.sum(
+            value.astype(f32), axis=0, keepdims=True
         )
 
-    leaving = lax.fori_loop(0, lax.axis_size("seq") - 1, backward_turn, jnp.zeros_like(own))
-    return leaving
+    def unit_of(slot):
+        return wbuf[slot].reshape(width, width)
+
+    for i in range(bands):
+        add_row(8, dy_ref[i * BAND : (i + 1) * BAND, :])
+    for j in range(blocks):
+        tick(j)
+        w_loads[2, j].wait()
+        u_loads[j].wait()
+
+        def hidden_back(i, carry):
+            span = band_span(i)
+            back = dot(dy_ref[span, :], unit_of(j % 2), True)
+            back = (back * gelu_slope(ubuf[j % 2, span, :])).astype(bf16)
+            big[j, span, :] = back
+            add_row(9 + j, back)
+            return carry
+
+        lax.fori_loop(0, bands, hidden_back, 0)
+        if j + 2 < blocks:
+            w_loads[2, j + 2] = load(w_ref.at[8 + j + 2], wbuf.at[j % 2])
+            u_loads[j + 2] = load(up_ref.at[j + 2], ubuf.at[j % 2])
+        else:
+            w_loads[1, j - 2] = load(w_ref.at[4 + j - 2], wbuf.at[j % 2])
+            u_loads[j + 2] = load(ratio_ref.at[j - 2], ubuf.at[j % 2])
+    for j in range(blocks):
+        if j % 2 == 0:
+            tick(blocks + j // 2)
+        w_loads[1, j].wait()
+
+        def up_back(i, carry):
+            span = band_span(i)
+            back = dot(big[j, span, :], unit_of(j % 2), True)
+            acc[span, :] = back if j == 0 else acc[span, :] + back
+            return carry
+
+        lax.fori_loop(0, bands, up_back, 0)
+        if j + 2 < blocks:
+            w_loads[1, j + 2] = load(w_ref.at[4 + j + 2], wbuf.at[j % 2])
+        elif j + 2 == blocks:
+            w_loads[0, 3] = load(w_ref.at[3], wbuf.at[0])
+        else:
+            low_loads = [load(low_ref.at[0], wbuf.at[1, 0]), load(low_ref.at[1], wbuf.at[1, 1])]
+    resid_load.wait()
+    w_loads[0, 3].wait()
+
+    def middle_back(i, carry):
+        span = band_span(i)
+        upstream = acc[span, :]
+        back, unit = norm_back(grad_ref[span, :], upstream, rows_ref[2:3, :])
+        add_row(2, upstream * unit)
+        add_row(3, upstream)
+        total = dy_ref[span, :].astype(f32) + back
+        grad_ref[span, :] = total
+        low = total.astype(bf16)
+        da[span, :] = low
+        add_row(7, low)
+        acc[span, :] = dot(low, unit_of(0), True)
+        return carry
+
+    lax.fori_loop(0, bands, middle_back, 0)
+    low_loads.append(load(low_ref.at[2], wbuf.at[0, 0]))
+    u_loads[blocks].wait()
+    u_loads[blocks + 1].wait()
+
+    def ratio_back(p, carry):
+        lanes = pair_span(p)
+        first = lanes_of(0)
+        for i in range(bands):
+            span = slice(i * BAND, (i + 1) * BAND)
+            inverse = 1.0 / ubuf[1, span, lanes]
+            scaled = acc[span, lanes] * inverse
+            dnum[span, lanes] = scaled.astype(bf16)
+            weighted = scaled * ubuf[0, span, lanes] * inverse
+            one = jnp.sum(jnp.where(first, weighted, 0.0), axis=1, keepdims=True)
+            two = jnp.sum(jnp.where(first, 0.0, weighted), axis=1, keepdims=True)
+            dden[span, lanes] = -jnp.where(first, one, two)
+        return carry
+
+    lax.fori_loop(0, pairs, ratio_back, 0)
+    for copy in low_loads:
+        copy.wait()
+    query, key, value = wbuf.at[1, 0], wbuf.at[1, 1], wbuf.at[0, 0]
+    pack_message(query, dnum, flags.at[0], dden, message)
+    relay = Relay(count, factors, message, across, part, spread, total_ref, state_back, (rs, rr), place)
+    relay.swap()
+    pre_load = load(pre_ref.at[0], acc)
+    pre_load.wait()
+
+    def attend_back(p, carry):
+        lanes = pair_span(p)
+        (state_high, state_low), totals = pick_message(state, p)
+        lane = lax.broadcasted_iota(jnp.int32, (1, PAIR), 1) % HALF
+        for band in range(bands):
+            span = slice(band * BAND, (band + 1) * BAND)
+            upto = (band + 1) * BAND
+            back = dnum[span, lanes]
+            below = dden[span, lanes]
+            high, low = split_two(pltpu.roll(below, HALF, 1))
+            extra = jnp.where(lane == 0, high, jnp.where(lane == 1, low, jnp.zeros_like(low)))
+            asked = query[span, lanes]
+            keys = key[0:upto, lanes]
+            held = value[0:upto, lanes]
+            kept = keep[span, 0:upto]
+            found, key_back, value_back = [], 0.0, 0.0
+            for head in range(2):
+                mine = lanes_of(head)
+                masked = jnp.where(mine, asked, 0)
+                scores = (dot(masked, keys, True) * kept).astype(bf16)
+                scores_back = dot(jnp.where(mine, back, extra), jnp.where(mine, held, 1), True)
+                scores_back = (scores_back * kept).astype(bf16)
+                found.append(dot(scores_back, keys))
+                key_back = key_back + dot_down(scores_back, masked)
+                value_back = value_back + dot_down(scores, jnp.where(mine, back, 0))
+            across_blocks = dot(back, state_high, True) + dot(back, state_low, True) + below * totals
+            query_back = jnp.where(lanes_of(0), found[0], found[1]) + flags[0, span, :] * across_blocks
+            pre = acc[span, lanes]
+            slope = jnp.where(pre > 0, 1.0, jnp.exp(jnp.minimum(pre, 0.0)))
+            dq_low[span, lanes] = (query_back * slope).astype(bf16)
+            for index, total in ((0, key_back), (1, value_back)):
+                if band:
+                    ubuf[index, 0 : upto - BAND, lanes] = (
+                        ubuf[index, 0 : upto - BAND, lanes] + total[: upto - BAND]
+                    )
+                ubuf[index, span, lanes] = total[upto - BAND :]
+        return carry
+
+    lax.fori_loop(0, pairs // 4, attend_back, 0)
+    tick(blocks + 2)
+    relay.spread_out()
+    lax.fori_loop(pairs // 4, pairs // 2, attend_back, 0)
+    tick(blocks + 3)
+    relay.join()
+    lax.fori_loop(pairs // 2, pairs, attend_back, 0)
+    pre_load = load(pre_ref.at[1], acc)
+    for i in range(blocks + 4, sums.total - count):
+        tick(i)
+    relay.finish()
+    pre_load.wait()
+
+    def attend_close(p, carry):
+        lanes = pair_span(p)
+        (back_high, back_low), totals = pick_message(state_back, p)
+        for i in range(bands):
+            span = slice(i * BAND, (i + 1) * BAND)
+            flag = flags[1, span, :]
+            held, keys = value[span, lanes], key[span, lanes]
+            key_back = ubuf[0, span, lanes] + flag * (
+                dot(held, back_high, True) + dot(held, back_low, True) + totals
+            )
+            pre = acc[span, lanes]
+            slope = jnp.where(pre > 0, 1.0, jnp.exp(jnp.minimum(pre, 0.0)))
+            big[1, span, lanes] = (key_back * slope).astype(bf16)
+            value_back = ubuf[1, span, lanes] + flag * (dot(keys, back_high) + dot(keys, back_low))
+            big[2, span, lanes] = value_back.astype(bf16)
+            big[0, span, lanes] = dq_low[span, lanes]
+            big[3, span, lanes] = da[span, lanes]
+        for index in range(3):
+            total = jnp.sum(big[index, :, lanes].astype(f32), axis=0, keepdims=True)
+            gs[4 + index : 5 + index, lanes] = total
+        return carry
+
+    lax.fori_loop(0, pairs, attend_close, 0)
+    w_loads[0, 0] = load(w_ref.at[0], wbuf.at[0])
+    w_loads[0, 1] = load(w_ref.at[1], wbuf.at[1])
+    step = sums.total - count
+    for j in range(3):
+        tick(step)
+        step += 1
+        w_loads[0, j].wait()
+
+        def input_back(i, carry):
+            span = band_span(i)
+            back = dot(big[j, span, :], unit_of(j % 2), True)
+            acc[span, :] = back if j == 0 else acc[span, :] + back
+            return carry
+
+        lax.fori_loop(0, bands, input_back, 0)
+        if j == 0:
+            w_loads[0, 2] = load(w_ref.at[2], wbuf.at[0])
+
+    def outer_back(i, carry):
+        span = band_span(i)
+        upstream = acc[span, :]
+        back, unit = norm_back(x_ref[span, :].astype(f32), upstream, rows_ref[0:1, :])
+        add_row(0, upstream * unit)
+        add_row(1, upstream)
+        grad_ref[span, :] = grad_ref[span, :] + back
+        return carry
+
+    lax.fori_loop(0, bands, outer_back, 0)
+    small, tail = [], []
+    if aligned:
+        share_rows = 13 * 1024 // 128 // (count * 2)
+        for j in range(13 * 8):
+            sm_send[j // share_rows, j % share_rows : j % share_rows + 1, :] = gs[
+                j // 8 : j // 8 + 1, (j % 8) * 128 : (j % 8 + 1) * 128
+            ]
+        seqs = [lax.rem(z + k, count) * 2 + x for k in range(1, count)]
+        seqs += [lax.rem(z + k, count) * 2 + 1 - x for k in range(count)]
+        for k, (peer, there) in enumerate(zip(straight + far, seqs)):
+            small.append(remote(sm_send.at[there], sm_recv.at[k], ms.at[k], mr.at[k], peer))
+            small[-1].start()
+    while step < sums.total:
+        tick(step)
+        step += 1
+    last = sums.total + 4
+    if aligned:
+        total = sm_send[z * 2 + x]
+        for k, copy in enumerate(small):
+            copy.wait_recv()
+            total = total + sm_recv[k]
+        sm_part[0] = total
+        for j in range(2):
+            index = len(small) + j
+            copy = remote(sm_part.at[j], sm_pair.at[j], ms.at[index], mr.at[index], pair[1 + j])
+            copy.start()
+            tail.append(copy)
+            tick(step)
+            step += 1
+            copy.wait_recv()
+            if j == 0:
+                sm_part[1] = sm_part[0] + sm_pair[0]
+            else:
+                small_out[...] = sm_part[1] + sm_pair[1]
+    else:
+        small_out[...] = gs[...]
+    while step < last:
+        tick(step)
+        step += 1
+    sums.wait_sends()
+    relay.wait_sends()
+    for copy in small + tail:
+        copy.wait_send()
+
+
+def backward(x, dy, w, rows, low, pre, ratio, left, resid, up, act, state, lengths, order, nseq, aligned):
+    group, width = x.shape
+    count, batches = nseq // 2, 3
+    share_rows = width // nseq
+    steps = batches * count
+    f32, bf16 = jnp.float32, jnp.bfloat16
+    V, S, R = pltpu.VMEM, jax.ShapeDtypeStruct, pltpu.SemaphoreType.REGULAR
+    smem = pl.BlockSpec(memory_space=pltpu.SMEM)
+    message = (2, 264, PAIR)
+    blocks = up.shape[0]
+    piece = (share_rows, width)
+    small = (16, 128)
+    return pl.pallas_call(
+        functools.partial(backward_kernel, count, aligned),
+        out_shape=(
+            S((group, width), f32),
+            S((batches,) + piece, f32),
+            S(small if aligned else (16, width), f32),
+        ),
+        in_specs=[VMEM, VMEM, ANY, VMEM] + [ANY] * 7 + [VMEM, smem, smem],
+        out_specs=[VMEM, VMEM, VMEM],
+        scratch_shapes=[
+            V((2, 2, 2, 2) + piece, bf16),
+            V((2, 2, 2, 2) + piece, bf16),
+            V((2, 2) + piece, f32),
+            V((3, 2, 2) + piece, bf16),
+            V((4, 2, 2) + piece, bf16),
+            V((2,) + piece, f32),
+            V((3, 2) + piece, bf16),
+            V((4, 2) + piece, bf16),
+            V(piece, f32),
+            V((count - 1, 2) + piece, bf16),
+            V((batches, count - 1, 2) + piece, bf16),
+            V((blocks, group, width), bf16),
+            V((2, blocks, 2 * share_rows, group), bf16),
+            V((2, width // group, group, width), bf16),
+            V((2, group, width), f32),
+            V((group, width), f32),
+            V((group, width), bf16),
+            V((group, width), bf16),
+            V((group, width), bf16),
+            V((group, width), f32),
+            V((group, group), f32),
+            V((2, group, PAIR), f32),
+            V((16, width), f32),
+            V(message, f32),
+            V(message, f32),
+            V(message[1:], f32),
+            V((count - 1,) + message[1:], f32),
+            V(message, f32),
+            V(message, f32),
+            V((nseq,) + small, f32),
+            V((nseq - 1,) + small, f32),
+            V((2,) + small, f32),
+            V((2,) + small, f32),
+            DMA((32,)),
+            DMA((steps,)),
+            DMA((steps,)),
+            DMA((steps,)),
+            DMA((steps,)),
+            DMA((steps,)),
+            DMA((steps,)),
+            DMA((steps,)),
+            DMA((batches, count - 1)),
+            DMA((batches, count - 1)),
+            R,
+            R((2,)),
+            R((2,)),
+            DMA((count + 1,)),
+            DMA((count + 1,)),
+            DMA((nseq + 1,)),
+            DMA((nseq + 1,)),
+        ],
+        compiler_params=pltpu.CompilerParams(
+            collective_id=1, has_side_effects=True, vmem_limit_bytes=VMEM_LIMIT
+        ),
+    )(x, dy, w.reshape(-1, width // group, group, width), rows, low, pre, ratio, left, resid, up, act, state, lengths, order)
+
+
+STEP = 10
 
 
 def padded(vector):
@@ -1091,12 +1383,7 @@
 def local(
     tokens, cotangent, lengths, order, weights, momentum, small_params, moment_one, moment_two
 ):
-    group = tokens.shape[1]
     width = tokens.shape[2]
-    heads = HEADS
-    depth = HEAD_DIM
-    blocks = FF // D
-    units = weights.shape[0]
     nseq = lax.axis_size("seq")
     share = small_params.shape[0]
     rounded = lax.reduce_precision(small_params, 8, 7)
@@ -1105,165 +1392,31 @@
         shared = padded(rounded)
     else:
         shared = lax.all_gather(rounded, "seq", axis=0, tiled=True).reshape(-1, width)
-    (gathered, block_out, rows, low, pre, ratio, left, resid, up, act, state) = forward(
+    (gathered, block_out, rows, *kept) = forward(
         tokens[0], weights, shared, lengths, order, nseq, aligned
     )
-    block_out = block_out[None]
-    gathered = gathered.reshape(units, width, width)
-    w_query, w_key, w_value, w_out = gathered[0], gathered[1], gathered[2], gathered[3]
-    w_up = gathered[4 : 4 + blocks]
-    w_down = gathered[4 + blocks :].reshape(blocks * width, width)
-    gain_one, bias_one, gain_two, bias_two = rows[0], rows[1], rows[2], rows[3]
-    start = lax.axis_index("seq") * group
-    positions = start + jnp.arange(group, dtype=jnp.int32)
-    segment = segment_of(lengths[0], order[0], positions)
-    before = segment_of(lengths[0], order[0], jnp.reshape(start - 1, (1,)))[0]
-    offsets = jnp.arange(group, dtype=jnp.int32)
-    keep = ((offsets[None, :] <= offsets[:, None]) & (segment[:, None] == segment[None, :])).astype(
-        jnp.float32
+    input_grad, sums, row_small = backward(
+        tokens[0], cotangent[0], gathered, rows, *kept, lengths, order, nseq, aligned
     )
-    incoming = (segment == before).astype(jnp.float32)
-    finals = (segment == segment[-1]).astype(jnp.float32)
-    passes = (segment[-1] == before).astype(jnp.float32)
-    inputs = tokens[0].astype(jnp.float32)
-    normed = left[0].T
-    query_low, key_low, value_low = [low[i].reshape(group, heads, depth) for i in range(3)]
-    query_pre, key_pre = pre[0], pre[1]
-    numer = ratio[0].reshape(group, heads, depth)
-    denom = ratio[1].reshape(group, heads, depth)[:, :, 0]
-    attended, hidden = left[1].T, left[2].T
-    scores_low = (
-        jnp.einsum("thd,shd->hts", query_low, key_low, preferred_element_type=jnp.float32)
-        * keep[None]
-    ).astype(jnp.bfloat16)
-    query_wide = query_low.astype(jnp.float32)
-    quads = state[:, :256].reshape(4, 128, 128)
-    state_in = jnp.stack(
-        [quads[:, :64, :64], quads[:, 64:, 64:], quads[:, :64, 64:], quads[:, 64:, :64]], axis=1
-    ).reshape(heads, depth, depth)
-    total_in = state[0, 256:].reshape(heads, depth)
-    up_pre = up.transpose(1, 0, 2).reshape(group, blocks * width)
-    active = act.transpose(2, 0, 1).reshape(group, blocks * width)
-    grad_out = cotangent[0]
-    grad_down = jnp.einsum("tf,td->fd", active, grad_out, preferred_element_type=jnp.float32)
-    grad_bias_down = jnp.sum(grad_out.astype(jnp.float32), axis=0)
-    grad_active = jnp.einsum("td,fd->tf", grad_out, w_down, preferred_element_type=jnp.float32)
-    _, gelu_pull = jax.vjp(jax.nn.gelu, up_pre)
-    grad_up_low = gelu_pull(grad_active)[0].astype(jnp.bfloat16)
-    grad_up_blocks = grad_up_low.reshape(group, blocks, width)
-    grad_w_up = jnp.einsum(
-        "td,tjf->jdf", hidden, grad_up_blocks, preferred_element_type=jnp.float32
-    )
-    grad_bias_up = jnp.sum(grad_up_low.astype(jnp.float32), axis=0)
-    grad_hidden = jnp.einsum(
-        "tjf,jdf->td", grad_up_blocks, w_up, preferred_element_type=jnp.float32
-    )
-    _, norm_two_pull = jax.vjp(layer_norm, resid, gain_two, bias_two)
-    grad_resid_norm, grad_gain_two, grad_bias_two = norm_two_pull(grad_hidden)
-    grad_resid = grad_out.astype(jnp.float32) + grad_resid_norm
-    grad_branch = grad_resid.astype(jnp.bfloat16)
-    grad_w_out = jnp.einsum("tk,td->kd", attended, grad_branch, preferred_element_type=jnp.float32)
-    grad_bias_o = jnp.sum(grad_branch.astype(jnp.float32), axis=0)
-    grad_ratio = jnp.einsum(
-        "td,kd->tk", grad_branch, w_out, preferred_element_type=jnp.float32
-    ).reshape(group, heads, depth)
-    grad_numer = (grad_ratio / denom[:, :, None]).astype(jnp.bfloat16)
-    grad_denom = -jnp.sum(grad_ratio * numer, axis=2) / (denom * denom)
-    grad_scores = jnp.einsum(
-        "the,she->hts", grad_numer, value_low, preferred_element_type=jnp.float32
-    )
-    grad_scores_low = ((grad_scores + grad_denom.T[:, :, None]) * keep[None]).astype(jnp.bfloat16)
-    grad_query = jnp.einsum(
-        "hts,shd->thd", grad_scores_low, key_low, preferred_element_type=jnp.float32
-    )
-    grad_key = jnp.einsum(
-        "hts,thd->shd", grad_scores_low, query_low, preferred_element_type=jnp.float32
-    )
-    grad_value = jnp.einsum(
-        "hts,the->she", scores_low, grad_numer, preferred_element_type=jnp.float32
-    )
-    numer_grad_wide = grad_numer.astype(jnp.float32)
-    grad_query = grad_query + incoming[:, None, None] * (
-        jnp.einsum("the,hde->thd", numer_grad_wide, state_in, precision=highest)
-        + grad_denom[:, :, None] * total_in[None]
-    )
-    query_masked = query_low * incoming.astype(jnp.bfloat16)[:, None, None]
-    grad_state_in = jnp.einsum(
-        "thd,the->hde", query_masked, grad_numer, preferred_element_type=jnp.float32
-    )
-    grad_total_in = jnp.einsum(
-        "thd,th->hd", query_wide * incoming[:, None, None], grad_denom, precision=highest
-    )
-    leaving = relay_backward(pack_state(grad_state_in, grad_total_in, passes))
-    grad_state = leaving[:, :depth, :]
-    grad_total = leaving[:, depth, :]
-    value_wide = value_low.astype(jnp.float32)
-    key_wide = key_low.astype(jnp.float32)
-    grad_key = grad_key + finals[:, None, None] * (
-        jnp.einsum("she,hde->shd", value_wide, grad_state, precision=highest) + grad_total[None]
-    )
-    grad_value = grad_value + finals[:, None, None] * jnp.einsum(
-        "shd,hde->she", key_wide, grad_state, precision=highest
-    )
-    _, query_pull = jax.vjp(feature, query_pre)
-    _, key_pull = jax.vjp(feature, key_pre)
-    grad_query_low = query_pull(grad_query.reshape(group, width))[0].astype(jnp.bfloat16)
-    grad_key_low = key_pull(grad_key.reshape(group, width))[0].astype(jnp.bfloat16)
-    grad_value_low = grad_value.reshape(group, width).astype(jnp.bfloat16)
-    grad_w_query = jnp.einsum(
-        "tk,tj->kj", normed, grad_query_low, preferred_element_type=jnp.float32
-    )
-    grad_w_key = jnp.einsum("tk,tj->kj", normed, grad_key_low, preferred_element_type=jnp.float32)
-    grad_w_value = jnp.einsum(
-        "tk,tj->kj", normed, grad_value_low, preferred_element_type=jnp.float32
-    )
-    grad_bias_q = jnp.sum(grad_query_low.astype(jnp.float32), axis=0)
-    grad_bias_k = jnp.sum(grad_key_low.astype(jnp.float32), axis=0)
-    grad_bias_v = jnp.sum(grad_value_low.astype(jnp.float32), axis=0)
-    grad_normed = jnp.einsum(
-        "tj,kj->tk", grad_query_low, w_query, preferred_element_type=jnp.float32
-    )
-    grad_normed = grad_normed + jnp.einsum(
-        "tj,kj->tk", grad_key_low, w_key, preferred_element_type=jnp.float32
-    )
-    grad_normed = grad_normed + jnp.einsum(
-        "tj,kj->tk", grad_value_low, w_value, preferred_element_type=jnp.float32
-    )
-    _, norm_one_pull = jax.vjp(layer_norm, inputs, gain_one, bias_one)
-    grad_inputs_norm, grad_gain_one, grad_bias_one = norm_one_pull(grad_normed)
-    input_grad = (grad_resid + grad_inputs_norm)[None]
-    grad_wide = jnp.stack([grad_w_query, grad_w_key, grad_w_value, grad_w_out])
-    grad_low = jnp.concatenate(
-        [grad_w_up, grad_down.reshape(blocks, width, width)], axis=0
-    ).astype(jnp.bfloat16)
-    grad_small = jnp.concatenate(
-        [
-            grad_gain_one,
-            grad_bias_one,
-            grad_gain_two,
-            grad_bias_two,
-            grad_bias_q,
-            grad_bias_k,
-            grad_bias_v,
-            grad_bias_o,
-            grad_bias_down,
-            grad_bias_up,
-        ]
-    )
-    sums, row_small = reduce_rows(
-        grad_wide, grad_low, padded(grad_small.reshape(nseq, share)), nseq
-    )
-    row_small = row_small.reshape(2048)[:share]
+    if aligned:
+        row_small = row_small.reshape(2048)[:share]
+    else:
+        row_small = lax.psum_scatter(
+            row_small[:13].reshape(-1), "seq", scatter_dimension=0, tiled=True
+        )
+        row_small = lax.psum(row_small, "stream")
     row_units, update = muon(sums, momentum, nseq)
     new_momentum = 0.5 * momentum + row_units
-    update = update.astype(jnp.float32)
-    rates = unit_rates(blocks)
-    new_weights = weights - rates[:, None, None] * (update + 0.01 * weights)
+    blocks = (weights.shape[0] - 4) // 2
+    rates = jnp.array([0.5] * 3 + [4.0] + [0.5] * blocks + [0.25] * blocks, dtype=jnp.float32)
+    new_weights = weights - rates[:, None, None] * (update.astype(jnp.float32) + 0.01 * weights)
     first_new = 0.9 * moment_one + 0.1 * row_small
     second_new = 0.95 * moment_two + 0.05 * row_small * row_small
     adjusted = first_new / (1.0 - 0.9**STEP) / (jnp.sqrt(second_new / (1.0 - 0.95**STEP)) + 1e-08)
     new_small = small_params - 0.05 * (adjusted + 0.01 * small_params)
-    return (block_out, input_grad, new_weights, new_momentum, new_small, first_new, second_new)
+    return (
+        block_out[None], input_grad[None], new_weights, new_momentum, new_small, first_new, second_new,
+    )
 
 
 def solution(mesh):

time: 749 us -> 588 us (0.79)
  matrix products: 87 us -> 0 us
  Pallas kernels: 472 us -> 557 us
  local copies, waits for them, and re-layouts: 62.2 us -> 2.93 us
  other arithmetic: 53.2 us -> 18 us
  starting transfers between devices: 35.2 us -> 0 us
  waiting for transfers between devices: 26.3 us -> 0 us
    dot_general x20 -> x0, matrix products: 83.8 us -> none  [the longest x1 14.2 us: local(): jnp.einsum('td,fd->tf', grad_out, w_down, preferred_element_type=jnp.floa...]
    pallas_call x1, Pallas kernels: 189 us -> 265 us  [backward(): pl.pallas_call(functools.partial(backward_kernel, count, aligned), out_sh...]
    slice x16 -> x0, local copies, waits for them, and re-layouts: 41.2 us -> none  [the longest x3 13.8 us: local(): query_pre, key_pre = (pre[0], pre[1])]
    ppermute x7 -> x0, starting transfers between devices: 35.2 us -> none  [passed_along(): return lax.ppermute(array, axis, pairs)]
    ppermute x7 -> x0, waiting for transfers between devices: 26.3 us -> none  [passed_along(): return lax.ppermute(array, axis, pairs)]
    convert_element_type x10 -> x0, other arithmetic: 9.79 us -> none  [the longest x7 7 us: backward_turn(): passed_along(combine_states(running, own).astype(jnp.bfloat16), 'seq', -1)]
    pallas_call x1, Pallas kernels: 139 us -> 148 us  [muon(): pl.pallas_call(functools.partial(muon_kernel, count), out_shape=(jax.Shap...]
    transpose x1 -> x0, local copies, waits for them, and re-layouts: 8.68 us -> none  [local(): up_pre = up.transpose(1, 0, 2).reshape(group, blocks * width)]
  transfers between devices with their start and end apart: 7 -> 0, of which waited for: 7 -> 0; matrix products, arithmetic and copies ran while one was open for 0% -> 0% of each run, Pallas kernels for 0% -> 0%
where the time goes in v3:
time: 588 us; the launch traced here: 579 us
  Pallas kernels  557 us (95%)
  other arithmetic  18 us (3%)
    pallas_call x1, Pallas kernels, backward(): pl.pallas_call(functools.partial(backward_kernel, count, aligned), out_sh...  265 us
    pallas_call x1, Pallas kernels, muon(): pl.pallas_call(functools.partial(muon_kernel, count), out_shape=(jax.Shap...  148 us
    pallas_call x1, Pallas kernels, forward(): pl.pallas_call(functools.partial(forward_kernel, count, aligned), out_sha...  144 us

profile of v3, /device:TPU:31, one launch (start us, length us, event | category | flops | bytes accessed | tf_op | source)
XLA Modules:
  0.0 578.7 jit_solution(557469791927882084)
XLA Ops:
  0.6 0.7 reduce_precision.3
  1.3 0.6 pad_bitcast_fusion.small_ref
  1.9 144.0 %shard_map.153 = (bf16[3,2,2,4,2,128,1024]{6,5,4,3,2,1,0:T(8,128)(2,1)}, bf16[512,1024]{1,0:T(8,128)(2,1)}, f32[16,1024]{1,0:T(8,128)}, bf16[3,512,1024]{2,1,0:T...) custom-call(bf16[512,1024]{1,0:T(8,128)(2,1)} %bitcast.24, ...), custom_call_target="tpu_custom_call" | custom-call | tf_op jit(solution)/shard_map/pallas_call | solution.py:741
  146.0 0.0 copy-start.3
  146.0 0.0 copy-start.4
  146.0 0.0 copy-start.5
  146.0 264.9 %shard_map.154 = (f32[512,1024]{1,0:T(8,128)}, f32[3,128,1024]{2,1,0:T(8,128)}, f32[16,128]{1,0:T(8,128)}) custom-call(bf16[512,1024]{1,0:T(8,128)(2,1)} %bitcast.25, bf16[512,1024]{1,0:T(8,128)(2,1)} %bitcast.27, bf16[12,2,512,1024]{3,2,1,0:T(8,128)(2,1)} %bitcast.21, f32[16,1024]{1,0:T(8,128)} %get-tuple-element.25.rows_ref, ...), custom_call_target="tpu_custom_call" | custom-call | tf_op jit(solution)/shard_map/pallas_call | solution.py:1307
  410.9 0.0 copy-start.6
  410.9 0.0 copy-done.3
  410.9 0.0 copy-done.4
  411.0 0.0 copy-done.5
  411.0 1.3 multiply_subtract_fusion
  412.3 147.8 %shard_map.155 = (f32[3,2,2,128,1024]{4,3,2,1,0:T(8,128)}, bf16[3,2,2,128,1024]{4,3,2,1,0:T(8,128)(2,1)}) custom-call(f32[3,128,1024]{2,1,0:T(8,128)} %get-tuple-element.35.g_ref, f32[3,2,2,128,1024]{4,3,2,1,0:T(8,128)} %bitcast.23), custom_call_target="tpu_custom_call" | custom-call | tf_op jit(solution)/shard_map/pallas_call | solution.py:253
  560.1 0.0 copy-done.6
  560.1 0.0 copy-start
  560.1 8.3 %fusion.1 = f32[12,128,1024]{2,1,0:T(8,128)} fusion(f32[12,128,1024]{2,1,0:T(8,128)} %param.14, bf16[3,2,2,128,1024]{4,3,2,1,0:T(8,128)(2,1)} %get-tuple-element.36, f32[12]{0:T(128)S(1)} %copy-done.6), kind=kLoop, calls=%fused_computation.2 | loop fusion | flops 7864320 | bytes 15728688 | tf_op jit(solution)/shard_map/sub | solution.py:1412
  568.4 0.0 copy-done
  568.4 0.0 copy-start.2
  568.4 0.0 copy-start.1
  568.4 7.6 %bitcast_add_fusion = f32[12,128,1024]{2,1,0:T(8,128)} fusion(f32[3,2,2,128,1024]{4,3,2,1,0:T(8,128)S(1)} %copy-done, f32[12,128,1024]{2,1,0:T(8,128)} %param.15), kind=kLoop, calls=%fused_computation.3 | loop fusion | flops 3145728 | bytes 18874368 | tf_op jit(solution)/shard_map/add | solution.py:1409
  576.1 0.0 copy-done.2
  576.1 1.0 copy.19
  577.0 0.0 copy-done.1
  577.0 1.3 copy.20
Async XLA Ops:
  146.0 265.0 %copy-start.3 = (f32[1664]{0:T(1024)S(1)}, f32[1664]{0:T(1024)}, u32[]{:S(2)}) copy-start(f32[1664]{0:T(1024)} %param.16) | copy-start | bytes 19972
  146.0 265.0 %copy-start.4 = (f32[1664]{0:T(1024)S(1)}, f32[1664]{0:T(1024)}, u32[]{:S(2)}) copy-start(f32[1664]{0:T(1024)} %param.17) | copy-start | bytes 19972
  146.0 265.0 %copy-start.5 = (f32[1664]{0:T(1024)S(1)}, f32[1664]{0:T(1024)}, u32[]{:S(2)}) copy-start(f32[1664]{0:T(1024)} %param.18) | copy-start | bytes 19972
  410.9 149.1 %copy-start.6 = (f32[12]{0:T(128)S(1)}, f32[12]{0:T(128)}, u32[]{:S(2)}) copy-start(f32[12]{0:T(128)} %constant.26.clone) | copy-start | bytes 148
  560.1 8.4 %copy-start = (f32[3,2,2,128,1024]{4,3,2,1,0:T(8,128)S(1)}, f32[3,2,2,128,1024]{4,3,2,1,0:T(8,128)}, u32[]{:S(2)}) copy-start(f32[3,2,2,128,1024]{4,3,2,1,0:T(8,128)} %get-tuple-element.37) | copy-start | bytes 18874372
  568.4 7.7 %copy-start.2 = (bf16[512,1024]{1,0:T(8,128)(2,1)S(1)}, bf16[512,1024]{1,0:T(8,128)(2,1)}, u32[]{:S(2)}) copy-start(bf16[512,1024]{1,0:T(8,128)(2,1)} %get-tuple-element.23) | copy-start | bytes 3145732
  568.4 8.6 %copy-start.1 = (f32[512,1024]{1,0:T(8,128)S(1)}, f32[512,1024]{1,0:T(8,128)}, u32[]{:S(2)}) copy-start(f32[512,1024]{1,0:T(8,128)} %get-tuple-element.34) | copy-start | bytes 6291460

commit v4 on v3

--- a/solution.py
+++ b/solution.py
@@ -52,7 +52,7 @@
 
 
 SHIFTS = (0.0, 0.0, 0.1, 0.7, 0.7)
-FINE = (False, False, False, True, True)
+FINE = (False, False, False, False, True)
 BAND = 256
 
 
@@ -837,6 +837,10 @@
         self.total = len(self.steps)
         self.cores, self.firsts, self.seconds, self.fars = [], [], [], {}
         self.rows = sums_ref.shape[1]
+        self.beat = 0
+        self.done = {name: 0 for name in "abcde"}
+        self.stamp = {}
+        self.needs = {"a": (("b", 1),), "b": (("c", 2),), "c": (("d", 2),)}
 
     def there(self, i):
         return lax.rem(self.z + 1 + self.steps[i][1], self.count)
@@ -847,8 +851,16 @@
     def span(self, ref, i):
         return ref if len(self.parts(i)) == 2 else ref.at[pl.ds(0, 1)]
 
+    def far_slots(self, i):
+        b, k = self.steps[i]
+        before = (self.count - 1) * sum(len(self.parts(j * self.count)) for j in range(2 - b))
+        return pl.ds(before + k * len(self.parts(i)), len(self.parts(i)))
+
     def give(self, semaphore, peer):
         pl.semaphore_signal(semaphore, inc=1, device_id=peer, device_id_type=MESH)
+
+    def take(self, semaphore):
+        pl.semaphore_wait(semaphore, 1)
 
     def store(self, value, targets):
         high = value.astype(jnp.bfloat16)
@@ -881,7 +893,7 @@
                 rows = slice(xx * self.rows, (xx + 1) * self.rows)
                 self.store(value[rows], [self.core_out.at[slot, h, yy, xx] for h in self.parts(i)])
         if i >= 2:
-            pl.semaphore_wait(self.credit_core, 1)
+            self.take(self.credit_core)
         source, target = self.span(self.core_out.at[slot], i), self.span(self.core_in.at[slot], i)
         self.cores.append(remote(source, target, self.cs.at[i], self.cr.at[i], self.pair[2]))
         self.cores[i].start()
@@ -902,14 +914,14 @@
             away, near = ((1 - y, j), (y, j)) if k % 2 == 0 else ((j, 1 - x), (j, x))
             for at, send, keep in (
                 (away, [out.at[h, j] for h in self.parts(i)], None),
-                (near, None, self.kept_one.at[j]),
+                (near, None, self.kept_one.at[i % 2, j]),
             ):
                 got = [self.core_in.at[slot, h, at[0], at[1]] for h in self.parts(i)]
                 self.add(i, self.own.at[at[0], at[1]], got, send, keep)
         if i + 2 < self.total:
             self.give(self.credit_core, self.pair[2])
         if i >= 4:
-            pl.semaphore_wait(self.credit_first.at[i % 2], 1)
+            self.take(self.credit_first.at[i % 2])
         peer = self.pair[1 - k % 2]
         source, target = self.span(out, i), self.span(self.first_in.at[i % 4], i)
         self.firsts.append(remote(source, target, self.fs.at[i], self.fr.at[i], peer))
@@ -923,13 +935,13 @@
             self.seconds[i - 3].wait_send()
         out = self.second_out.at[i % 3]
         got = self.first_in.at[i % 4]
-        self.add(i, self.kept_one.at[1 - mine], [got.at[h, 1 - mine] for h in self.parts(i)],
+        self.add(i, self.kept_one.at[i % 2, 1 - mine], [got.at[h, 1 - mine] for h in self.parts(i)],
                  [out.at[h] for h in self.parts(i)], None)
-        self.add(i, self.kept_one.at[mine], [got.at[h, mine] for h in self.parts(i)], None, self.kept_two)
+        self.add(i, self.kept_one.at[i % 2, mine], [got.at[h, mine] for h in self.parts(i)], None, self.kept_two.at[i % 2])
         if i + 4 < self.total:
             self.give(self.credit_first.at[i % 2], self.pair[1 - k % 2])
         if i >= 4:
-            pl.semaphore_wait(self.credit_second.at[i % 2], 1)
+            self.take(self.credit_second.at[i % 2])
         source, target = self.span(out, i), self.span(self.second_in.at[i % 4], i)
         self.seconds.append(remote(source, target, self.es.at[i], self.er.at[i], self.pair[k % 2]))
         self.seconds[i].start()
@@ -942,13 +954,13 @@
             if i >= self.count:
                 self.fars[i - self.count].wait_send()
             out = self.far_out.at[k]
-            self.add(i, self.kept_two, got, [out.at[h] for h in self.parts(i)], None)
+            self.add(i, self.kept_two.at[i % 2], got, [out.at[h] for h in self.parts(i)], None)
             peer = device(self.there(i), self.x, self.y, self.c)
-            source, target = self.span(out, i), self.span(self.far_in.at[b, k], i)
+            source, target = self.span(out, i), self.far_in.at[self.far_slots(i)]
             self.fars[i] = remote(source, target, self.zs.at[b, k], self.zr.at[b, k], peer)
             self.fars[i].start()
         else:
-            self.add(i, self.kept_two, got, None, self.sums_ref.at[b])
+            self.add(i, self.kept_two.at[i % 2], got, None, self.sums_ref.at[b])
         if i + 4 < self.total:
             self.give(self.credit_second.at[i % 2], self.pair[k % 2])
 
@@ -958,13 +970,28 @@
             return
         for j in range(self.count - 1):
             self.fars[i - self.count + 1 + j].wait_recv()
-            got = [self.far_in.at[b, j, h] for h in self.parts(i)]
+            start = self.far_slots(i - self.count + 1 + j).start
+            got = [self.far_in.at[start + h] for h in self.parts(i)]
             self.add(i, self.sums_ref.at[b], got, None, self.sums_ref.at[b])
 
-    def tick(self, i):
-        for lag, stage in ((4, self.stage_e), (3, self.stage_d), (2, self.stage_c), (1, self.stage_b), (0, self.stage_a)):
-            if 0 <= i - lag < self.total:
-                stage(i - lag)
+    def run(self, name):
+        i = self.done[name]
+        for other, back in self.needs.get(name, ()):
+            while self.done[other] <= i - back:
+                self.run(other)
+        getattr(self, "stage_" + name)(i)
+        self.done[name] = i + 1
+        self.stamp[name, i] = self.beat
+
+    def pump(self, make=False):
+        self.beat += 1
+        for before, name, lag in (("d", "e", 2), ("c", "d", 2), ("b", "c", 2), ("a", "b", 1)):
+            while self.done[name] < self.done[before]:
+                if self.beat - self.stamp[before, self.done[name]] < lag:
+                    break
+                self.run(name)
+        if make:
+            self.run("a")
 
     def wait_sends(self):
         for copy in self.cores[-2:] + self.firsts[-3:] + self.seconds[-3:]:
@@ -986,7 +1013,7 @@
     place = z, x, y, c = places()
     straight, far = others_along_seq(z, x, y, c, count)
     pair = [device(z, 1 - x, y, c), device(z, x, 1 - y, c), device(z, x, y, 1 - c)]
-    group, width = x_ref.shape
+    group, width = dy_ref.shape
     bands = group // BAND
     pairs = width // PAIR
     block_rows = 2 * sums_ref.shape[1]
@@ -1032,13 +1059,18 @@
         (cs, cr, fs, fr, es, er, zs, zr, credit_core, credit_first, credit_second), sums_ref,
     )
 
-    def tick(i):
-        if i < sums.total:
+    def pump(make=False):
+        i = sums.done["a"]
+        if make:
             for copy in lefts[i]:
                 copy.wait()
             if i + 1 < sums.total:
                 lefts[i + 1] = load_left(i + 1)
-        sums.tick(i)
+        sums.pump(make)
+
+    def make_until(limit):
+        while sums.done["a"] < limit:
+            pump(True)
 
     lefts[0] = load_left(0)
     blocks = big.shape[0]
@@ -1062,7 +1094,8 @@
     for i in range(bands):
         add_row(8, dy_ref[i * BAND : (i + 1) * BAND, :])
     for j in range(blocks):
-        tick(j)
+        if j != 2:
+            pump(True)
         w_loads[2, j].wait()
         u_loads[j].wait()
 
@@ -1082,8 +1115,8 @@
             w_loads[1, j - 2] = load(w_ref.at[4 + j - 2], wbuf.at[j % 2])
             u_loads[j + 2] = load(ratio_ref.at[j - 2], ubuf.at[j % 2])
     for j in range(blocks):
-        if j % 2 == 0:
-            tick(blocks + j // 2)
+        if j % 2:
+            pump(True)
         w_loads[1, j].wait()
 
         def up_back(i, carry):
@@ -1116,7 +1149,10 @@
         acc[span, :] = dot(low, unit_of(0), True)
         return carry
 
-    lax.fori_loop(0, bands, middle_back, 0)
+    for i in range(bands):
+        middle_back(i, 0)
+        if i == 0:
+            pump(True)
     low_loads.append(load(low_ref.at[2], wbuf.at[0, 0]))
     u_loads[blocks].wait()
     u_loads[blocks + 1].wait()
@@ -1142,6 +1178,7 @@
     pack_message(query, dnum, flags.at[0], dden, message)
     relay = Relay(count, factors, message, across, part, spread, total_ref, state_back, (rs, rr), place)
     relay.swap()
+    pump(True)
     pre_load = load(pre_ref.at[0], acc)
     pre_load.wait()
 
@@ -1183,16 +1220,17 @@
                 ubuf[index, span, lanes] = total[upto - BAND :]
         return carry
 
-    lax.fori_loop(0, pairs // 4, attend_back, 0)
-    tick(blocks + 2)
-    relay.spread_out()
-    lax.fori_loop(pairs // 4, pairs // 2, attend_back, 0)
-    tick(blocks + 3)
-    relay.join()
-    lax.fori_loop(pairs // 2, pairs, attend_back, 0)
+    quarter = pairs // 4
+    early = sums.total - count
+    for part in range(4):
+        lax.fori_loop(part * quarter, (part + 1) * quarter, attend_back, 0)
+        if part == 0:
+            relay.spread_out()
+        elif part == 2:
+            relay.join()
+        pump(sums.done["a"] < early)
     pre_load = load(pre_ref.at[1], acc)
-    for i in range(blocks + 4, sums.total - count):
-        tick(i)
+    make_until(early)
     relay.finish()
     pre_load.wait()
 
@@ -1219,12 +1257,11 @@
         return carry
 
     lax.fori_loop(0, pairs, attend_close, 0)
+    x_load = load(x_ref, dq_low)
     w_loads[0, 0] = load(w_ref.at[0], wbuf.at[0])
     w_loads[0, 1] = load(w_ref.at[1], wbuf.at[1])
-    step = sums.total - count
     for j in range(3):
-        tick(step)
-        step += 1
+        pump(True)
         w_loads[0, j].wait()
 
         def input_back(i, carry):
@@ -1237,10 +1274,12 @@
         if j == 0:
             w_loads[0, 2] = load(w_ref.at[2], wbuf.at[0])
 
+    x_load.wait()
+
     def outer_back(i, carry):
         span = band_span(i)
         upstream = acc[span, :]
-        back, unit = norm_back(x_ref[span, :].astype(f32), upstream, rows_ref[0:1, :])
+        back, unit = norm_back(dq_low[span, :].astype(f32), upstream, rows_ref[0:1, :])
         add_row(0, upstream * unit)
         add_row(1, upstream)
         grad_ref[span, :] = grad_ref[span, :] + back
@@ -1259,10 +1298,7 @@
         for k, (peer, there) in enumerate(zip(straight + far, seqs)):
             small.append(remote(sm_send.at[there], sm_recv.at[k], ms.at[k], mr.at[k], peer))
             small[-1].start()
-    while step < sums.total:
-        tick(step)
-        step += 1
-    last = sums.total + 4
+    make_until(sums.total)
     if aligned:
         total = sm_send[z * 2 + x]
         for k, copy in enumerate(small):
@@ -1274,8 +1310,7 @@
             copy = remote(sm_part.at[j], sm_pair.at[j], ms.at[index], mr.at[index], pair[1 + j])
             copy.start()
             tail.append(copy)
-            tick(step)
-            step += 1
+            pump()
             copy.wait_recv()
             if j == 0:
                 sm_part[1] = sm_part[0] + sm_pair[0]
@@ -1283,9 +1318,8 @@
                 small_out[...] = sm_part[1] + sm_pair[1]
     else:
         small_out[...] = gs[...]
-    while step < last:
-        tick(step)
-        step += 1
+    while sums.done["e"] < sums.total:
+        pump()
     sums.wait_sends()
     relay.wait_sends()
     for copy in small + tail:
@@ -1311,7 +1345,7 @@
             S((batches,) + piece, f32),
             S(small if aligned else (16, width), f32),
         ),
-        in_specs=[VMEM, VMEM, ANY, VMEM] + [ANY] * 7 + [VMEM, smem, smem],
+        in_specs=[ANY, VMEM, ANY, VMEM] + [ANY] * 7 + [VMEM, smem, smem],
         out_specs=[VMEM, VMEM, VMEM],
         scratch_shapes=[
             V((2, 2, 2, 2) + piece, bf16),
@@ -1319,12 +1353,12 @@
             V((2, 2) + piece, f32),
             V((3, 2, 2) + piece, bf16),
             V((4, 2, 2) + piece, bf16),
-            V((2,) + piece, f32),
+            V((2, 2) + piece, f32),
             V((3, 2) + piece, bf16),
             V((4, 2) + piece, bf16),
-            V(piece, f32),
+            V((2,) + piece, f32),
             V((count - 1, 2) + piece, bf16),
-            V((batches, count - 1, 2) + piece, bf16),
+            V(((batches + 1) * (count - 1),) + piece, bf16),
             V((blocks, group, width), bf16),
             V((2, blocks, 2 * share_rows, group), bf16),
             V((2, width // group, group, width), bf16),

time: 588 us -> 505 us (0.86)
  Pallas kernels: 557 us -> 474 us
    pallas_call x1, Pallas kernels: 265 us -> 197 us  [backward(): pl.pallas_call(functools.partial(backward_kernel, count, aligned), out_sh...]
    pallas_call x1, Pallas kernels: 148 us -> 133 us  [muon(): pl.pallas_call(functools.partial(muon_kernel, count), out_shape=(jax.Shap...]
where the time goes in v4:
time: 505 us; the launch traced here: 496 us
  Pallas kernels  474 us (94%)
  other arithmetic  18 us (4%)
    pallas_call x1, Pallas kernels, backward(): pl.pallas_call(functools.partial(backward_kernel, count, aligned), out_sh...  197 us
    pallas_call x1, Pallas kernels, forward(): pl.pallas_call(functools.partial(forward_kernel, count, aligned), out_sha...  144 us
    pallas_call x1, Pallas kernels, muon(): pl.pallas_call(functools.partial(muon_kernel, count), out_shape=(jax.Shap...  133 us

profile of v4, /device:TPU:31, one launch (start us, length us, event | category | flops | bytes accessed | tf_op | source)
XLA Modules:
  0.0 496.4 jit_solution(15454237018365111489)
XLA Ops:
  0.6 0.7 reduce_precision.3
  1.3 0.6 pad_bitcast_fusion.small_ref
  1.9 144.0 %shard_map.153 = (bf16[3,2,2,4,2,128,1024]{6,5,4,3,2,1,0:T(8,128)(2,1)}, bf16[512,1024]{1,0:T(8,128)(2,1)}, f32[16,1024]{1,0:T(8,128)}, bf16[3,512,1024]{2,1,0:T...) custom-call(bf16[512,1024]{1,0:T(8,128)(2,1)} %bitcast.24, ...), custom_call_target="tpu_custom_call" | custom-call | tf_op jit(solution)/shard_map/pallas_call | solution.py:741
  146.0 0.0 copy-start.3
  146.0 0.0 copy-start.4
  146.0 0.0 copy-start.5
  146.0 197.3 %shard_map.154 = (f32[512,1024]{1,0:T(8,128)}, f32[3,128,1024]{2,1,0:T(8,128)}, f32[16,128]{1,0:T(8,128)}) custom-call(bf16[512,1024]{1,0:T(8,128)(2,1)} %bitcast.25, bf16[512,1024]{1,0:T(8,128)(2,1)} %bitcast.27, bf16[12,2,512,1024]{3,2,1,0:T(8,128)(2,1)} %bitcast.21, f32[16,1024]{1,0:T(8,128)} %get-tuple-element.25.rows_ref, ...), custom_call_target="tpu_custom_call" | custom-call | tf_op jit(solution)/shard_map/pallas_call | solution.py:1341
  343.3 0.0 copy-start.6
  343.3 0.0 copy-done.3
  343.3 0.0 copy-done.4
  343.3 0.0 copy-done.5
  343.3 1.3 multiply_subtract_fusion
  344.7 132.9 %shard_map.155 = (f32[3,2,2,128,1024]{4,3,2,1,0:T(8,128)}, bf16[3,2,2,128,1024]{4,3,2,1,0:T(8,128)(2,1)}) custom-call(f32[3,128,1024]{2,1,0:T(8,128)} %get-tuple-element.35.g_ref, f32[3,2,2,128,1024]{4,3,2,1,0:T(8,128)} %bitcast.23), custom_call_target="tpu_custom_call" | custom-call | tf_op jit(solution)/shard_map/pallas_call | solution.py:253
  477.6 0.0 copy-done.6
  477.6 0.0 copy-start
  477.6 8.3 %fusion.1 = f32[12,128,1024]{2,1,0:T(8,128)} fusion(f32[12,128,1024]{2,1,0:T(8,128)} %param.14, bf16[3,2,2,128,1024]{4,3,2,1,0:T(8,128)(2,1)} %get-tuple-element.36, f32[12]{0:T(128)S(1)} %copy-done.6), kind=kLoop, calls=%fused_computation.2 | loop fusion | flops 7864320 | bytes 15728688 | tf_op jit(solution)/shard_map/sub | solution.py:1446
  486.0 0.0 copy-done
  486.0 0.0 copy-start.2
  486.0 0.0 copy-start.1
  486.0 7.6 %bitcast_add_fusion = f32[12,128,1024]{2,1,0:T(8,128)} fusion(f32[3,2,2,128,1024]{4,3,2,1,0:T(8,128)S(1)} %copy-done, f32[12,128,1024]{2,1,0:T(8,128)} %param.15), kind=kLoop, calls=%fused_computation.3 | loop fusion | flops 3145728 | bytes 18874368 | tf_op jit(solution)/shard_map/add | solution.py:1443
  493.6 0.0 copy-done.2
  493.6 1.0 copy.19
  494.6 0.0 copy-done.1
  494.6 1.3 copy.20
Async XLA Ops:
  146.0 197.3 %copy-start.3 = (f32[1664]{0:T(1024)S(1)}, f32[1664]{0:T(1024)}, u32[]{:S(2)}) copy-start(f32[1664]{0:T(1024)} %param.16) | copy-start | bytes 19972
  146.0 197.3 %copy-start.4 = (f32[1664]{0:T(1024)S(1)}, f32[1664]{0:T(1024)}, u32[]{:S(2)}) copy-start(f32[1664]{0:T(1024)} %param.17) | copy-start | bytes 19972
  146.0 197.3 %copy-start.5 = (f32[1664]{0:T(1024)S(1)}, f32[1664]{0:T(1024)}, u32[]{:S(2)}) copy-start(f32[1664]{0:T(1024)} %param.18) | copy-start | bytes 19972
  343.3 134.3 %copy-start.6 = (f32[12]{0:T(128)S(1)}, f32[12]{0:T(128)}, u32[]{:S(2)}) copy-start(f32[12]{0:T(128)} %constant.26.clone) | copy-start | bytes 148
  477.6 8.4 %copy-start = (f32[3,2,2,128,1024]{4,3,2,1,0:T(8,128)S(1)}, f32[3,2,2,128,1024]{4,3,2,1,0:T(8,128)}, u32[]{:S(2)}) copy-start(f32[3,2,2,128,1024]{4,3,2,1,0:T(8,128)} %get-tuple-element.37) | copy-start | bytes 18874372
  486.0 7.7 %copy-start.2 = (bf16[512,1024]{1,0:T(8,128)(2,1)S(1)}, bf16[512,1024]{1,0:T(8,128)(2,1)}, u32[]{:S(2)}) copy-start(bf16[512,1024]{1,0:T(8,128)(2,1)} %get-tuple-element.23) | copy-start | bytes 3145732
  486.0 8.6 %copy-start.1 = (f32[512,1024]{1,0:T(8,128)S(1)}, f32[512,1024]{1,0:T(8,128)}, u32[]{:S(2)}) copy-start(f32[512,1024]{1,0:T(8,128)} %get-tuple-element.34) | copy-start | bytes 6291460
